TPU v7x, 128 devices: a whole 4x4x4 slice. The times are simulated.
128 devices in a mesh: dp: 16 (over y_hi, x, core), row: 2 (over y_lo), col: 4 (over z).
Axes of the slice: x: 4, y: 4 (y_hi: 2, y_lo: 2; y = y_hi * 2 + y_lo), z: 4, core: 2. Of those that a mesh axis runs over, the one named last changes fastest.
Arguments:
- tokens: bfloat16 [16384, 1024], P(('dp', 'col'), 'row'), may hold values from -13 to 13
- segment_ids: int32 [16384], P('dp'), may hold values from 0 to 2, as said below
- w_qkv: bfloat16 [3, 1024, 1024], P(None, 'row', 'col'), may hold values from -0.1875 to 0.1875
- b_qkv: bfloat16 [3, 1024], P(None, 'col'), may hold values from -3 to 3
- w_out: bfloat16 [1024, 1024], P('col', 'row'), may hold values from -0.75 to 0.75
- b_out: bfloat16 [1024], P('row'), may hold values from -2 to 2
- w_up: bfloat16 [1024, 4096], P('row', 'col'), may hold values from -0.1875 to 0.1875
- b_up: bfloat16 [4096], P('col'), may hold values from -3 to 3
- w_down: bfloat16 [4096, 1024], P('col', 'row'), may hold values from -0.09375 to 0.09375
- b_down: bfloat16 [1024], P('row'), may hold values from -2 to 2
- norm_gain: bfloat16 [2, 1024], P(None, 'row'), may hold values from 0.2 to 2.5
- norm_bias: bfloat16 [2, 1024], P(None, 'row'), may hold values from -2 to 2
- cotangent: bfloat16 [16384, 1024], P(('dp', 'col'), 'row'), may hold values from -6 to 6
Outputs:
- output: bfloat16 [16384, 1024], P(('dp', 'col'), 'row')
- tokens_grad: bfloat16 [16384, 1024], P(('dp', 'col'), 'row')
- w_qkv_grad: float32 [3, 1024, 1024], P(None, 'row', 'col')
- b_qkv_grad: float32 [3, 1024], P(None, 'col')
- w_out_grad: float32 [1024, 1024], P('col', 'row')
- b_out_grad: float32 [1024], P('row')
- w_up_grad: float32 [1024, 4096], P('row', 'col')
- b_up_grad: float32 [4096], P('col')
- w_down_grad: float32 [4096, 1024], P('col', 'row')
- b_down_grad: float32 [1024], P('row')
- norm_gain_grad: float32 [2, 1024], P(None, 'row')
- norm_bias_grad: float32 [2, 1024], P(None, 'row')
Inputs may be any that keep to these rules, and one draw needn't show every extreme that they name: `segment_ids`: within each packed sequence of 1024 tokens the ids never fall, the first token has 0 and the last 2.
All inputs are finite; a program needn't handle non-finite values.
Results may differ from a plain program's by a relative error of at most 0.012.
The roundings to bfloat16 on the way count: a program that leaves them out, or rounds other values in their place, can miss the bound.
Values may be sent and summed in bfloat16 or wider, within the bound.
A program may use at most 128 MiB of HBM per device.

v0:
```python
from functools import partial
import math

import jax
import jax.numpy as jnp
from jax import lax
from jax.sharding import PartitionSpec as P

HD = 64
ROT = 16


EPSILON = 1e-05


def rotary_tables(position):
    freq_index = jnp.arange(ROT // 2, dtype=jnp.float32)
    inverse = 10000.0 ** (-2.0 * freq_index / ROT)
    angles = position[:, None] * inverse[None, :]
    return (jnp.cos(angles), jnp.sin(angles))


def rotate(values_in, cosine_tab, sine_tab, rotation_sign):
    length = values_in.shape[0]
    shaped = values_in.reshape(length, -1, HD)
    half_rot = ROT // 2
    front_part = shaped[:, :, :half_rot]
    behind = shaped[:, :, half_rot:ROT]
    remain = shaped[:, :, ROT:]
    cos_b = cosine_tab[:, None, :]
    sin_b = sine_tab[:, None, :]
    turned_front = front_part * cos_b - rotation_sign * behind * sin_b
    turned_back = behind * cos_b + rotation_sign * front_part * sin_b
    return jnp.concatenate([turned_front, turned_back, remain], axis=2).reshape(values_in.shape)


def on_device(
    tokens,
    segment_ids,
    w_qkv,
    b_qkv,
    w_out,
    b_out,
    w_up,
    b_up,
    w_down,
    b_down,
    norm_gain,
    norm_bias,
    cotangent,
):
    local_width = tokens.shape[1]
    full_width = lax.axis_size("row") * local_width
    x_in = tokens.astype(jnp.float32)
    sum_first, sum_second = lax.psum((jnp.sum(x_in, axis=1), jnp.sum(x_in * x_in, axis=1)), "row")
    mean_val = sum_first / full_width
    inv_std = lax.rsqrt(sum_second / full_width - mean_val * mean_val + EPSILON)
    normed = (x_in - mean_val[:, None]) * inv_std[:, None]
    attn_in = (normed * norm_gain[0] + norm_bias[0]).astype(jnp.bfloat16)
    mlp_in = (normed * norm_gain[1] + norm_bias[1]).astype(jnp.bfloat16)
    attn_all, mlp_all = (
        lax.all_gather(attn_in, "col", axis=0, tiled=True),
        lax.all_gather(mlp_in, "col", axis=0, tiled=True),
    )
    qkv_part = jnp.einsum("td,kde->kte", attn_all, w_qkv, preferred_element_type=jnp.float32)
    up_part = jnp.dot(mlp_all, w_up, preferred_element_type=jnp.float32)
    qkv_sum, up_sum = lax.psum((qkv_part, up_part), "row")
    qkv_pre = qkv_sum + b_qkv[:, None, :]
    hidden_pre = up_sum + b_up
    group_len = attn_all.shape[0]
    cosine_tab, sine_tab = rotary_tables(jnp.arange(group_len, dtype=jnp.float32))
    query_low = rotate(qkv_pre[0], cosine_tab, sine_tab, 1.0).astype(jnp.bfloat16)
    key_low = rotate(qkv_pre[1], cosine_tab, sine_tab, 1.0).astype(jnp.bfloat16)
    value_low = qkv_pre[2].astype(jnp.bfloat16)
    head_count = query_low.shape[1] // HD
    block_rows = min(512, group_len)
    block_count = group_len // block_rows
    score_scale = 1.0 / math.sqrt(HD)

    def to_heads(values_in):
        return values_in.reshape(group_len, head_count, HD).transpose(1, 0, 2)

    def to_blocks(values_in):
        return (
            to_heads(values_in)
            .reshape(head_count, block_count, block_rows, HD)
            .transpose(1, 0, 2, 3)
        )

    def from_blocks(blocked):
        return blocked.transpose(0, 2, 1, 3).reshape(group_len, head_count * HD)

    def from_heads(headed):
        return headed.transpose(1, 0, 2).reshape(group_len, head_count * HD)

    key_heads = to_heads(key_low)
    value_heads = to_heads(value_low)
    seg_blocks = segment_ids.reshape(block_count, block_rows)
    row_starts = jnp.arange(block_count, dtype=jnp.int32) * block_rows
    column_ids = jnp.arange(group_len, dtype=jnp.int32)

    def block_scores(query_blk, seg_blk, row_start):
        scores = (
            jnp.einsum("hqd,hkd->hqk", query_blk, key_heads, preferred_element_type=jnp.float32)
            * score_scale
        )
        row_ids = row_start + jnp.arange(block_rows, dtype=jnp.int32)
        allowed = (column_ids[None, :] <= row_ids[:, None]) & (
            seg_blk[:, None] == segment_ids[None, :]
        )
        return jnp.where(allowed[None], scores, -1e30)

    def attend(inputs):
        query_blk, seg_blk, row_start = inputs
        scores = block_scores(query_blk, seg_blk, row_start)
        row_max = jnp.max(scores, axis=2, keepdims=True)
        expo_val = jnp.exp(scores - row_max)
        denom = jnp.sum(expo_val, axis=2, keepdims=True)
        prob_low = (expo_val / denom).astype(jnp.bfloat16)
        mixed_blk = jnp.einsum(
            "hqk,hkd->hqd", prob_low, value_heads, preferred_element_type=jnp.float32
        )
        return (mixed_blk, (row_max + jnp.log(denom))[:, :, 0])

    mixed_blocks, log_total = lax.map(attend, (to_blocks(query_low), seg_blocks, row_starts))
    attn_local = from_blocks(mixed_blocks).astype(jnp.bfloat16)
    hidden_local = jax.nn.gelu(hidden_pre, approximate=False).astype(jnp.bfloat16)
    attn_out, hidden_low = (attn_local, hidden_local)
    hidden_rows = hidden_low
    branch = lax.psum_scatter(
        jnp.dot(attn_out, w_out, preferred_element_type=jnp.float32)
        + jnp.dot(hidden_rows, w_down, preferred_element_type=jnp.float32),
        "col",
        scatter_dimension=0,
        tiled=True,
    )
    output = (x_in + branch + b_out.astype(jnp.float32) + b_down.astype(jnp.float32)).astype(
        jnp.bfloat16
    )
    grad_all = lax.all_gather(cotangent, "col", axis=0, tiled=True)
    out_bias_grad = jnp.sum(grad_all, axis=0, dtype=jnp.float32)
    w_out_grad = jnp.einsum("tc,td->cd", attn_out, grad_all, preferred_element_type=jnp.float32)
    w_down_grad = jnp.einsum("tf,td->fd", hidden_low, grad_all, preferred_element_type=jnp.float32)
    attn_part = jnp.einsum("td,cd->tc", grad_all, w_out, preferred_element_type=jnp.float32)
    hidden_part = jnp.einsum("td,fd->tf", grad_all, w_down, preferred_element_type=jnp.float32)
    attn_grad, hidden_grad = lax.psum((attn_part, hidden_part), "row")
    gelu_value, gelu_back = jax.vjp(partial(jax.nn.gelu, approximate=False), hidden_pre)
    hidden_grad_local = gelu_back(hidden_grad)[0].astype(jnp.bfloat16)
    grad_mixed = attn_grad.astype(jnp.bfloat16)

    def back_step(carry_acc, inputs):
        key_acc, value_acc = carry_acc
        query_blk, grad_blk, seg_blk, log_blk, row_start = inputs
        scores = block_scores(query_blk, seg_blk, row_start)
        prob_full = jnp.exp(scores - log_blk[:, :, None])
        prob_low = prob_full.astype(jnp.bfloat16)
        prob_grad = jnp.einsum(
            "hqd,hkd->hqk", grad_blk, value_heads, preferred_element_type=jnp.float32
        )
        inner_sum = jnp.sum(prob_full * prob_grad, axis=2, keepdims=True)
        score_grad = (prob_full * (prob_grad - inner_sum)).astype(jnp.bfloat16)
        query_grad = (
            jnp.einsum("hqk,hkd->hqd", score_grad, key_heads, preferred_element_type=jnp.float32)
            * score_scale
        )
        key_acc = (
            key_acc
            + jnp.einsum("hqk,hqd->hkd", score_grad, query_blk, preferred_element_type=jnp.float32)
            * score_scale
        )
        value_acc = value_acc + jnp.einsum(
            "hqk,hqd->hkd", prob_low, grad_blk, preferred_element_type=jnp.float32
        )
        return ((key_acc, value_acc), query_grad)

    zero_heads = jnp.zeros((head_count, group_len, HD), jnp.float32)
    accums, query_grads = lax.scan(
        back_step,
        (zero_heads, zero_heads),
        (to_blocks(query_low), to_blocks(grad_mixed), seg_blocks, log_total, row_starts),
    )
    query_pre_grad = rotate(from_blocks(query_grads), cosine_tab, sine_tab, -1.0).astype(
        jnp.bfloat16
    )
    key_pre_grad = rotate(from_heads(accums[0]), cosine_tab, sine_tab, -1.0).astype(jnp.bfloat16)
    value_pre_grad = from_heads(accums[1]).astype(jnp.bfloat16)
    qkv_grad_local = jnp.stack([query_pre_grad, key_pre_grad, value_pre_grad])
    qkv_grad, hidden_pre_grad = (qkv_grad_local, hidden_grad_local)
    w_up_grad = jnp.einsum(
        "tm,tf->mf", mlp_all, hidden_pre_grad, preferred_element_type=jnp.float32
    )
    b_up_grad = jnp.sum(hidden_pre_grad, axis=0, dtype=jnp.float32)
    w_qkv_grad = jnp.einsum("td,kte->kde", attn_all, qkv_grad, preferred_element_type=jnp.float32)
    b_qkv_grad = jnp.sum(qkv_grad, axis=1, dtype=jnp.float32)
    hidden_rows = hidden_pre_grad
    first_term = jnp.einsum("kte,kde->td", qkv_grad, w_qkv, preferred_element_type=jnp.float32)
    second_term = jnp.einsum("tf,df->td", hidden_rows, w_up, preferred_element_type=jnp.float32)
    both_grads = lax.psum_scatter(
        jnp.concatenate([first_term, second_term], axis=1), "col", scatter_dimension=0, tiled=True
    )
    attn_in_grad = both_grads[:, :local_width]
    mlp_in_grad = both_grads[:, local_width:]
    normed_grad = attn_in_grad * norm_gain[0] + mlp_in_grad * norm_gain[1]
    total_first, total_second = lax.psum(
        (jnp.sum(normed_grad, axis=1), jnp.sum(normed_grad * normed, axis=1)), "row"
    )
    x_grad = cotangent.astype(jnp.float32) + inv_std[:, None] * (
        normed_grad
        - total_first[:, None] / full_width
        - normed * total_second[:, None] / full_width
    )
    gain_grad = jnp.stack(
        [jnp.sum(attn_in_grad * normed, axis=0), jnp.sum(mlp_in_grad * normed, axis=0)]
    )
    shift_grad = jnp.stack([jnp.sum(attn_in_grad, axis=0), jnp.sum(mlp_in_grad, axis=0)])
    gain_grad, shift_grad = lax.psum((gain_grad, shift_grad), ("dp", "col"))
    w_qkv_grad, b_qkv_grad, w_out_grad, out_bias_grad, w_up_grad, b_up_grad, w_down_grad = lax.psum(
        (w_qkv_grad, b_qkv_grad, w_out_grad, out_bias_grad, w_up_grad, b_up_grad, w_down_grad), "dp"
    )
    return (
        output,
        x_grad.astype(jnp.bfloat16),
        w_qkv_grad,
        b_qkv_grad,
        w_out_grad,
        out_bias_grad,
        w_up_grad,
        b_up_grad,
        w_down_grad,
        out_bias_grad,
        gain_grad,
        shift_grad,
    )


def solution(mesh):
    in_specs = (
        P(("dp", "col"), "row"),
        P("dp"),
        P(None, "row", "col"),
        P(None, "col"),
        P("col", "row"),
        P("row"),
        P("row", "col"),
        P("col"),
        P("col", "row"),
        P("row"),
        P(None, "row"),
        P(None, "row"),
        P(("dp", "col"), "row"),
    )
    out_specs = (
        P(("dp", "col"), "row"),
        P(("dp", "col"), "row"),
        P(None, "row", "col"),
        P(None, "col"),
        P("col", "row"),
        P("row"),
        P("row", "col"),
        P("col"),
        P("col", "row"),
        P("row"),
        P(None, "row"),
        P(None, "row"),
    )
    return jax.shard_map(
        on_device, mesh=mesh, in_specs=in_specs, out_specs=out_specs, check_vma=False
    )
```

profile of v0, /device:TPU:1, one launch (start us, length us, event | category | flops | bytes accessed | tf_op | source)
XLA Modules:
  0.0 947.4 jit_solution(4665736250177076354)
XLA Ops:
  10.6 25.6 %all-gather.8.cloned.1.call-done = bf16[1024,512]{1,0:T(8,128)(2,1)} async-done(((bf16[256,512]{1,0:T(8,128)(2,1)}), bf16[1024,512]{1,0:T(8,128)(2,1)}) %all-gather.8.cloned.1.call-update) | async-done | bytes 1048592 | tf_op jit(solution)/shard_map/all_gather | solution.py:140
  38.0 25.7 %all-reduce.13 = (f32[256]{0:T(256)S(1)}, f32[256]{0:T(256)S(1)}, bf16[1024,256]{1,0:T(8,128)(2,1)}) all-reduce(f32[256]{0:T(256)S(1)} %get-tuple-element.254, f32[256]{0:T(256)S(1)} %get-tuple-element.253, f32[1024,256]{1,0:T(8,128)S(1)} %fusion.81), channel_id=1, replica_groups=mesh['dp'=16,'row'=2,'col'=4] {'row'}, use_global_device_ids=true, to_apply=%region_3.0 | all-reduce | flops 262656 | bytes 1576960 | tf_op jit(solution)/shard_map/psum | solution.py:55
  66.6 3.2 fusion.82
  69.8 22.3 %all-gather.6.cloned.1.call-done = bf16[1024,512]{1,0:T(8,128)(2,1)} async-done(((bf16[256,512]{1,0:T(8,128)(2,1)}), bf16[1024,512]{1,0:T(8,128)(2,1)}) %all-gather.6.cloned.1.call-update) | async-done | bytes 1048592 | tf_op jit(solution)/shard_map/all_gather | solution.py:63
  92.1 4.8 fusion.79
  96.9 22.1 %all-gather.4.cloned.1.call-done = bf16[1024,512]{1,0:T(8,128)(2,1)} async-done(((bf16[256,512]{1,0:T(8,128)(2,1)}), bf16[1024,512]{1,0:T(8,128)(2,1)}) %all-gather.4.cloned.1.call-update) | async-done | bytes 1048592 | tf_op jit(solution)/shard_map/all_gather | solution.py:62
  119.0 3.9 convolution_bitcast_fusion
  126.7 271.1 %all-reduce.12.cloned.1.call-done = (f32[1024,1024]{1,0:T(8,128)}, f32[3,1024,256]{2,1,0:T(8,128)}, f32[1024,1024]{1,0:T(8,128)}) async-done(((f32[1024,1024]{1,0:T(8,128)}, f32[3,1024,256]{2,1,0:T(8,128)}, f32[1024,1024]{1,0:T(8,128)}), (f32[1024,1024]{1,0:T(8,128)}, f32[3,1024,256]{2,1,0:T(8,128)}, f32[1024,1024]{1,0:T(8,128)})) %all-reduce.12.cloned.1.call-update) | async-done | bytes 11534352 | tf_op jit(solution)/shard_map/psum | solution.py:67
  402.0 2.5 copy.40
  410.3 2.2 reshape.285
  416.5 20.9 %while.30 = (s32[]{:T(128)}, bf16[2,4,512,64]{2,3,1,0:T(8,128)(2,1)S(1)}, f32[2,4,512]{2,1,0:T(4,128)S(1)}, s32[2]{0:T(128)S(1)}, s32[2,512]{1,0:T(2,128)S(1)}, ...) while((s32[]{:T(128)}, ...), condition=%wide.region_8.9_spmd.clone.clone, body=%wide.region_5.8_spmd.clone.sunk.clone | while | flops 563608064 | bytes 29178488 | solution.py:125
  418.3 2.6 fusion.157
  420.9 2.3 fusion.158
  423.3 3.7 fusion.159
  428.7 2.6 fusion.157
  431.4 2.3 fusion.158
  433.7 3.7 fusion.159
  438.9 12.7 %convert_reduce_fusion = (f32[1024]{0:T(1024)S(1)}, bf16[1024,1024]{1,0:T(8,128)(2,1)}, f32[1024,1024]{1,0:T(8,128)S(1)}) fusion(f32[1024,1024]{1,0:T(8,128)} %get-tuple-element.313, f32[1024,1024]{1,0:T(8,128)} %get-tuple-element.311, f32[1024]{0:T(1024)S(1)} %convert_element_type.132), kind=kLoop, calls=%fused_computation.57 | loop fusion | flops 78642176 | bytes 14688256 | tf_op jit(solution)/shard_map/reduce_sum | solution.py:192
  451.6 2.5 multiply_convert_fusion.1
  454.0 49.3 %while.31 = (s32[]{:T(128)}, f32[4,1024,64]{1,2,0:T(8,128)S(1)}, f32[4,1024,64]{1,2,0:T(8,128)}, f32[2,4,512,64]{2,3,1,0:T(8,128)}, s32[2]{0:T(128)S(1)}, /*inde...) while((s32[]{:T(128)}, f32[4,1024,64]{1,2,0:T(8,128)S(1)}, ...), condition=%wide.region_14.15_spmd.clone.clone, body=%wide.region_12.14_spmd.clone.sunk.clone | while | flops 1376647680 | bytes 143728416 | solution.py:177
  455.8 2.3 fusion.169
  458.1 4.6 multiply_reduce_fusion.3
  462.8 3.7 multiply_convert_fusion.4
  466.5 3.4 fusion.171
  469.8 4.8 fusion.173
  474.6 3.6 fusion.172
  479.9 2.3 fusion.169
  482.3 4.6 multiply_reduce_fusion.3
  486.9 3.7 multiply_convert_fusion.4
  490.6 3.4 fusion.171
  494.0 4.8 fusion.173
  498.8 4.6 fusion.172
  509.6 2.3 convert_element_type.141
  513.9 2.4 fusion.84
  516.3 4.3 fusion.86
  520.6 2.6 fusion.85
  525.5 2.9 fusion.80
  530.3 2.6 convolution_bitcast_fusion.1
  534.2 2.4 pad_maximum_fusion
  538.9 63.9 %all-reduce.1 = (f32[3,256]{1,0:T(4,128)}, f32[512]{0:T(512)S(1)}, f32[1024]{0:T(1024)}) all-reduce(f32[3,256]{1,0:T(4,128)S(1)} %convert_reduce_fusion.1, f32[512]{0:T(512)S(1)} %convert_reduce_fusion.2, f32[1024]{0:T(1024)S(1)} %get-tuple-element.314), channel_id=1, replica_groups=mesh['dp'=16,'row'=2,'col'=4] {'dp'}, use_global_device_ids=true, to_apply=%region_23.24 | all-reduce | flops 2304 | bytes 18432 | tf_op jit(solution)/shard_map/psum | solution.py:217
  602.8 80.3 %all-reduce.10.cloned.1.call-done = (f32[3,512,256]{1,2,0:T(8,128)}, f32[256,512]{1,0:T(8,128)}, f32[512,1024]{1,0:T(8,128)}, f32[1024,512]{1,0:T(8,128)}) async-done(((f32[3,512,256]{1,2,0:T(8,128)}, f32[256,512]{1,0:T(8,128)}, f32[512,1024]{1,0:T(8,128)}, f32[1024,512]{1,0:T(8,128)}), (f32[3,512,256]{1,2,0:T(8,128)}, f32[256,512]{1,0:T(8,128)}, f32[512,1024]{1,0:T(8,128)}, ...) | async-done | bytes 6291472 | tf_op jit(solution)/shard_map/psum | solution.py:217
  683.1 3.1 copy.55
  686.2 31.4 %reduce-scatter.3.cloned.1.call-done = f32[256,512]{1,0:T(8,128)} async-done(((f32[1024,512]{1,0:T(8,128)}), f32[256,512]{1,0:T(8,128)}) %reduce-scatter.3.cloned.1.call-update) | async-done | bytes 524304 | tf_op jit(solution)/shard_map/reduce_scatter | solution.py:130
  717.6 49.1 %reduce-scatter.5.cloned.1.call-done = f32[256,1024]{1,0:T(8,128)} async-done(((f32[1024,1024]{1,0:T(8,128)}), f32[256,1024]{1,0:T(8,128)}) %reduce-scatter.5.cloned.1.call-update) | async-done | bytes 1048592 | tf_op jit(solution)/shard_map/reduce_scatter | solution.py:198
  766.8 2.4 slice_reduce_fusion.1
  769.2 3.8 all-reduce.3
  773.0 160.8 %all-reduce = (f32[2,512]{1,0:T(2,128)}, f32[2,512]{1,0:T(2,128)}) all-reduce(f32[2,512]{1,0:T(2,128)S(1)} %pad_maximum_fusion.4, f32[2,512]{1,0:T(2,128)S(1)} %pad_maximum_fusion.5), channel_id=1, replica_groups=mesh['dp'=16,'row'=2,'col'=4] {'dp','col'}, use_global_device_ids=true, to_apply=%region_33.34 | all-reduce | flops 2048 | bytes 16384 | tf_op jit(solution)/shard_map/psum | solution.py:216
  936.1 3.2 copy.102
  (175 shorter events, 53.8 us)
Async XLA Ops:
  7.2 59.4 %copy-start = (bf16[1024,512]{1,0:T(8,128)(2,1)S(1)}, bf16[1024,512]{1,0:T(8,128)(2,1)}, u32[]{:S(2)}) copy-start(bf16[1024,512]{1,0:T(8,128)(2,1)} %param.25) | copy-start | bytes 3145732
  7.2 29.0 %all-gather.8.cloned.1.call-start = ((), (), s32[]{:S(2)}) async-start(), calls=%async_computation.5 | async-start | bytes 1310720 | tf_op jit(solution)/shard_map/all_gather | solution.py:140
  7.9 84.2 %all-gather.6.cloned.1.call-start = ((), (), s32[]{:S(2)}) async-start(), calls=%async_computation.3 | async-start | bytes 1310720 | tf_op jit(solution)/shard_map/all_gather | solution.py:63
  9.9 59.9 %copy-start.25 = (f32[1,512]{1,0:T(1,128)}, f32[1,512]{1,0:T(1,128)S(1)}, u32[]{:S(2)}) copy-start(f32[1,512]{1,0:T(1,128)S(1)} %get-tuple-element.342) | copy-start | bytes 6148
  9.9 59.9 %copy-start.27 = (f32[1,512]{1,0:T(1,128)}, f32[1,512]{1,0:T(1,128)S(1)}, u32[]{:S(2)}) copy-start(f32[1,512]{1,0:T(1,128)S(1)} %get-tuple-element.343) | copy-start | bytes 6148
  36.2 30.3 %copy-start.4 = (bf16[1024,512]{1,0:T(8,128)(2,1)S(1)}, bf16[1024,512]{1,0:T(8,128)(2,1)}, u32[]{:S(2)}) copy-start(bf16[1024,512]{1,0:T(8,128)(2,1)} %all-gather.8.cloned.1.call-done) | copy-start | bytes 3145732
  63.8 6.0 copy-start.29
  63.8 6.0 copy-start.31
  65.8 53.2 %all-gather.4.cloned.1.call-start = ((), (), s32[]{:S(2)}) async-start(), calls=%async_computation.2 | async-start | bytes 1310720 | tf_op jit(solution)/shard_map/all_gather | solution.py:62
  66.5 331.3 %all-reduce.12.cloned.1.call-start = ((), (), s32[]{:S(2)}) async-start(), calls=%async_computation.8 | async-start | bytes 23068672 | tf_op jit(solution)/shard_map/psum | solution.py:67
  69.8 49.2 %copy-start.16 = (bf16[3,512,256]{2,1,0:T(8,128)(2,1)S(1)}, bf16[3,512,256]{2,1,0:T(8,128)(2,1)}, u32[]{:S(2)}) copy-start(bf16[3,512,256]{2,1,0:T(8,128)(2,1)} %param.19) | copy-start | bytes 2359300
  122.9 0.7 copy-start.23
  122.9 0.7 copy-start.34
  122.9 2.4 copy-start.22
  122.9 560.2 %all-reduce.10.cloned.1.call-start = ((), (), s32[]{:S(2)}) async-start(), calls=%async_computation.7 | async-start | bytes 12582912 | tf_op jit(solution)/shard_map/psum | solution.py:217
  125.3 283.0 %copy-start.24 = (f32[1024,8]{0,1:T(8,128)}, f32[1024,8]{0,1:T(8,128)S(1)}, u32[]{:S(2)}) copy-start(f32[1024,8]{0,1:T(8,128)S(1)} %get-tuple-element.350) | copy-start | bytes 98308
  405.8 10.7 %copy-start.15 = (bf16[2,4,512,64]{2,3,1,0:T(8,128)(2,1)S(1)}, bf16[2,4,512,64]{2,3,1,0:T(8,128)(2,1)}, u32[]{:S(2)}) copy-start(bf16[2,4,512,64]{2,3,1,0:T(8,128)(2,1)} %broadcast_convert_fusion) | copy-start | bytes 1572868
  438.9 12.7 %copy-start.3 = (f32[1024,1024]{1,0:T(8,128)S(1)}, f32[1024,1024]{1,0:T(8,128)}, u32[]{:S(2)}) copy-start(f32[1024,1024]{1,0:T(8,128)} %get-tuple-element.311) | copy-start | bytes 12582916
  455.8 2.3 copy-start.8
  458.1 4.7 copy-start.1
  466.5 8.1 copy-start.2
  469.8 4.8 copy-start.9
  479.9 2.3 copy-start.8
  482.2 4.7 copy-start.1
  490.6 8.1 copy-start.2
  494.0 4.8 copy-start.9
  504.7 9.2 copy-start.5
  509.5 13.7 %copy-start.12 = (bf16[1,1024,256]{2,1,0:T(8,128)(2,1)}, bf16[1,1024,256]{2,1,0:T(8,128)(2,1)S(1)}, u32[]{:S(2)}) copy-start(bf16[1,1024,256]{2,1,0:T(8,128)(2,1)S(1)} %copy.50) | copy-start | bytes 1572868
  513.9 6.7 copy-start.6
  513.9 6.7 copy-start.17
  520.6 2.6 copy-start.13
  520.6 2.6 copy-start.20
  525.4 3.0 copy-start.10
  525.4 3.0 copy-start.18
  525.4 192.1 %reduce-scatter.3.cloned.1.call-start = ((), (), s32[]{:S(2)}) async-start(), calls=%async_computation.4 | async-start | bytes 2621440 | tf_op jit(solution)/shard_map/reduce_scatter | solution.py:130
  530.2 236.5 %reduce-scatter.5.cloned.1.call-start = ((), (), s32[]{:S(2)}) async-start(), calls=%async_computation.6 | async-start | bytes 5242880 | tf_op jit(solution)/shard_map/reduce_scatter | solution.py:198
  530.3 2.6 copy-start.7
  530.3 2.6 copy-start.38
  536.6 0.7 copy-start.37
  536.6 230.1 %copy-start.11 = (bf16[256,512]{1,0:T(8,128)(2,1)S(1)}, bf16[256,512]{1,0:T(8,128)(2,1)}, u32[]{:S(2)}) copy-start(bf16[256,512]{1,0:T(8,128)(2,1)} %param.17) | copy-start | bytes 786436
  536.6 230.1 %copy-start.26 = (f32[1,512]{1,0:T(1,128)S(1)}, f32[1,512]{1,0:T(1,128)}, u32[]{:S(2)}) copy-start(f32[1,512]{1,0:T(1,128)} %copy-done.25) | copy-start | bytes 6148
  536.6 230.1 %copy-start.28 = (f32[1,512]{1,0:T(1,128)S(1)}, f32[1,512]{1,0:T(1,128)}, u32[]{:S(2)}) copy-start(f32[1,512]{1,0:T(1,128)} %copy-done.27) | copy-start | bytes 6148
  536.6 230.1 %copy-start.30 = (f32[256]{0:T(256)S(1)}, f32[256]{0:T(256)}, u32[]{:S(2)}) copy-start(f32[256]{0:T(256)} %copy-done.29) | copy-start | bytes 3076
  536.6 230.1 %copy-start.32 = (f32[256]{0:T(256)S(1)}, f32[256]{0:T(256)}, u32[]{:S(2)}) copy-start(f32[256]{0:T(256)} %copy-done.31) | copy-start | bytes 3076
  537.3 396.5 %copy-start.19 = (bf16[256,512]{1,0:T(8,128)(2,1)S(1)}, bf16[256,512]{1,0:T(8,128)(2,1)}, u32[]{:S(2)}) copy-start(bf16[256,512]{1,0:T(8,128)(2,1)} %param.29) | copy-start | bytes 786436
  602.8 336.5 %copy-start.35 = (f32[512]{0:T(512)}, f32[512]{0:T(512)S(1)}, u32[]{:S(2)}) copy-start(f32[512]{0:T(512)S(1)} %get-tuple-element.632) | copy-start | bytes 6148
  683.1 252.2 %copy-start.21 = (f32[256,512]{1,0:T(8,128)S(1)}, f32[256,512]{1,0:T(8,128)}, u32[]{:S(2)}) copy-start(f32[256,512]{1,0:T(8,128)} %get-tuple-element.631) | copy-start | bytes 1572868
  933.8 5.5 copy-start.14
  (2 other events, 1.4 us)
Sparse Core Ops, SparseCore 0:
  9.7 26.4 all-gather.7
  65.9 26.1 all-gather.5
  94.4 24.5 all-gather.3
  123.0 274.7 all-reduce.11
  525.5 157.5 all-reduce.9
  686.0 31.5 reduce-scatter.2
  720.1 46.5 reduce-scatter.4
where the time goes:
time: 957 us; the launch traced here: 947 us
  waiting for transfers between devices  503 us (53%)
  blocking collectives  254 us (27%)
  matrix products  84.5 us (9%)
  other arithmetic  55.4 us (6%)
  local copies, waits for them, and re-layouts  34.8 us (4%)
  between operations  14.5 us (2%)
    psum x1, waiting for transfers between devices, on_device(): qkv_sum, up_sum = lax.psum((qkv_part, up_part), 'row')  271 us
    psum x1, blocking collectives, on_device(): gain_grad, shift_grad = lax.psum((gain_grad, shift_grad), ('dp', 'col'))  161 us
    psum x1, waiting for transfers between devices, on_device(): lax.psum((w_qkv_grad, b_qkv_grad, w_out_grad, out_bias_grad, w_up_grad, b...  80.3 us
    psum x1, blocking collectives, on_device(): lax.psum((w_qkv_grad, b_qkv_grad, w_out_grad, out_bias_grad, w_up_grad, b...  63.9 us
    reduce_scatter x1, waiting for transfers between devices, on_device(): lax.psum_scatter(jnp.concatenate([first_term, second_term], axis=1), 'col...  49.1 us
    reduce_scatter x1, waiting for transfers between devices, on_device(): lax.psum_scatter(jnp.dot(attn_out, w_out, preferred_element_type=jnp.floa...  31.4 us
    psum x1, blocking collectives, on_device(): lax.psum((jnp.sum(x_in, axis=1), jnp.sum(x_in * x_in, axis=1)), 'row')  25.7 us
    all_gather x1, waiting for transfers between devices, on_device(): grad_all = lax.all_gather(cotangent, 'col', axis=0, tiled=True)  25.6 us
  transfers between devices with their start and end apart: 7, of which 7 were waited for; matrix products, arithmetic and copies ran while one was open for 3% of the time, Pallas kernels for 0%

commit v1 on v0

v1 whole, which is shorter than its diff:
```python
from types import SimpleNamespace
import math

import numpy as np
import jax
import jax.numpy as jnp
from jax import lax
from jax.experimental import pallas as pl
from jax.experimental.pallas import tpu as pltpu
from jax.sharding import PartitionSpec as P

MESH = pl.DeviceIdType.MESH
BF = jnp.bfloat16
F32 = jnp.float32
T = 1024
D = 1024
HD = 64
ROT = 16
E = 128
F = 512
B = 256
EPSILON = 1e-05
NSEM = 96


def nn(a, b):
    return jnp.dot(a, b, preferred_element_type=F32)


def nt(a, b):
    return lax.dot_general(a, b, (((1,), (1,)), ((), ())), preferred_element_type=F32)


def tn(a, b):
    return lax.dot_general(a, b, (((0,), (0,)), ((), ())), preferred_element_type=F32)


def rows(block, size=B):
    return pl.ds(pl.multiple_of(block * size, size), size)


class Net:
    def __init__(self, send, recv):
        self.send, self.recv, self.count, self.sent = send, recv, 0, []

    def go(self, src, dst, device):
        k = self.count
        self.count += 1
        assert k < NSEM
        copy = pltpu.make_async_remote_copy(
            src_ref=src,
            dst_ref=dst,
            send_sem=self.send.at[k],
            recv_sem=self.recv.at[k],
            device_id=device,
            device_id_type=MESH,
        )
        copy.start()
        self.sent.append(copy)
        return copy

    def local(self, src, dst):
        k = self.count
        self.count += 1
        assert k < NSEM
        copy = pltpu.make_async_copy(src, dst, self.send.at[k])
        copy.start()
        return copy


def gather_tokens(net, own, full, at, half, col, row):
    right, left, peer = at["z1"], at["z3"], at["y1"]

    def place(c, h):
        return full.at[rows(c), pl.ds(pl.multiple_of(h * half, half), half)]

    mine, other = place(col, row), place(col, 1 - row)
    lcol, rcol = lax.rem(col + 3, 4), lax.rem(col + 1, 4)
    c0 = net.go(own, mine, peer)
    c1 = net.go(own, mine, right)
    c2 = net.go(own, mine, left)
    keep = net.local(own, mine)
    yield
    c0.wait_recv()
    c3 = net.go(other, other, right)
    c4 = net.go(other, other, left)
    yield
    c1.wait_recv()
    c5 = net.go(place(lcol, row), place(lcol, row), right)
    yield
    c4.wait_recv()
    c6 = net.go(place(rcol, 1 - row), place(rcol, 1 - row), left)
    yield
    keep.wait()
    c2.wait_recv()
    c3.wait_recv()
    yield
    c5.wait_recv()
    c6.wait_recv()


def ring_scatter(net, part, bufs, me, right, left, size, width):
    ta, tb, inl, inr = bufs
    lo, hi = pl.ds(0, width), pl.ds(width, width)
    far, rb, lb = lax.rem(me + 2, 4), lax.rem(me + 1, 4), lax.rem(me + 3, 4)
    a = net.go(part(far, lo), ta, right)
    b = net.go(part(far, hi), tb, left)
    c = net.go(part(rb, hi), inl.at[:, hi], right)
    d = net.go(part(lb, lo), inr.at[:, lo], left)
    yield
    a.wait_recv()
    view = part(rb, lo)
    view[...] = (view[...].astype(F32) + ta[...].astype(F32)).astype(BF)
    e = net.go(view, inl.at[:, lo], right)
    b.wait_recv()
    view = part(lb, hi)
    view[...] = (view[...].astype(F32) + tb[...].astype(F32)).astype(BF)
    f = net.go(view, inr.at[:, hi], left)
    yield
    for copy in (c, d, e, f):
        copy.wait_recv()


def reduce_weights(net, grad, s, at, me, n):
    core, x, row = me["core"], me["x"], me["row"]
    half, size = n // 2, n // 8
    base = core * half
    away = (1 - core) * half
    c = net.go(grad.at[pl.ds(pl.multiple_of(away, half), half)], s.rc, at["core"])
    yield
    c.wait_recv()
    own = grad.at[pl.ds(pl.multiple_of(base, half), half)]
    own[...] = (own[...].astype(F32) + s.rc[...].astype(F32)).astype(BF)

    def part(block, cols):
        return grad.at[pl.ds(pl.multiple_of(base + block * size, size), size), cols]

    yield from ring_scatter(
        net, part, (s.ta, s.tb, s.inl, s.inr), x, at["x1"], at["x3"], size, D // 2
    )
    for h in range(2):
        cols = pl.ds(h * (D // 2), D // 2)
        total = (
            part(x, cols)[...].astype(F32) + s.inl[:, cols].astype(F32) + s.inr[:, cols].astype(F32)
        )
        s.sy[h] = total.astype(BF)
    g0 = net.go(s.sy.at[row], s.ry.at[0], at["y2"])
    g1 = net.go(s.sy.at[1 - row], s.ry.at[1], at["y1"])
    g2 = net.go(s.sy.at[1 - row], s.ry.at[2], at["y3"])
    yield
    g0.wait_recv()
    s.fin[core, x, row] = (s.sy[row].astype(F32) + s.ry[0].astype(F32)).astype(BF)
    g1.wait_recv()
    g2.wait_recv()
    s.fin[core, x, 1 - row] = (s.ry[1].astype(F32) + s.ry[2].astype(F32)).astype(BF)
    h0 = s.fin.at[core, x, 0]
    h1 = s.fin.at[core, x, 1]
    a0 = net.go(h0, h0, at["x1"])
    a1 = net.go(h1, h1, at["x3"])
    a2 = net.go(h1, h1, at["x1"])
    a3 = net.go(h0, h0, at["x3"])
    k0 = net.go(s.fin.at[core, x], s.fin.at[core, x], at["core"])
    yield
    lx, rx = lax.rem(x + 3, 4), lax.rem(x + 1, 4)
    a0.wait_recv()
    v = s.fin.at[core, lx, 0]
    a4 = net.go(v, v, at["x1"])
    a1.wait_recv()
    v = s.fin.at[core, rx, 1]
    a5 = net.go(v, v, at["x3"])
    a2.wait_recv()
    v = s.fin.at[core, lx]
    k1 = net.go(v, v, at["core"])
    a3.wait_recv()
    v = s.fin.at[core, rx]
    k2 = net.go(v, v, at["core"])
    yield
    a4.wait_recv()
    a5.wait_recv()
    v = s.fin.at[core, lax.rem(x + 2, 4)]
    k3 = net.go(v, v, at["core"])
    for copy in (k0, k1, k2):
        copy.wait_recv()
    yield
    k3.wait_recv()


def reduce_vectors(net, s, at):
    c = net.go(s.vec, s.vr.at[0], at["core"])
    yield
    c.wait_recv()
    s.vs[0] = s.vec[...] + s.vr[0]
    for n, axis in enumerate("xyz"):
        copies = [net.go(s.vs.at[n], s.vr.at[3 * n + k], at[axis + str(k)]) for k in (1, 2, 3)]
        yield
        for copy in copies:
            copy.wait_recv()
        s.vs[n + 1] = (s.vs[n] + s.vr[3 * n + 1]) + (s.vr[3 * n + 2] + s.vr[3 * n + 3])


def step(gen):
    next(gen, None)


def finish(gen):
    for _ in gen:
        pass


def interleave(*gens):
    live = list(gens)
    while live:
        for gen in list(live):
            try:
                next(gen)
            except StopIteration:
                live.remove(gen)


def turn(values, cos, sin):
    lane = lax.broadcasted_iota(jnp.int32, values.shape, 1)
    other = jnp.where(lane % HD < ROT // 2, pltpu.roll(values, E - ROT // 2, 1), pltpu.roll(values, ROT // 2, 1))
    return values * cos + other * sin


def split_heads(ref, at_rows, values):
    lane = lax.broadcasted_iota(jnp.int32, values.shape, 1)
    zero = jnp.zeros_like(values)
    ref[0, at_rows, :] = jnp.where(lane < HD, values, zero).astype(BF)
    ref[1, at_rows, :] = jnp.where(lane < HD, zero, values).astype(BF)


SCRATCH = dict(
    xall=((T, D), BF),
    gall=((T, D), BF),
    ain=((T, D), BF),
    mim=((T, D), BF),
    wq=((D, 3 * E), BF),
    wo=((E, D), BF),
    wu=((D, F), BF),
    wd=((F, D), BF),
    nb=((2, 8, D // 2), F32),
    mean=((T, 1), F32),
    inv=((T, 1), F32),
    hid=((T, F), BF),
    hpg=((T, F), BF),
    qs=((T, E), BF),
    qsm=((2, T, E), BF),
    km=((2, T, E), BF),
    vm=((2, T, E), BF),
    kt=((E, T), BF),
    vt=((E, T), BF),
    do=((T, E), BF),
    dom=((2, T, E), BF),
    probs=((2, 2560, B), F32),
    mt=((E, T), BF),
    mixed=((T, E), BF),
    dqt=((E, T), F32),
    dk=((T, E), F32),
    dv=((T, E), F32),
    qkvg=((T, 3 * E), BF),
    op=((T, D), BF),
    ng=((T, D), BF),
    ota=((B, D // 2), BF),
    otb=((B, D // 2), BF),
    oinl=((B, D), BF),
    oinr=((B, D), BF),
    nta=((B, D // 2), BF),
    ntb=((B, D // 2), BF),
    ninl=((B, D), BF),
    ninr=((B, D), BF),
    ysend=((2, B, D // 2), BF),
    yrecv=((2, B, D // 2), BF),
    ssend=((B, 128), F32),
    srecv=((B, 128), F32),
    gm=((2 * F, D), BF),
    ga=((4 * E, D), BF),
    mrc=((F, D), BF),
    mta=((F // 4, D // 2), BF),
    mtb=((F // 4, D // 2), BF),
    minl=((F // 4, D), BF),
    minr=((F // 4, D), BF),
    msy=((2, F // 4, D // 2), BF),
    mry=((3, F // 4, D // 2), BF),
    arc=((2 * E, D), BF),
    ata=((E // 2, D // 2), BF),
    atb=((E // 2, D // 2), BF),
    ainl=((E // 2, D), BF),
    ainr=((E // 2, D), BF),
    asy=((2, E // 2, D // 2), BF),
    ary=((3, E // 2, D // 2), BF),
    vec=((8, D), F32),
    vr=((10, 8, D), F32),
    vs=((4, 8, D), F32),
)


def body(
    tok, cot, wqkv, wout, wup, wdown, small, segc, segr, ctab, stab,
    out, tgrad, fm, fa, vout, *scratch,
):
    s = SimpleNamespace(**dict(zip(SCRATCH, scratch)))
    send, recv = scratch[len(SCRATCH) :]
    net = Net(send, recv)
    dp, row, col = lax.axis_index("dp"), lax.axis_index("row"), lax.axis_index("col")
    core, x, yh = lax.rem(dp, 2), lax.rem(dp // 2, 4), dp // 8
    half = D // 2

    def dev(core=core, x=x, yh=yh, row=row, col=col):
        return (yh * 8 + x * 2 + core, row, col)

    at = {"core": dev(core=1 - core)}
    for k in (1, 2, 3):
        at[f"x{k}"] = dev(x=lax.rem(x + k, 4))
        at[f"z{k}"] = dev(col=lax.rem(col + k, 4))
    at["y1"] = dev(row=1 - row)
    at["y2"] = dev(yh=1 - yh)
    at["y3"] = dev(yh=1 - yh, row=1 - row)

    barrier = pltpu.get_barrier_semaphore()
    for device in at.values():
        pl.semaphore_signal(barrier, inc=1, device_id=device, device_id_type=MESH)
    pl.semaphore_wait(barrier, len(at))

    gx = gather_tokens(net, tok, s.xall, at, half, col, row)
    gg = gather_tokens(net, cot, s.gall, at, half, col, row)
    step(gx)

    mine, theirs = row, 1 - row
    drows = rows(row, half)
    y1, y3 = at["y1"], at["y3"]
    nbc = net.go(small.at[pl.ds(8, 8), pl.ds(0, half)], s.nb.at[row], y1)

    def shares(which):
        ecols = pl.ds(pl.multiple_of(which * E, E), E)
        fcols = pl.ds(pl.multiple_of(which * F, F), F)
        pairs = [(wqkv.at[k, :, ecols], s.wq.at[drows, pl.ds(k * E, E)]) for k in range(3)]
        pairs.append((wup.at[:, fcols], s.wu.at[drows]))
        pairs.append((wout.at[ecols], s.wo.at[:, drows]))
        pairs.append((wdown.at[fcols], s.wd.at[:, drows]))
        return pairs

    far = [y1, y1, y1, y3, y1, y3]
    wc = [net.go(a, b, d) for (a, b), d in zip(shares(theirs), far)]
    wl = [net.local(a, b) for a, b in shares(mine)]
    step(gx)
    s.nb[row] = small[pl.ds(8, 8), pl.ds(0, half)]
    s.vec[...] = jnp.zeros_like(s.vec)
    s.dk[...] = jnp.zeros_like(s.dk)
    s.dv[...] = jnp.zeros_like(s.dv)
    step(gg)
    step(gx)
    step(gx)
    step(gg)
    nbc.wait_recv()
    finish(gx)

    def wide(k):
        return jnp.concatenate([s.nb[0, k : k + 1, :], s.nb[1, k : k + 1, :]], axis=1)

    gain0, gain1, bias0, bias1 = wide(0), wide(1), wide(2), wide(3)

    @pl.loop(0, 8)
    def _(b):
        r = rows(b, 128)
        xv = s.xall[r, :].astype(F32)
        mean = jnp.sum(xv, axis=1, keepdims=True) * (1.0 / D)
        square = jnp.sum(xv * xv, axis=1, keepdims=True) * (1.0 / D)
        inv = lax.rsqrt(square - mean * mean + EPSILON)
        normed = (xv - mean) * inv
        s.mean[r, :] = mean
        s.inv[r, :] = inv
        s.ain[r, :] = (normed * gain0 + bias0).astype(BF)
        s.mim[r, :] = (normed * gain1 + bias1).astype(BF)

    step(gg)
    for copy in wl:
        copy.wait()
    for copy in wc:
        copy.wait_recv()

    ecols = pl.ds(pl.multiple_of(row * E, E), E)
    bq = jnp.concatenate([small[k : k + 1, ecols] for k in range(3)], axis=1)
    bu = small[3:4, pl.ds(pl.multiple_of(row * F, F), F)]

    @pl.loop(0, 4)
    def _(b):
        r = rows(b)
        pre = nn(s.ain[r, :], s.wq[...]) + bq
        cos, sin = ctab[r, :], stab[r, :]
        query = (turn(pre[:, :E], cos, sin)).astype(BF).astype(F32) * (1.0 / math.sqrt(HD))
        key = turn(pre[:, E : 2 * E], cos, sin).astype(BF).astype(F32)
        value = pre[:, 2 * E :].astype(BF).astype(F32)
        s.qs[r, :] = query.astype(BF)
        split_heads(s.qsm, r, query)
        split_heads(s.km, r, key)
        split_heads(s.vm, r, value)
        s.kt[:, r] = key.T.astype(BF)
        s.vt[:, r] = value.T.astype(BF)

    finish(gg)

    @pl.loop(0, 4)
    def _(b):
        r = rows(b)
        pre = nn(s.mim[r, :], s.wu[...]) + bu
        cdf = 0.5 * (1.0 + lax.erf(pre * math.sqrt(0.5)))
        s.hid[r, :] = (pre * cdf).astype(BF)
        slope = cdf + pre * jnp.exp(-0.5 * pre * pre) * (1.0 / math.sqrt(2.0 * math.pi))
        back = (nt(s.gall[r, :], s.wd[...]) * slope).astype(BF)
        s.hpg[r, :] = back
        fcols = pl.ds(pl.multiple_of(row * F, F), F)
        s.vec[6:7, fcols] += jnp.sum(back.astype(F32), axis=0, keepdims=True)
        gcols = pl.ds(pl.multiple_of(row * half, half), half)
        s.vec[4:5, gcols] += jnp.sum(s.gall[r, gcols].astype(F32), axis=0, keepdims=True)
        dout = nt(s.gall[r, :], s.wo[...]).astype(BF).astype(F32)
        s.do[r, :] = dout.astype(BF)
        split_heads(s.dom, r, dout)

    @pl.loop(0, 4)
    def _(b):
        r = rows(b, 128)
        s.gm[r, :] = tn(s.hid[:, r], s.gall[...]).astype(BF)
        r2 = pl.ds(pl.multiple_of(F + b * 128, 128), 128)
        s.gm[r2, :] = tn(s.hpg[:, r], s.mim[...]).astype(BF)

    sm = SimpleNamespace(
        rc=s.mrc, ta=s.mta, tb=s.mtb, inl=s.minl, inr=s.minr, sy=s.msy, ry=s.mry, fin=fm
    )
    sa = SimpleNamespace(
        rc=s.arc, ta=s.ata, tb=s.atb, inl=s.ainl, inr=s.ainr, sy=s.asy, ry=s.ary, fin=fa
    )
    where = dict(core=core, x=x, row=row)
    rm = reduce_weights(net, s.gm, sm, at, where, 2 * F)
    step(rm)

    first = [0, 256, 768, 1536]
    for i in range(4):
        n = (i + 1) * B
        q = pl.ds(i * B, B)

        @pl.loop(0, 2)
        def _(h):
            scores = nt(s.km[h, pl.ds(0, n), :], s.qs[q, :])
            kid = lax.broadcasted_iota(jnp.int32, (n, B), 0)
            qid = lax.broadcasted_iota(jnp.int32, (n, B), 1) + i * B
            allowed = (kid <= qid) & (segc[pl.ds(0, n), :] == segr[:, q])
            scores = jnp.where(allowed, scores, -1e30)
            top = jnp.max(scores, axis=0, keepdims=True)
            expo = jnp.exp(scores - top)
            probs = expo * (1.0 / jnp.sum(expo, axis=0, keepdims=True))
            s.probs[h, pl.ds(first[i], n), :] = probs
            hrows = rows(h, HD)
            s.mt[hrows, q] = nn(s.vt[hrows, pl.ds(0, n)], probs.astype(BF)).astype(BF)

        s.mixed[q, :] = s.mt[:, q].astype(F32).T.astype(BF)
        step(rm) if i in (0, 2, 3) else None

    @pl.loop(0, 4)
    def _(b):
        r = rows(b)
        s.op[r, :] = (nn(s.mixed[r, :], s.wo[...]) + nn(s.hid[r, :], s.wd[...])).astype(BF)

    def opart(block, cols):
        return s.op.at[rows(block), cols]

    def npart(block, cols):
        return s.ng.at[rows(block), cols]

    ro = ring_scatter(
        net, opart, (s.ota, s.otb, s.oinl, s.oinr), col, at["z1"], at["z3"], B, half
    )
    step(ro)
    s.ga[0:E, :] = nn(s.mt[...], s.gall[...]).astype(BF)

    for i in range(4):
        n = (i + 1) * B
        q = pl.ds(i * B, B)

        @pl.loop(0, 2)
        def _(h):
            probs = s.probs[h, pl.ds(first[i], n), :]
            dprob = nt(s.vm[h, pl.ds(0, n), :], s.do[q, :])
            inner = jnp.sum(probs * dprob, axis=0, keepdims=True)
            dscore = (probs * (dprob - inner)).astype(BF)
            s.dv[pl.ds(0, n), :] += nn(probs.astype(BF), s.dom[h, q, :])
            s.dk[pl.ds(0, n), :] += nn(dscore, s.qsm[h, q, :])
            hrows = rows(h, HD)
            s.dqt[hrows, q] = nn(s.kt[hrows, pl.ds(0, n)], dscore) * (1.0 / math.sqrt(HD))

        step(rm) if i in (0, 2) else None
        step(ro) if i == 1 else None

    @pl.loop(0, 4)
    def _(b):
        r = rows(b)
        cos, sin = ctab[r, :], -stab[r, :]
        dq = turn(s.dqt[:, r].T, cos, sin).astype(BF)
        dk = turn(s.dk[r, :], cos, sin).astype(BF)
        dv = s.dv[r, :].astype(BF)
        both = jnp.concatenate([dq, dk, dv], axis=1)
        s.qkvg[r, :] = both
        ecols3 = pl.ds(pl.multiple_of(row * 3 * E, 3 * E), 3 * E)
        s.vec[5:6, ecols3] += jnp.sum(both.astype(F32), axis=0, keepdims=True)

    @pl.loop(0, 4)
    def _(b):
        r = rows(b)
        attn = nt(s.qkvg[r, :], s.wq[...])
        mlp = nt(s.hpg[r, :], s.wu[...])
        normed = (s.xall[r, :].astype(F32) - s.mean[r, :]) * s.inv[r, :]
        s.ng[r, :] = (attn * gain0 + mlp * gain1).astype(BF)
        s.vec[0:1, :] += jnp.sum(attn * normed, axis=0, keepdims=True)
        s.vec[1:2, :] += jnp.sum(mlp * normed, axis=0, keepdims=True)
        s.vec[2:3, :] += jnp.sum(attn, axis=0, keepdims=True)
        s.vec[3:4, :] += jnp.sum(mlp, axis=0, keepdims=True)

    rn = ring_scatter(
        net, npart, (s.nta, s.ntb, s.ninl, s.ninr), col, at["z1"], at["z3"], B, half
    )
    step(rn)

    @pl.loop(0, 3)
    def _(b):
        r = rows(b, E)
        r2 = pl.ds(pl.multiple_of(E + b * E, E), E)
        s.ga[r2, :] = tn(s.qkvg[:, r], s.ain[...]).astype(BF)

    ra = reduce_weights(net, s.ga, sa, at, where, 4 * E)
    step(ra)
    rv = reduce_vectors(net, s, at)
    step(rv)
    finish(ro)

    def summed(part, inl, inr, h):
        cols = pl.ds(h * half, half)
        return (
            part(col, cols)[...].astype(F32) + inl[:, cols].astype(F32) + inr[:, cols].astype(F32)
        )

    for h in range(2):
        s.ysend[h] = summed(opart, s.oinl, s.oinr, h).astype(BF)
    yo = net.go(s.ysend.at[1 - row], s.yrecv.at[0], y1)
    step(rv)
    step(ra)
    step(rm)
    step(rn)
    yo.wait_recv()
    out[...] = (
        tok[...].astype(F32)
        + s.ysend[row].astype(F32)
        + s.yrecv[0].astype(F32)
        + small[4:5, pl.ds(0, half)]
        + small[5:6, pl.ds(0, half)]
    ).astype(BF)
    step(rv)
    step(ra)
    step(rv)
    step(ra)
    finish(rn)
    r = rows(col)
    mean, inv = s.mean[r, :], s.inv[r, :]
    first_sum = jnp.zeros((B, 1), F32)
    second_sum = jnp.zeros((B, 1), F32)
    for h in range(2):
        total = summed(npart, s.ninl, s.ninr, h)
        normed = (s.xall[r, pl.ds(h * half, half)].astype(F32) - mean) * inv
        first_sum += jnp.sum(total, axis=1, keepdims=True)
        second_sum += jnp.sum(total * normed, axis=1, keepdims=True)
        npart(col, pl.ds(h * half, half))[...] = total.astype(BF)
    lane = lax.broadcasted_iota(jnp.int32, (B, 128), 1)
    s.ssend[...] = jnp.where(lane < 64, first_sum, second_sum)
    rhalf = pl.ds(pl.multiple_of(row * half, half), half)
    ohalf = pl.ds(pl.multiple_of((1 - row) * half, half), half)
    yn = net.go(npart(col, ohalf), s.yrecv.at[1], y1)
    ys = net.go(s.ssend, s.srecv, y1)
    interleave(rv, ra, rm)
    vout[0] = s.vs[2]
    vout[1] = s.vs[3]
    yn.wait_recv()
    ys.wait_recv()
    sums = (s.ssend[...] + s.srecv[...]) * (1.0 / D)
    normed = (tok[...].astype(F32) - mean) * inv
    total = npart(col, rhalf)[...].astype(F32) + s.yrecv[1].astype(F32)
    tgrad[...] = (
        cot[...].astype(F32) + inv * (total - sums[:, 0:1] - normed * sums[:, 64:65])
    ).astype(BF)
    for copy in net.sent:
        copy.wait_send()


def tables():
    freq = np.arange(ROT // 2, dtype=np.float32)
    inverse = np.float32(10000.0) ** (np.float32(-2.0) * freq / np.float32(ROT))
    angle = np.arange(T, dtype=np.float32)[:, None] * inverse[None, :].astype(np.float32)
    cos, sin = np.cos(angle), np.sin(angle)
    ones, zeros = np.ones((T, HD - ROT), np.float32), np.zeros((T, HD - ROT), np.float32)
    ctab = np.concatenate([cos, cos, ones] * 2, axis=1)
    stab = np.concatenate([-sin, sin, zeros] * 2, axis=1)
    return ctab.astype(np.float32), stab.astype(np.float32)


def on_device(
    tokens, segment_ids, w_qkv, b_qkv, w_out, b_out, w_up, b_up, w_down, b_down, norm_gain, norm_bias, cotangent
):
    def line(values):
        values = values.astype(F32).reshape(-1, values.shape[-1])
        return jnp.pad(values, ((0, 0), (0, D - values.shape[1])))

    small = jnp.concatenate(
        [line(v) for v in (b_qkv, b_up, b_out, b_down)]
        + [jnp.zeros((2, D), F32), line(norm_gain), line(norm_bias), jnp.zeros((4, D), F32)]
    )
    ctab, stab = tables()
    vmem = pl.BlockSpec(memory_space=pltpu.VMEM)
    hbm = pl.BlockSpec(memory_space=pl.ANY)
    shape = jax.ShapeDtypeStruct
    out, tgrad, fm, fa, vec = pl.pallas_call(
        body,
        out_shape=[
            shape((B, D // 2), BF),
            shape((B, D // 2), BF),
            shape((2, 4, 2, F // 4, D // 2), BF),
            shape((2, 4, 2, E // 2, D // 2), BF),
            shape((2, 8, D), F32),
        ],
        in_specs=[vmem, vmem, hbm, hbm, hbm, hbm, vmem, vmem, vmem, vmem, vmem],
        out_specs=[vmem] * 5,
        scratch_shapes=[pltpu.VMEM(*spec) for spec in SCRATCH.values()]
        + [pltpu.SemaphoreType.DMA((NSEM,)), pltpu.SemaphoreType.DMA((NSEM,))],
        compiler_params=pltpu.CompilerParams(
            collective_id=0, has_side_effects=True, vmem_limit_bytes=60 * 1024 * 1024
        ),
        name="block",
    )(
        tokens, cotangent, w_qkv, w_out, w_up, w_down, small,
        segment_ids.reshape(T, 1), segment_ids.reshape(1, T), jnp.asarray(ctab), jnp.asarray(stab),
    )
    row = lax.axis_index("row")
    fm = fm.astype(F32)
    w_down_grad = fm[0].transpose(1, 0, 2, 3).reshape(2 * F, D // 2)
    w_up_grad = fm[1].transpose(3, 1, 0, 2).reshape(D // 2, 2 * F)
    fa = fa.astype(F32).reshape(4, 2, 2, E // 2, D // 2)
    w_out_grad = fa[0].transpose(1, 0, 2, 3).reshape(2 * E, D // 2)
    w_qkv_grad = fa[1:].transpose(0, 4, 2, 1, 3).reshape(3, D // 2, 2 * E)
    rhalf = lambda v: lax.dynamic_slice_in_dim(v, row * (D // 2), D // 2, axis=-1)
    b_out_grad = rhalf(vec[0, 4])
    b_qkv_grad = vec[0, 5, : 6 * E].reshape(2, 3, E).transpose(1, 0, 2).reshape(3, 2 * E)
    b_up_grad = vec[0, 6]
    gain_grad = rhalf(vec[1, 0:2])
    bias_grad = rhalf(vec[1, 2:4])
    return (
        out, tgrad, w_qkv_grad, b_qkv_grad, w_out_grad, b_out_grad,
        w_up_grad, b_up_grad, w_down_grad, b_out_grad, gain_grad, bias_grad,
    )


def solution(mesh):
    in_specs = (
        P(("dp", "col"), "row"),
        P("dp"),
        P(None, "row", "col"),
        P(None, "col"),
        P("col", "row"),
        P("row"),
        P("row", "col"),
        P("col"),
        P("col", "row"),
        P("row"),
        P(None, "row"),
        P(None, "row"),
        P(("dp", "col"), "row"),
    )
    out_specs = (
        P(("dp", "col"), "row"),
        P(("dp", "col"), "row"),
        P(None, "row", "col"),
        P(None, "col"),
        P("col", "row"),
        P("row"),
        P("row", "col"),
        P("col"),
        P("col", "row"),
        P("row"),
        P(None, "row"),
        P(None, "row"),
    )
    return jax.shard_map(
        on_device, mesh=mesh, in_specs=in_specs, out_specs=out_specs, check_vma=False
    )
```

time: 957 us -> 147 us (0.15)
  waiting for transfers between devices: 503 us -> 0 us
  blocking collectives: 254 us -> 0 us
  Pallas kernels: 0 us -> 120 us
  matrix products: 84.5 us -> 0 us
  other arithmetic: 55.4 us -> 4.51 us
  between operations: 14.5 us -> 0.72 us
  local copies, waits for them, and re-layouts: 34.8 us -> 21.1 us
    psum x2 -> x0, waiting for transfers between devices: 351 us -> none  [the longest x1 271 us: on_device(): qkv_sum, up_sum = lax.psum((qkv_part, up_part), 'row')]
    psum x4 -> x0, blocking collectives: 254 us -> none  [the longest x1 161 us: on_device(): gain_grad, shift_grad = lax.psum((gain_grad, shift_grad), ('dp', 'col'))]
    pallas_call x0 -> x1, Pallas kernels: none -> 120 us  [on_device(): pl.pallas_call(body, out_shape=[shape((B, D // 2), BF), shape((B, D // 2)...]
    dot_general x26 -> x0, matrix products: 84.5 us -> none  [the longest x4 9.87 us: block_scores(): jnp.einsum('hqd,hkd->hqk', query_blk, key_heads, preferred_element_type=j...]
    reduce_scatter x2 -> x0, waiting for transfers between devices: 80.5 us -> none  [the longest x1 49.1 us: on_device(): lax.psum_scatter(jnp.concatenate([first_term, second_term], axis=1), 'col...]
    all_gather x3 -> x0, waiting for transfers between devices: 70 us -> none  [the longest x1 25.6 us: on_device(): grad_all = lax.all_gather(cotangent, 'col', axis=0, tiled=True)]
    reduce_sum x7 -> x0, other arithmetic: 22.6 us -> none  [the longest x1 12.7 us: on_device(): b_up_grad = jnp.sum(hidden_pre_grad, axis=0, dtype=jnp.float32)]
    convert_element_type x10 -> x1, other arithmetic: 15.1 us -> 2.15 us  [on_device(): fm = fm.astype(F32)]
  transfers between devices with their start and end apart: 7 -> 0, of which waited for: 7 -> 0; matrix products, arithmetic and copies ran while one was open for 3% -> 0% of each run, Pallas kernels for 0% -> 0%
where the time goes in v1:
time: 147 us; the launch traced here: 146 us
  Pallas kernels  120 us (82%)
  local copies, waits for them, and re-layouts  21.1 us (14%)
  other arithmetic  4.51 us (3%)
    pallas_call x1, Pallas kernels, on_device(): pl.pallas_call(body, out_shape=[shape((B, D // 2), BF), shape((B, D // 2)...  120 us
    unnamed x14, local copies, waits for them, and re-layouts  5.55 us
    transpose x2, local copies, waits for them, and re-layouts, on_device(): w_down_grad = fm[0].transpose(1, 0, 2, 3).reshape(2 * F, D // 2)  5.15 us

profile of v1, /device:TPU:1, one launch (start us, length us, event | category | flops | bytes accessed | tf_op | source)
XLA Modules:
  0.0 146.2 jit_solution(11789414574608867215)
XLA Ops:
  0.6 0.7 pad_convert_fusion.1
  1.3 0.7 reshape.70
  2.0 0.7 reshape.71
  2.7 0.7 pad_convert_fusion
  3.4 0.7 reshape.81
  4.1 1.3 concatenate.3.small
  5.4 1.7 %copy.30.segc = s32[1024,1]{1,0:T(8,128)} copy(s32[1024,1]{0,1:T(1,128)} %bitcast.38) | data formatting | bytes 8192 | tf_op jit(solution)/shard_map/reshape | solution.py:637
  7.1 119.9 %block.1 = (bf16[256,512]{1,0:T(8,128)(2,1)}, bf16[256,512]{1,0:T(8,128)(2,1)}, bf16[2,4,2,128,512]{4,3,2,1,0:T(8,128)(2,1)}, bf16[2,4,2,64,512]{4,3,2,1,0:T(8,128)(2,1)}, f32[2,8,1024]{2,1,0:T(8,128)}) custom-call(bf16[256,512]{1,0:T(8,128)(2,1)} %tok.1, bf16[256,512]{1,0:T(8,128)(2,1)} %cot.1, bf16[3,512,256]{2,1,0:T(8,128)(2,1)} %wqkv.1, ...), custom_call_target="tpu_custom_call" | custom-call | tf_op jit(solution)/shard_map/block/pallas_call | solution.py:618
  127.0 1.4 fusion.1
  128.4 0.0 copy-start.3
  128.4 0.8 fusion
  129.3 0.6 dynamic-slice_bitcast_fusion
  129.8 0.6 dynamic-slice_bitcast_fusion.1
  130.4 0.8 slice_reduce_fusion
  131.2 0.6 reshape_squeeze.3
  131.8 2.1 %convert_element_type.9 = f32[2,4,2,128,512]{4,3,2,1,0:T(8,128)S(1)} convert(bf16[2,4,2,128,512]{4,3,2,1,0:T(8,128)(2,1)} %get-tuple-element.21) | non-fusion elementwise | flops 1048576 | bytes 6291456 | tf_op jit(solution)/shard_map/convert_element_type | solution.py:640
  134.0 2.0 %slice_bitcast_fusion = (f32[2,4,128,512]{3,2,0,1:T(8,128)}, f32[512,2,4,128]{0,3,1,2:T(8,128)S(1)}) fusion(f32[2,4,2,128,512]{4,3,2,1,0:T(8,128)S(1)} %convert_element_type.9), kind=kLoop, calls=%fused_computation | loop fusion | bytes 8388608 | tf_op jit(solution)/shard_map/transpose | solution.py:641
  135.9 0.2 copy.33
  136.1 1.8 %copy.36 = f32[512,1024]{1,0:T(8,128)} copy(f32[512,1024]{0,1:T(8,128)S(1)} %bitcast.32) | data formatting | bytes 4194304
  137.9 0.0 copy-start
  137.9 3.2 %copy.34 = f32[2,4,128,512]{3,2,1,0:T(8,128)} copy(f32[2,4,128,512]{3,2,0,1:T(8,128)} %get-tuple-element.34) | data formatting | bytes 4194304 | tf_op jit(solution)/shard_map/transpose | solution.py:641
  141.1 0.0 copy-done
  141.1 0.2 slice.36
  141.3 0.1 copy.37
  141.4 1.6 %copy.35 = f32[3,512,256]{2,1,0:T(8,128)} copy(f32[3,512,256]{1,2,0:T(8,128)S(1)} %bitcast.35) | data formatting | bytes 3145728
  143.0 0.0 copy-start.2
  143.1 0.3 convert.14
  143.3 0.0 copy-start.1
  143.4 0.8 copy.32
  144.2 0.0 copy-done.3
  144.2 0.6 copy.41
  144.8 0.0 copy-done.2
  144.8 0.7 copy.42
  145.5 0.0 copy-done.1
  145.5 0.7 copy.43
  (5 shorter events, 0.1 us)
Async XLA Ops:
  128.4 15.8 %copy-start.3 = (f32[1,1,512]{2,1,0:T(1,128)}, f32[1,1,512]{2,1,0:T(1,128)S(1)}, u32[]{:S(2)}) copy-start(f32[1,1,512]{2,1,0:T(1,128)S(1)} %constant_dynamic-slice_fusion) | copy-start | bytes 6148
  137.9 3.2 %copy-start = (bf16[2,4,2,64,512]{4,3,2,1,0:T(8,128)(2,1)S(1)}, bf16[2,4,2,64,512]{4,3,2,1,0:T(8,128)(2,1)}, u32[]{:S(2)}) copy-start(bf16[2,4,2,64,512]{4,3,2,1,0:T(8,128)(2,1)} %get-tuple-element.19) | copy-start | bytes 3145732
  143.0 1.8 %copy-start.2 = (bf16[256,512]{1,0:T(8,128)(2,1)S(1)}, bf16[256,512]{1,0:T(8,128)(2,1)}, u32[]{:S(2)}) copy-start(bf16[256,512]{1,0:T(8,128)(2,1)} %get-tuple-element.80) | copy-start | bytes 786436
  143.3 2.2 %copy-start.1 = (bf16[256,512]{1,0:T(8,128)(2,1)S(1)}, bf16[256,512]{1,0:T(8,128)(2,1)}, u32[]{:S(2)}) copy-start(bf16[256,512]{1,0:T(8,128)(2,1)} %get-tuple-element.81) | copy-start | bytes 786436

commit v2 on v1

--- a/solution.py
+++ b/solution.py
@@ -20,7 +20,7 @@
 F = 512
 B = 256
 EPSILON = 1e-05
-NSEM = 96
+NSEM = 128
 
 
 def nn(a, b):
@@ -77,10 +77,12 @@
     mine, other = place(col, row), place(col, 1 - row)
     lcol, rcol = lax.rem(col + 3, 4), lax.rem(col + 1, 4)
     c0 = net.go(own, mine, peer)
+    keep = net.local(own, mine)
+    yield
     c1 = net.go(own, mine, right)
     c2 = net.go(own, mine, left)
-    keep = net.local(own, mine)
-    yield
+    yield
+    keep.wait()
     c0.wait_recv()
     c3 = net.go(other, other, right)
     c4 = net.go(other, other, left)
@@ -91,12 +93,66 @@
     c4.wait_recv()
     c6 = net.go(place(rcol, 1 - row), place(rcol, 1 - row), left)
     yield
-    keep.wait()
     c2.wait_recv()
     c3.wait_recv()
     yield
     c5.wait_recv()
     c6.wait_recv()
+
+
+def gather_weights(net, wqkv, wup, wout, wdown, s, at, core, row):
+    half, part = D // 2, D // 4
+    mine, theirs = row, 1 - row
+    drows = rows(row, half)
+
+    def cut(which, size):
+        return pl.ds(pl.multiple_of(which * size, size), size)
+
+    local = []
+    for k in range(3):
+        kcols = pl.ds(k * E, E)
+        local.append(net.local(wqkv.at[k, :, cut(mine, E)], s.wq.at[drows, kcols]))
+    local.append(net.local(wup.at[:, cut(mine, F)], s.wu.at[drows]))
+    local.append(net.local(wout.at[cut(mine, E)], s.wo.at[:, drows]))
+    local.append(net.local(wdown.at[cut(mine, F)], s.wd.at[:, drows]))
+    src = cut(core, part)
+    dst = cut(row * 2 + core, part)
+    got = cut((1 - row) * 2 + core, part)
+    ocols = rows(1 - row, half)
+    far, near = at["y3"], at["core"]
+    q = [
+        net.go(wqkv.at[k, src, cut(theirs, E)], s.wq.at[dst, pl.ds(k * E, E)], far)
+        for k in range(3)
+    ]
+    u = net.go(wup.at[src, cut(theirs, F)], s.wu.at[dst], far)
+    o = net.go(wout.at[cut(theirs * 2 + core, E // 2)], s.wo.at[cut(core, E // 2), drows], far)
+    d = net.go(wdown.at[cut(theirs * 2 + core, F // 2)], s.wd.at[cut(core, F // 2), drows], far)
+    yield
+    for copy in q:
+        copy.wait_recv()
+    q2 = net.go(s.wq.at[got], s.wq.at[got], near)
+    yield
+    u.wait_recv()
+    u2 = net.go(s.wu.at[got], s.wu.at[got], near)
+    yield
+    q2.wait_recv()
+    for copy in local[:3]:
+        copy.wait()
+    yield
+    u2.wait_recv()
+    local[3].wait()
+    yield
+    o.wait_recv()
+    ov = s.wo.at[cut(core, E // 2), ocols]
+    o2 = net.go(ov, ov, near)
+    d.wait_recv()
+    dv = s.wd.at[cut(core, F // 2), ocols]
+    d2 = net.go(dv, dv, near)
+    yield
+    local[4].wait()
+    local[5].wait()
+    o2.wait_recv()
+    d2.wait_recv()
 
 
 def ring_scatter(net, part, bufs, me, right, left, size, width):
@@ -243,6 +299,9 @@
     mean=((T, 1), F32),
     inv=((T, 1), F32),
     hid=((T, F), BF),
+    slope=((T, F), F32),
+    segc=((T, 8), F32),
+    nbs=((8, D // 2), F32),
     hpg=((T, F), BF),
     qs=((T, E), BF),
     qsm=((2, T, E), BF),
@@ -296,7 +355,7 @@
 
 
 def body(
-    tok, cot, wqkv, wout, wup, wdown, small, segc, segr, ctab, stab,
+    tok, cot, wqkv, wout, wup, wdown, bqkv, bup, bout, bdown, gain, bias, seg, ctab, stab,
     out, tgrad, fm, fa, vout, *scratch,
 ):
     s = SimpleNamespace(**dict(zip(SCRATCH, scratch)))
@@ -316,7 +375,11 @@
     at["y1"] = dev(row=1 - row)
     at["y2"] = dev(yh=1 - yh)
     at["y3"] = dev(yh=1 - yh, row=1 - row)
-
+    y1 = at["y1"]
+
+    s.nbs[...] = jnp.concatenate(
+        [gain[...].astype(F32), bias[...].astype(F32), jnp.zeros((4, half), F32)]
+    )
     barrier = pltpu.get_barrier_semaphore()
     for device in at.values():
         pl.semaphore_signal(barrier, inc=1, device_id=device, device_id_type=MESH)
@@ -324,68 +387,55 @@
 
     gx = gather_tokens(net, tok, s.xall, at, half, col, row)
     gg = gather_tokens(net, cot, s.gall, at, half, col, row)
+    gw = gather_weights(net, wqkv, wup, wout, wdown, s, at, core, row)
+    nbc = net.go(s.nbs, s.nb.at[row], y1)
     step(gx)
-
-    mine, theirs = row, 1 - row
-    drows = rows(row, half)
-    y1, y3 = at["y1"], at["y3"]
-    nbc = net.go(small.at[pl.ds(8, 8), pl.ds(0, half)], s.nb.at[row], y1)
-
-    def shares(which):
-        ecols = pl.ds(pl.multiple_of(which * E, E), E)
-        fcols = pl.ds(pl.multiple_of(which * F, F), F)
-        pairs = [(wqkv.at[k, :, ecols], s.wq.at[drows, pl.ds(k * E, E)]) for k in range(3)]
-        pairs.append((wup.at[:, fcols], s.wu.at[drows]))
-        pairs.append((wout.at[ecols], s.wo.at[:, drows]))
-        pairs.append((wdown.at[fcols], s.wd.at[:, drows]))
-        return pairs
-
-    far = [y1, y1, y1, y3, y1, y3]
-    wc = [net.go(a, b, d) for (a, b), d in zip(shares(theirs), far)]
-    wl = [net.local(a, b) for a, b in shares(mine)]
     step(gx)
-    s.nb[row] = small[pl.ds(8, 8), pl.ds(0, half)]
+    step(gw)
+    s.nb[row] = s.nbs[...]
     s.vec[...] = jnp.zeros_like(s.vec)
     s.dk[...] = jnp.zeros_like(s.dk)
     s.dv[...] = jnp.zeros_like(s.dv)
-    step(gg)
-    step(gx)
-    step(gx)
-    step(gg)
+
+    def flat(values):
+        values = values.astype(F32)
+        return jnp.concatenate([values[k : k + 1, :] for k in range(values.shape[0])], axis=1)
+
+    segr = flat(seg[...])
+    s.segc[...] = jnp.broadcast_to(segr, (8, T)).T
+    bq_all = bqkv[...].astype(F32)
+    mine = row == 0
+    bq = jnp.concatenate(
+        [jnp.where(mine, bq_all[k : k + 1, :E], bq_all[k : k + 1, E:]) for k in range(3)], axis=1
+    )
+    bu_all = flat(bup[...])
+    bu = jnp.where(mine, bu_all[:, :F], bu_all[:, F:])
+    fcols = pl.ds(pl.multiple_of(row * F, F), F)
+    gcols = pl.ds(pl.multiple_of(row * half, half), half)
+
     nbc.wait_recv()
-    finish(gx)
 
     def wide(k):
         return jnp.concatenate([s.nb[0, k : k + 1, :], s.nb[1, k : k + 1, :]], axis=1)
 
     gain0, gain1, bias0, bias1 = wide(0), wide(1), wide(2), wide(3)
 
-    @pl.loop(0, 8)
-    def _(b):
-        r = rows(b, 128)
-        xv = s.xall[r, :].astype(F32)
-        mean = jnp.sum(xv, axis=1, keepdims=True) * (1.0 / D)
-        square = jnp.sum(xv * xv, axis=1, keepdims=True) * (1.0 / D)
-        inv = lax.rsqrt(square - mean * mean + EPSILON)
-        normed = (xv - mean) * inv
-        s.mean[r, :] = mean
-        s.inv[r, :] = inv
-        s.ain[r, :] = (normed * gain0 + bias0).astype(BF)
-        s.mim[r, :] = (normed * gain1 + bias1).astype(BF)
-
-    step(gg)
-    for copy in wl:
-        copy.wait()
-    for copy in wc:
-        copy.wait_recv()
-
-    ecols = pl.ds(pl.multiple_of(row * E, E), E)
-    bq = jnp.concatenate([small[k : k + 1, ecols] for k in range(3)], axis=1)
-    bu = small[3:4, pl.ds(pl.multiple_of(row * F, F), F)]
-
-    @pl.loop(0, 4)
-    def _(b):
-        r = rows(b)
+    def norm(c):
+        @pl.loop(0, 2)
+        def _(b):
+            r = rows(c * 2 + b, 128)
+            xv = s.xall[r, :].astype(F32)
+            mean = jnp.sum(xv, axis=1, keepdims=True) * (1.0 / D)
+            square = jnp.sum(xv * xv, axis=1, keepdims=True) * (1.0 / D)
+            inv = lax.rsqrt(square - mean * mean + EPSILON)
+            normed = (xv - mean) * inv
+            s.mean[r, :] = mean
+            s.inv[r, :] = inv
+            s.ain[r, :] = (normed * gain0 + bias0).astype(BF)
+            s.mim[r, :] = (normed * gain1 + bias1).astype(BF)
+
+    def project(c):
+        r = rows(c)
         pre = nn(s.ain[r, :], s.wq[...]) + bq
         cos, sin = ctab[r, :], stab[r, :]
         query = (turn(pre[:, :E], cos, sin)).astype(BF).astype(F32) * (1.0 / math.sqrt(HD))
@@ -398,41 +448,49 @@
         s.kt[:, r] = key.T.astype(BF)
         s.vt[:, r] = value.T.astype(BF)
 
-    finish(gg)
-
-    @pl.loop(0, 4)
-    def _(b):
-        r = rows(b)
+    def expand(c):
+        r = rows(c)
         pre = nn(s.mim[r, :], s.wu[...]) + bu
         cdf = 0.5 * (1.0 + lax.erf(pre * math.sqrt(0.5)))
         s.hid[r, :] = (pre * cdf).astype(BF)
-        slope = cdf + pre * jnp.exp(-0.5 * pre * pre) * (1.0 / math.sqrt(2.0 * math.pi))
-        back = (nt(s.gall[r, :], s.wd[...]) * slope).astype(BF)
+        s.slope[r, :] = cdf + pre * jnp.exp(-0.5 * pre * pre) * (1.0 / math.sqrt(2.0 * math.pi))
+
+    def contract(c):
+        r = rows(c)
+        back = (nt(s.gall[r, :], s.wd[...]) * s.slope[r, :]).astype(BF)
         s.hpg[r, :] = back
-        fcols = pl.ds(pl.multiple_of(row * F, F), F)
         s.vec[6:7, fcols] += jnp.sum(back.astype(F32), axis=0, keepdims=True)
-        gcols = pl.ds(pl.multiple_of(row * half, half), half)
         s.vec[4:5, gcols] += jnp.sum(s.gall[r, gcols].astype(F32), axis=0, keepdims=True)
         dout = nt(s.gall[r, :], s.wo[...]).astype(BF).astype(F32)
         s.do[r, :] = dout.astype(BF)
         split_heads(s.dom, r, dout)
 
-    @pl.loop(0, 4)
-    def _(b):
-        r = rows(b, 128)
-        s.gm[r, :] = tn(s.hid[:, r], s.gall[...]).astype(BF)
-        r2 = pl.ds(pl.multiple_of(F + b * 128, 128), 128)
-        s.gm[r2, :] = tn(s.hpg[:, r], s.mim[...]).astype(BF)
-
-    sm = SimpleNamespace(
-        rc=s.mrc, ta=s.mta, tb=s.mtb, inl=s.minl, inr=s.minr, sy=s.msy, ry=s.mry, fin=fm
-    )
-    sa = SimpleNamespace(
-        rc=s.arc, ta=s.ata, tb=s.atb, inl=s.ainl, inr=s.ainr, sy=s.asy, ry=s.ary, fin=fa
-    )
-    where = dict(core=core, x=x, row=row)
-    rm = reduce_weights(net, s.gm, sm, at, where, 2 * F)
-    step(rm)
+    rb, lb, fb = lax.rem(col + 1, 4), lax.rem(col + 3, 4), lax.rem(col + 2, 4)
+    step(gx)
+    step(gg)
+    norm(col)
+    step(gx)
+    step(gw)
+    step(gx)
+    step(gx)
+    step(gg)
+    norm(lb)
+    norm(rb)
+    step(gw)
+    step(gw)
+    project(col)
+    step(gg)
+    project(lb)
+    project(rb)
+    step(gw)
+    expand(col)
+    expand(lb)
+    expand(rb)
+    step(gw)
+    finish(gx)
+    norm(fb)
+    project(fb)
+    expand(fb)
 
     first = [0, 256, 768, 1536]
     for i in range(4):
@@ -444,7 +502,7 @@
             scores = nt(s.km[h, pl.ds(0, n), :], s.qs[q, :])
             kid = lax.broadcasted_iota(jnp.int32, (n, B), 0)
             qid = lax.broadcasted_iota(jnp.int32, (n, B), 1) + i * B
-            allowed = (kid <= qid) & (segc[pl.ds(0, n), :] == segr[:, q])
+            allowed = (kid <= qid) & (s.segc[pl.ds(0, n), 0:1] == segr[:, i * B : (i + 1) * B])
             scores = jnp.where(allowed, scores, -1e30)
             top = jnp.max(scores, axis=0, keepdims=True)
             expo = jnp.exp(scores - top)
@@ -454,13 +512,21 @@
             s.mt[hrows, q] = nn(s.vt[hrows, pl.ds(0, n)], probs.astype(BF)).astype(BF)
 
         s.mixed[q, :] = s.mt[:, q].astype(F32).T.astype(BF)
-        step(rm) if i in (0, 2, 3) else None
+        step(gg) if i in (1, 3) else None
+
+    finish(gw)
 
     @pl.loop(0, 4)
     def _(b):
         r = rows(b)
         s.op[r, :] = (nn(s.mixed[r, :], s.wo[...]) + nn(s.hid[r, :], s.wd[...])).astype(BF)
 
+    contract(col)
+    step(gg)
+    contract(lb)
+    contract(rb)
+    finish(gg)
+
     def opart(block, cols):
         return s.op.at[rows(block), cols]
 
@@ -471,6 +537,25 @@
         net, opart, (s.ota, s.otb, s.oinl, s.oinr), col, at["z1"], at["z3"], B, half
     )
     step(ro)
+    contract(fb)
+
+    @pl.loop(0, 4)
+    def _(b):
+        r = rows(b, 128)
+        s.gm[r, :] = tn(s.hid[:, r], s.gall[...]).astype(BF)
+        r2 = pl.ds(pl.multiple_of(F + b * 128, 128), 128)
+        s.gm[r2, :] = tn(s.hpg[:, r], s.mim[...]).astype(BF)
+
+    sm = SimpleNamespace(
+        rc=s.mrc, ta=s.mta, tb=s.mtb, inl=s.minl, inr=s.minr, sy=s.msy, ry=s.mry, fin=fm
+    )
+    sa = SimpleNamespace(
+        rc=s.arc, ta=s.ata, tb=s.atb, inl=s.ainl, inr=s.ainr, sy=s.asy, ry=s.ary, fin=fa
+    )
+    where = dict(core=core, x=x, row=row)
+    rm = reduce_weights(net, s.gm, sm, at, where, 2 * F)
+    step(rm)
+
     s.ga[0:E, :] = nn(s.mt[...], s.gall[...]).astype(BF)
 
     for i in range(4):
@@ -488,8 +573,8 @@
             hrows = rows(h, HD)
             s.dqt[hrows, q] = nn(s.kt[hrows, pl.ds(0, n)], dscore) * (1.0 / math.sqrt(HD))
 
-        step(rm) if i in (0, 2) else None
-        step(ro) if i == 1 else None
+        step(rm) if i == 0 else None
+        step(ro) if i == 2 else None
 
     @pl.loop(0, 4)
     def _(b):
@@ -515,6 +600,7 @@
         s.vec[2:3, :] += jnp.sum(attn, axis=0, keepdims=True)
         s.vec[3:4, :] += jnp.sum(mlp, axis=0, keepdims=True)
 
+    step(rm)
     rn = ring_scatter(
         net, npart, (s.nta, s.ntb, s.ninl, s.ninr), col, at["z1"], at["z3"], B, half
     )
@@ -530,6 +616,7 @@
     step(ra)
     rv = reduce_vectors(net, s, at)
     step(rv)
+    step(rm)
     finish(ro)
 
     def summed(part, inl, inr, h):
@@ -541,22 +628,23 @@
     for h in range(2):
         s.ysend[h] = summed(opart, s.oinl, s.oinr, h).astype(BF)
     yo = net.go(s.ysend.at[1 - row], s.yrecv.at[0], y1)
+    step(ra)
     step(rv)
-    step(ra)
+    step(rn)
     step(rm)
-    step(rn)
     yo.wait_recv()
     out[...] = (
         tok[...].astype(F32)
         + s.ysend[row].astype(F32)
         + s.yrecv[0].astype(F32)
-        + small[4:5, pl.ds(0, half)]
-        + small[5:6, pl.ds(0, half)]
+        + flat(bout[...])
+        + flat(bdown[...])
     ).astype(BF)
-    step(rv)
     step(ra)
     step(rv)
+    step(rm)
     step(ra)
+    step(rv)
     finish(rn)
     r = rows(col)
     mean, inv = s.mean[r, :], s.inv[r, :]
@@ -570,7 +658,6 @@
         npart(col, pl.ds(h * half, half))[...] = total.astype(BF)
     lane = lax.broadcasted_iota(jnp.int32, (B, 128), 1)
     s.ssend[...] = jnp.where(lane < 64, first_sum, second_sum)
-    rhalf = pl.ds(pl.multiple_of(row * half, half), half)
     ohalf = pl.ds(pl.multiple_of((1 - row) * half, half), half)
     yn = net.go(npart(col, ohalf), s.yrecv.at[1], y1)
     ys = net.go(s.ssend, s.srecv, y1)
@@ -581,7 +668,7 @@
     ys.wait_recv()
     sums = (s.ssend[...] + s.srecv[...]) * (1.0 / D)
     normed = (tok[...].astype(F32) - mean) * inv
-    total = npart(col, rhalf)[...].astype(F32) + s.yrecv[1].astype(F32)
+    total = npart(col, gcols)[...].astype(F32) + s.yrecv[1].astype(F32)
     tgrad[...] = (
         cot[...].astype(F32) + inv * (total - sums[:, 0:1] - normed * sums[:, 64:65])
     ).astype(BF)
@@ -600,17 +687,62 @@
     return ctab.astype(np.float32), stab.astype(np.float32)
 
 
+def last(
+    fm, fa, vec, out, tgrad,
+    out_o, tgrad_o, wq_o, bq_o, wo_o, bo_o, wu_o, bu_o, wd_o, bd_o, gain_o, bias_o,
+    wq, wo, wu, wd, sems,
+):
+    row = lax.axis_index("row")
+    copies = []
+
+    def write(src, dst):
+        copy = pltpu.make_async_copy(src, dst, sems.at[len(copies)])
+        copy.start()
+        copies.append(copy)
+
+    write(out, out_o)
+    write(tgrad, tgrad_o)
+    for r in range(2):
+        for x in range(4):
+            at = r * F + x * (F // 4)
+            wd[pl.ds(at, F // 4), :] = fm[0, x, r].astype(F32)
+        write(wd.at[pl.ds(r * F, F)], wd_o.at[pl.ds(r * F, F)])
+    for r in range(2):
+        for x in range(4):
+            at = r * F + x * (F // 4)
+            wu[:, pl.ds(at, F // 4)] = fm[1, x, r].astype(F32).T
+        write(wu.at[:, pl.ds(r * F, F)], wu_o.at[:, pl.ds(r * F, F)])
+    for r in range(2):
+        for p in range(2):
+            wo[pl.ds(r * E + p * (E // 2), E // 2), :] = fa[0, p, r].astype(F32)
+    write(wo, wo_o)
+    for k in range(3):
+        for r in range(2):
+            a = fa[(k + 1) // 2, 2 * ((k + 1) % 2), r].astype(F32)
+            b = fa[(k + 1) // 2, 2 * ((k + 1) % 2) + 1, r].astype(F32)
+            wq[k, :, pl.ds(r * E, E)] = jnp.concatenate([a, b], axis=0).T
+        write(wq.at[k], wq_o.at[k])
+    half = D // 2
+    left = row == 0
+
+    def cut(values):
+        return jnp.where(left, values[:, :half], values[:, half:])
+
+    bo_o[...] = cut(vec[0, 4:5, :])
+    bd_o[...] = cut(vec[0, 4:5, :])
+    for k in range(3):
+        bq_o[k : k + 1, :E] = vec[0, 5:6, k * E : (k + 1) * E]
+        bq_o[k : k + 1, E:] = vec[0, 5:6, (k + 3) * E : (k + 4) * E]
+    bu_o[...] = vec[0, 6:7, :]
+    gain_o[...] = cut(vec[1, 0:2, :])
+    bias_o[...] = cut(vec[1, 2:4, :])
+    for copy in copies:
+        copy.wait()
+
+
 def on_device(
     tokens, segment_ids, w_qkv, b_qkv, w_out, b_out, w_up, b_up, w_down, b_down, norm_gain, norm_bias, cotangent
 ):
-    def line(values):
-        values = values.astype(F32).reshape(-1, values.shape[-1])
-        return jnp.pad(values, ((0, 0), (0, D - values.shape[1])))
-
-    small = jnp.concatenate(
-        [line(v) for v in (b_qkv, b_up, b_out, b_down)]
-        + [jnp.zeros((2, D), F32), line(norm_gain), line(norm_bias), jnp.zeros((4, D), F32)]
-    )
     ctab, stab = tables()
     vmem = pl.BlockSpec(memory_space=pltpu.VMEM)
     hbm = pl.BlockSpec(memory_space=pl.ANY)
@@ -624,7 +756,7 @@
             shape((2, 4, 2, E // 2, D // 2), BF),
             shape((2, 8, D), F32),
         ],
-        in_specs=[vmem, vmem, hbm, hbm, hbm, hbm, vmem, vmem, vmem, vmem, vmem],
+        in_specs=[vmem, vmem, hbm, hbm, hbm, hbm] + [vmem] * 9,
         out_specs=[vmem] * 5,
         scratch_shapes=[pltpu.VMEM(*spec) for spec in SCRATCH.values()]
         + [pltpu.SemaphoreType.DMA((NSEM,)), pltpu.SemaphoreType.DMA((NSEM,))],
@@ -633,26 +765,41 @@
         ),
         name="block",
     )(
-        tokens, cotangent, w_qkv, w_out, w_up, w_down, small,
-        segment_ids.reshape(T, 1), segment_ids.reshape(1, T), jnp.asarray(ctab), jnp.asarray(stab),
-    )
-    row = lax.axis_index("row")
-    fm = fm.astype(F32)
-    w_down_grad = fm[0].transpose(1, 0, 2, 3).reshape(2 * F, D // 2)
-    w_up_grad = fm[1].transpose(3, 1, 0, 2).reshape(D // 2, 2 * F)
-    fa = fa.astype(F32).reshape(4, 2, 2, E // 2, D // 2)
-    w_out_grad = fa[0].transpose(1, 0, 2, 3).reshape(2 * E, D // 2)
-    w_qkv_grad = fa[1:].transpose(0, 4, 2, 1, 3).reshape(3, D // 2, 2 * E)
-    rhalf = lambda v: lax.dynamic_slice_in_dim(v, row * (D // 2), D // 2, axis=-1)
-    b_out_grad = rhalf(vec[0, 4])
-    b_qkv_grad = vec[0, 5, : 6 * E].reshape(2, 3, E).transpose(1, 0, 2).reshape(3, 2 * E)
-    b_up_grad = vec[0, 6]
-    gain_grad = rhalf(vec[1, 0:2])
-    bias_grad = rhalf(vec[1, 2:4])
-    return (
-        out, tgrad, w_qkv_grad, b_qkv_grad, w_out_grad, b_out_grad,
-        w_up_grad, b_up_grad, w_down_grad, b_out_grad, gain_grad, bias_grad,
-    )
+        tokens, cotangent, w_qkv, w_out, w_up, w_down, b_qkv, b_up.reshape(8, 128),
+        b_out.reshape(4, 128), b_down.reshape(4, 128), norm_gain, norm_bias,
+        segment_ids.reshape(8, 128), jnp.asarray(ctab), jnp.asarray(stab),
+    )
+    big = [
+        ((3, D // 2, 2 * E), F32),
+        ((2 * E, D // 2), F32),
+        ((D // 2, 2 * F), F32),
+        ((2 * F, D // 2), F32),
+    ]
+    results = pl.pallas_call(
+        last,
+        out_shape=[
+            shape((B, D // 2), BF),
+            shape((B, D // 2), BF),
+            shape(*big[0]),
+            shape((3, 2 * E), F32),
+            shape(*big[1]),
+            shape((1, D // 2), F32),
+            shape(*big[2]),
+            shape((1, 2 * F), F32),
+            shape(*big[3]),
+            shape((1, D // 2), F32),
+            shape((2, D // 2), F32),
+            shape((2, D // 2), F32),
+        ],
+        in_specs=[vmem] * 5,
+        out_specs=[hbm, hbm, hbm, vmem, hbm, vmem, hbm, vmem, hbm, vmem, vmem, vmem],
+        scratch_shapes=[pltpu.VMEM(*spec) for spec in big] + [pltpu.SemaphoreType.DMA((12,))],
+        compiler_params=pltpu.CompilerParams(vmem_limit_bytes=40 * 1024 * 1024),
+        name="last",
+    )(fm, fa, vec, out, tgrad)
+    out, tgrad, wq, bq, wo, bo, wu, bu, wd, bd, gain, bias = results
+    bo, bu, bd = bo.reshape(-1), bu.reshape(-1), bd.reshape(-1)
+    return (out, tgrad, wq, bq, wo, bo, wu, bu, wd, bd, gain, bias)
 
 
 def solution(mesh):

time: 147 us -> 114 us (0.78)
  local copies, waits for them, and re-layouts: 21.1 us -> 5.55 us
  Pallas kernels: 120 us -> 108 us
  other arithmetic: 4.51 us -> 0 us
    pallas_call x1, Pallas kernels: 120 us -> 104 us  [on_device(): pl.pallas_call(body, out_shape=[shape((B, D // 2), BF), shape((B, D // 2)...]
    transpose x5 -> x0, local copies, waits for them, and re-layouts: 6.19 us -> none  [the longest x2 5.15 us: on_device(): w_down_grad = fm[0].transpose(1, 0, 2, 3).reshape(2 * F, D // 2)]
    pallas_call x0 -> x1, Pallas kernels: none -> 3.64 us  [on_device(): pl.pallas_call(last, out_shape=[shape((B, D // 2), BF), shape((B, D // 2)...]
    slice x4 -> x0, local copies, waits for them, and re-layouts: 3.22 us -> none  [the longest x1 1.43 us: on_device(): b_up_grad = vec[0, 6]]
    reshape x3 -> x0, local copies, waits for them, and re-layouts: 3.07 us -> none  [the longest x1 1.71 us: on_device(): segment_ids.reshape(T, 1)]
    convert_element_type x1 -> x0, other arithmetic: 2.15 us -> none  [on_device(): fm = fm.astype(F32)]
    unnamed x14 -> x10, local copies, waits for them, and re-layouts: 5.55 us -> 5.55 us
where the time goes in v2:
time: 114 us
  Pallas kernels  108 us (95%)
  local copies, waits for them, and re-layouts  5.55 us (5%)
    pallas_call x1, Pallas kernels, on_device(): pl.pallas_call(body, out_shape=[shape((B, D // 2), BF), shape((B, D // 2)...  104 us
    unnamed x10, local copies, waits for them, and re-layouts  5.55 us
    pallas_call x1, Pallas kernels, on_device(): pl.pallas_call(last, out_shape=[shape((B, D // 2), BF), shape((B, D // 2)...  3.64 us

profile of v2, /device:TPU:1, one launch (start us, length us, event | category | flops | bytes accessed | tf_op | source)
XLA Modules:
  0.0 113.9 jit_solution(17455668959598764800)
XLA Ops:
  0.6 103.9 %block.1 = (bf16[256,512]{1,0:T(8,128)(2,1)}, bf16[256,512]{1,0:T(8,128)(2,1)}, bf16[2,4,2,128,512]{4,3,2,1,0:T(8,128)(2,1)}, bf16[2,4,2,64,512]{4,3,2,1,0:T(8,128)(2,1)}, f32[2,8,1024]{2,1,0:T(8,128)}) custom-call(bf16[256,512]{1,0:T(8,128)(2,1)} %tok.1, bf16[256,512]{1,0:T(8,128)(2,1)} %cot.1, bf16[3,512,256]{2,1,0:T(8,128)(2,1)} %wqkv.1, ...), custom_call_target="tpu_custom_call" | custom-call | tf_op jit(solution)/shard_map/block/pallas_call | solution.py:750
  104.5 0.0 copy-start
  104.5 1.6 %copy-done = bf16[2,4,2,128,512]{4,3,2,1,0:T(8,128)(2,1)S(1)} copy-done((bf16[2,4,2,128,512]{4,3,2,1,0:T(8,128)(2,1)S(1)}, bf16[2,4,2,128,512]{4,3,2,1,0:T(8,128)(2,1)}, u32[]{:S(2)}) %copy-start) | copy-done | bytes 2097176
  106.1 0.0 copy-start.1
  106.1 1.2 %copy-done.1 = bf16[2,4,2,64,512]{4,3,2,1,0:T(8,128)(2,1)S(1)} copy-done((bf16[2,4,2,64,512]{4,3,2,1,0:T(8,128)(2,1)S(1)}, bf16[2,4,2,64,512]{4,3,2,1,0:T(8,128)(2,1)}, u32[]{:S(2)}) %copy-start.1) | copy-done | bytes 1048600
  107.3 0.0 copy-start.2
  107.3 0.9 copy-done.2
  108.3 0.0 copy-start.3
  108.3 0.9 copy-done.3
  109.2 0.0 copy-start.4
  109.2 0.8 copy-done.4
  110.1 3.6 %last.1 = (bf16[256,512]{1,0:T(8,128)(2,1)}, bf16[256,512]{1,0:T(8,128)(2,1)}, f32[3,512,256]{2,1,0:T(8,128)}, f32[3,256]{1,0:T(4,128)}, f32[256,512]{1,0:T(8,12...) custom-call(bf16[2,4,2,128,512]{4,3,2,1,0:T(8,128)(2,1)S(1)} %copy-d, ...), custom_call_target="tpu_custom_call" | custom-call | tf_op jit(solution)/shard_map/last/pallas_call | solution.py:778
Async XLA Ops:
  104.5 1.6 %copy-start = (bf16[2,4,2,128,512]{4,3,2,1,0:T(8,128)(2,1)S(1)}, bf16[2,4,2,128,512]{4,3,2,1,0:T(8,128)(2,1)}, u32[]{:S(2)}) copy-start(bf16[2,4,2,128,512]{4,3,2,1,0:T(8,128)(2,1)} %get-tuple-element.29.fm) | copy-start | bytes 6291460
  106.1 1.2 %copy-start.1 = (bf16[2,4,2,64,512]{4,3,2,1,0:T(8,128)(2,1)S(1)}, bf16[2,4,2,64,512]{4,3,2,1,0:T(8,128)(2,1)}, u32[]{:S(2)}) copy-start(bf16[2,4,2,64,512]{4,3,2,1,0:T(8,128)(2,1)} %get-tuple-element.30.fa) | copy-start | bytes 3145732
  107.3 0.9 copy-start.2
  108.3 0.9 copy-start.3
  109.2 0.8 copy-start.4

commit v3 on v2

--- a/solution.py
+++ b/solution.py
@@ -20,7 +20,9 @@
 F = 512
 B = 256
 EPSILON = 1e-05
-NSEM = 128
+NSEM = 200
+YR = 144
+ZR = B - YR
 
 
 def nn(a, b):
@@ -70,34 +72,47 @@
 
 def gather_tokens(net, own, full, at, half, col, row):
     right, left, peer = at["z1"], at["z3"], at["y1"]
-
-    def place(c, h):
-        return full.at[rows(c), pl.ds(pl.multiple_of(h * half, half), half)]
-
-    mine, other = place(col, row), place(col, 1 - row)
-    lcol, rcol = lax.rem(col + 3, 4), lax.rem(col + 1, 4)
+    cut = YR + 48
+
+    def place(c, h, start=0, size=B):
+        r = pl.ds(pl.multiple_of(c * B + start, 16), size)
+        return full.at[r, pl.ds(pl.multiple_of(h * half, half), half)]
+
+    def move(device, *where):
+        return net.go(place(*where), place(*where), device)
+
+    mine = place(col, row)
+    lcol, rcol, fcol = lax.rem(col + 3, 4), lax.rem(col + 1, 4), lax.rem(col + 2, 4)
     c0 = net.go(own, mine, peer)
-    keep = net.local(own, mine)
-    yield
     c1 = net.go(own, mine, right)
     c2 = net.go(own, mine, left)
+    keep = net.local(own, mine)
     yield
     keep.wait()
     c0.wait_recv()
-    c3 = net.go(other, other, right)
-    c4 = net.go(other, other, left)
+    c3 = move(right, col, 1 - row, 0, YR)
+    c4 = move(left, col, 1 - row, 0, YR)
     yield
     c1.wait_recv()
-    c5 = net.go(place(lcol, row), place(lcol, row), right)
+    c5 = move(right, lcol, row, 0, cut)
+    e5 = move(peer, lcol, row, YR, ZR)
+    c2.wait_recv()
+    d4 = move(left, rcol, row, cut, B - cut)
+    e6 = move(peer, rcol, row, YR, ZR)
     yield
     c4.wait_recv()
-    c6 = net.go(place(rcol, 1 - row), place(rcol, 1 - row), left)
-    yield
-    c2.wait_recv()
+    c6 = move(left, rcol, 1 - row, 0, YR)
     c3.wait_recv()
     yield
+    e5.wait_recv()
+    e6.wait_recv()
+    yield
     c5.wait_recv()
+    d4.wait_recv()
+    e7 = move(peer, fcol, row, YR, ZR)
+    yield
     c6.wait_recv()
+    e7.wait_recv()
 
 
 def gather_weights(net, wqkv, wup, wout, wdown, s, at, core, row):
@@ -175,6 +190,70 @@
     yield
     for copy in (c, d, e, f):
         copy.wait_recv()
+
+
+def scatter(net, p, s, at, col, row, look=None):
+    half = D // 2
+    far, rb, lb = lax.rem(col + 2, 4), lax.rem(col + 1, 4), lax.rem(col + 3, 4)
+    mcols, ocols = rows(row, half), rows(1 - row, half)
+
+    def yrows(b):
+        return pl.ds(pl.multiple_of(b * B, B), YR)
+
+    def zrows(b):
+        return pl.ds(pl.multiple_of(b * B + YR, 16), ZR)
+
+    def zpart(b, cols):
+        return p.at[zrows(b), pl.ds(pl.multiple_of(row * half + cols.start, 256), cols.size)]
+
+    order = (far, rb, lb, col)
+    first = [net.go(p.at[zrows(b), ocols], s.ry.at[k], at["y1"]) for k, b in enumerate(order)]
+    right, left = at["z1"], at["z3"]
+    ring = ring_scatter(
+        net, lambda b, cols: p.at[yrows(b), cols], (s.ta, s.tb, s.inl, s.inr), col, right, left, YR, half
+    )
+    step(ring)
+    yield
+
+    def add(k):
+        first[k].wait_recv()
+        view = p.at[zrows(order[k]), mcols]
+        view[...] = (view[...].astype(F32) + s.ry[k].astype(F32)).astype(BF)
+
+    step(ring)
+    yield
+    for k in range(3):
+        add(k)
+    ring2 = ring_scatter(
+        net, zpart, (s.ta2, s.tb2, s.inl2, s.inr2), col, right, left, ZR, half // 2
+    )
+    step(ring2)
+    yield
+    add(3)
+    finish(ring)
+    for h in range(2):
+        cols = pl.ds(h * half, half)
+        total = (
+            p[yrows(col), cols].astype(F32) + s.inl[:, cols].astype(F32) + s.inr[:, cols].astype(F32)
+        )
+        s.ysend[h] = total.astype(BF)
+        if look is not None:
+            look(h, total)
+    last = net.go(s.ysend.at[1 - row], s.yrecv, at["y1"])
+    yield
+    step(ring2)
+    yield
+    finish(ring2)
+    last.wait_recv()
+
+
+def total_y(s, row):
+    return s.ysend[row].astype(F32) + s.yrecv[...].astype(F32)
+
+
+def total_z(p, s, col, row):
+    own = p[pl.ds(pl.multiple_of(col * B + YR, 16), ZR), rows(row, D // 2)]
+    return own.astype(F32) + s.inl2[...].astype(F32) + s.inr2[...].astype(F32)
 
 
 def reduce_weights(net, grad, s, at, me, n):
@@ -320,43 +399,59 @@
     qkvg=((T, 3 * E), BF),
     op=((T, D), BF),
     ng=((T, D), BF),
-    ota=((B, D // 2), BF),
-    otb=((B, D // 2), BF),
-    oinl=((B, D), BF),
-    oinr=((B, D), BF),
-    nta=((B, D // 2), BF),
-    ntb=((B, D // 2), BF),
-    ninl=((B, D), BF),
-    ninr=((B, D), BF),
-    ysend=((2, B, D // 2), BF),
-    yrecv=((2, B, D // 2), BF),
-    ssend=((B, 128), F32),
-    srecv=((B, 128), F32),
-    gm=((2 * F, D), BF),
-    ga=((4 * E, D), BF),
-    mrc=((F, D), BF),
-    mta=((F // 4, D // 2), BF),
-    mtb=((F // 4, D // 2), BF),
-    minl=((F // 4, D), BF),
-    minr=((F // 4, D), BF),
-    msy=((2, F // 4, D // 2), BF),
-    mry=((3, F // 4, D // 2), BF),
-    arc=((2 * E, D), BF),
-    ata=((E // 2, D // 2), BF),
-    atb=((E // 2, D // 2), BF),
-    ainl=((E // 2, D), BF),
-    ainr=((E // 2, D), BF),
-    asy=((2, E // 2, D // 2), BF),
-    ary=((3, E // 2, D // 2), BF),
+    ctab=((T, E), F32),
+    stab=((T, E), F32),
+    ssend=((8, B), F32),
+    srecv=((8, B), F32),
+    g1=((F + E, D), BF),
+    g2=((F, D), BF),
+    g3=((3 * E, D), BF),
     vec=((8, D), F32),
     vr=((10, 8, D), F32),
     vs=((4, 8, D), F32),
 )
+SCATTER = dict(
+    ta=((YR, D // 2), BF),
+    tb=((YR, D // 2), BF),
+    inl=((YR, D), BF),
+    inr=((YR, D), BF),
+    ry=((4, ZR, D // 2), BF),
+    ta2=((ZR, D // 4), BF),
+    tb2=((ZR, D // 4), BF),
+    inl2=((ZR, D // 2), BF),
+    inr2=((ZR, D // 2), BF),
+    ysend=((2, YR, D // 2), BF),
+    yrecv=((YR, D // 2), BF),
+)
+
+
+def reduce_scratch(n):
+    return dict(
+        rc=((n // 2, D), BF),
+        ta=((n // 8, D // 2), BF),
+        tb=((n // 8, D // 2), BF),
+        inl=((n // 8, D), BF),
+        inr=((n // 8, D), BF),
+        sy=((2, n // 8, D // 2), BF),
+        ry=((3, n // 8, D // 2), BF),
+    )
+
+
+ROWS = (F + E, F, 3 * E)
+for name in "on":
+    SCRATCH.update({name + "_" + key: spec for key, spec in SCATTER.items()})
+for k, n in enumerate(ROWS):
+    SCRATCH.update({f"r{k}_{key}": spec for key, spec in reduce_scratch(n).items()})
+
+
+def under(s, prefix, **more):
+    picked = {k[len(prefix) :]: v for k, v in vars(s).items() if k.startswith(prefix)}
+    return SimpleNamespace(**picked, **more)
 
 
 def body(
-    tok, cot, wqkv, wout, wup, wdown, bqkv, bup, bout, bdown, gain, bias, seg, ctab, stab,
-    out, tgrad, fm, fa, vout, *scratch,
+    tok, cot, wqkv, wout, wup, wdown, bqkv, bup, bout, bdown, gain, bias, seg, ctab_h, stab_h,
+    out, tgrad, f0, f1, f2, vout, *scratch,
 ):
     s = SimpleNamespace(**dict(zip(SCRATCH, scratch)))
     send, recv = scratch[len(SCRATCH) :]
@@ -390,8 +485,8 @@
     gw = gather_weights(net, wqkv, wup, wout, wdown, s, at, core, row)
     nbc = net.go(s.nbs, s.nb.at[row], y1)
     step(gx)
-    step(gx)
     step(gw)
+    tabs = [net.local(ctab_h, s.ctab), net.local(stab_h, s.stab)]
     s.nb[row] = s.nbs[...]
     s.vec[...] = jnp.zeros_like(s.vec)
     s.dk[...] = jnp.zeros_like(s.dk)
@@ -437,7 +532,7 @@
     def project(c):
         r = rows(c)
         pre = nn(s.ain[r, :], s.wq[...]) + bq
-        cos, sin = ctab[r, :], stab[r, :]
+        cos, sin = s.ctab[r, :], s.stab[r, :]
         query = (turn(pre[:, :E], cos, sin)).astype(BF).astype(F32) * (1.0 / math.sqrt(HD))
         key = turn(pre[:, E : 2 * E], cos, sin).astype(BF).astype(F32)
         value = pre[:, 2 * E :].astype(BF).astype(F32)
@@ -467,7 +562,6 @@
 
     rb, lb, fb = lax.rem(col + 1, 4), lax.rem(col + 3, 4), lax.rem(col + 2, 4)
     step(gx)
-    step(gg)
     norm(col)
     step(gx)
     step(gw)
@@ -476,14 +570,17 @@
     step(gg)
     norm(lb)
     norm(rb)
+    for copy in tabs:
+        copy.wait()
     step(gw)
     step(gw)
     project(col)
-    step(gg)
     project(lb)
+    step(gx)
     project(rb)
     step(gw)
     expand(col)
+    step(gg)
     expand(lb)
     expand(rb)
     step(gw)
@@ -515,48 +612,43 @@
         step(gg) if i in (1, 3) else None
 
     finish(gw)
+    step(gg)
 
     @pl.loop(0, 4)
     def _(b):
         r = rows(b)
         s.op[r, :] = (nn(s.mixed[r, :], s.wo[...]) + nn(s.hid[r, :], s.wd[...])).astype(BF)
 
+    step(gg)
     contract(col)
-    step(gg)
     contract(lb)
     contract(rb)
     finish(gg)
-
-    def opart(block, cols):
-        return s.op.at[rows(block), cols]
-
-    def npart(block, cols):
-        return s.ng.at[rows(block), cols]
-
-    ro = ring_scatter(
-        net, opart, (s.ota, s.otb, s.oinl, s.oinr), col, at["z1"], at["z3"], B, half
-    )
+    contract(fb)
+    so, sn = under(s, "o_"), under(s, "n_")
+    ro = scatter(net, s.op, so, at, col, row)
     step(ro)
-    contract(fb)
+
+    where = dict(core=core, x=x, row=row)
+    r0 = reduce_weights(net, s.g1, under(s, "r0_", fin=f0), at, where, ROWS[0])
+    r1 = reduce_weights(net, s.g2, under(s, "r1_", fin=f1), at, where, ROWS[1])
+    r2 = reduce_weights(net, s.g3, under(s, "r2_", fin=f2), at, where, ROWS[2])
 
     @pl.loop(0, 4)
     def _(b):
         r = rows(b, 128)
-        s.gm[r, :] = tn(s.hid[:, r], s.gall[...]).astype(BF)
-        r2 = pl.ds(pl.multiple_of(F + b * 128, 128), 128)
-        s.gm[r2, :] = tn(s.hpg[:, r], s.mim[...]).astype(BF)
-
-    sm = SimpleNamespace(
-        rc=s.mrc, ta=s.mta, tb=s.mtb, inl=s.minl, inr=s.minr, sy=s.msy, ry=s.mry, fin=fm
-    )
-    sa = SimpleNamespace(
-        rc=s.arc, ta=s.ata, tb=s.atb, inl=s.ainl, inr=s.ainr, sy=s.asy, ry=s.ary, fin=fa
-    )
-    where = dict(core=core, x=x, row=row)
-    rm = reduce_weights(net, s.gm, sm, at, where, 2 * F)
-    step(rm)
-
-    s.ga[0:E, :] = nn(s.mt[...], s.gall[...]).astype(BF)
+        s.g1[r, :] = tn(s.hid[:, r], s.gall[...]).astype(BF)
+
+    s.g1[F:, :] = nn(s.mt[...], s.gall[...]).astype(BF)
+    step(r0)
+
+    @pl.loop(0, 4)
+    def _(b):
+        r = rows(b, 128)
+        s.g2[r, :] = tn(s.hpg[:, r], s.mim[...]).astype(BF)
+
+    step(r1)
+    step(r0)
 
     for i in range(4):
         n = (i + 1) * B
@@ -573,13 +665,18 @@
             hrows = rows(h, HD)
             s.dqt[hrows, q] = nn(s.kt[hrows, pl.ds(0, n)], dscore) * (1.0 / math.sqrt(HD))
 
-        step(rm) if i == 0 else None
-        step(ro) if i == 2 else None
+        if i == 0:
+            step(r1)
+        if i == 2:
+            step(ro)
+        if i == 3:
+            step(r0)
+            step(ro)
 
     @pl.loop(0, 4)
     def _(b):
         r = rows(b)
-        cos, sin = ctab[r, :], -stab[r, :]
+        cos, sin = s.ctab[r, :], -s.stab[r, :]
         dq = turn(s.dqt[:, r].T, cos, sin).astype(BF)
         dk = turn(s.dk[r, :], cos, sin).astype(BF)
         dv = s.dv[r, :].astype(BF)
@@ -587,6 +684,16 @@
         s.qkvg[r, :] = both
         ecols3 = pl.ds(pl.multiple_of(row * 3 * E, 3 * E), 3 * E)
         s.vec[5:6, ecols3] += jnp.sum(both.astype(F32), axis=0, keepdims=True)
+
+    step(r1)
+    step(ro)
+
+    @pl.loop(0, 3)
+    def _(b):
+        r = rows(b, E)
+        s.g3[r, :] = tn(s.qkvg[:, r], s.ain[...]).astype(BF)
+
+    step(r2)
 
     @pl.loop(0, 4)
     def _(b):
@@ -600,77 +707,62 @@
         s.vec[2:3, :] += jnp.sum(attn, axis=0, keepdims=True)
         s.vec[3:4, :] += jnp.sum(mlp, axis=0, keepdims=True)
 
-    step(rm)
-    rn = ring_scatter(
-        net, npart, (s.nta, s.ntb, s.ninl, s.ninr), col, at["z1"], at["z3"], B, half
-    )
+    r = rows(col)
+    mean, inv = s.mean[r, :], s.inv[r, :]
+    sums = []
+
+    def look(h, total):
+        xv = s.xall[pl.ds(pl.multiple_of(col * B, B), YR), pl.ds(h * half, half)].astype(F32)
+        normed = (xv - mean[:YR]) * inv[:YR]
+        sums.append(jnp.sum(total, axis=1, keepdims=True))
+        sums.append(jnp.sum(total * normed, axis=1, keepdims=True))
+
+    rn = scatter(net, s.ng, sn, at, col, row, look)
     step(rn)
-
-    @pl.loop(0, 3)
-    def _(b):
-        r = rows(b, E)
-        r2 = pl.ds(pl.multiple_of(E + b * E, E), E)
-        s.ga[r2, :] = tn(s.qkvg[:, r], s.ain[...]).astype(BF)
-
-    ra = reduce_weights(net, s.ga, sa, at, where, 4 * E)
-    step(ra)
     rv = reduce_vectors(net, s, at)
     step(rv)
-    step(rm)
+    step(r2)
+    step(r0)
+    step(ro)
+    step(r1)
     finish(ro)
-
-    def summed(part, inl, inr, h):
-        cols = pl.ds(h * half, half)
-        return (
-            part(col, cols)[...].astype(F32) + inl[:, cols].astype(F32) + inr[:, cols].astype(F32)
-        )
-
-    for h in range(2):
-        s.ysend[h] = summed(opart, s.oinl, s.oinr, h).astype(BF)
-    yo = net.go(s.ysend.at[1 - row], s.yrecv.at[0], y1)
-    step(ra)
+    bias_out = flat(bout[...]) + flat(bdown[...])
+    xv = s.xall[r, gcols].astype(F32) + bias_out
+    out[...] = (xv + jnp.concatenate([total_y(so, row), total_z(s.op, so, col, row)])).astype(BF)
+    step(rv)
+    step(r0)
+    step(rn)
+    step(r2)
+    step(r1)
     step(rv)
     step(rn)
-    step(rm)
-    yo.wait_recv()
-    out[...] = (
-        tok[...].astype(F32)
-        + s.ysend[row].astype(F32)
-        + s.yrecv[0].astype(F32)
-        + flat(bout[...])
-        + flat(bdown[...])
-    ).astype(BF)
-    step(ra)
+    step(r0)
+    step(r2)
+    step(r1)
     step(rv)
-    step(rm)
-    step(ra)
-    step(rv)
+    step(rn)
+    step(r2)
+    step(r0)
+    step(rn)
+    step(r1)
     finish(rn)
-    r = rows(col)
-    mean, inv = s.mean[r, :], s.inv[r, :]
-    first_sum = jnp.zeros((B, 1), F32)
-    second_sum = jnp.zeros((B, 1), F32)
-    for h in range(2):
-        total = summed(npart, s.ninl, s.ninr, h)
-        normed = (s.xall[r, pl.ds(h * half, half)].astype(F32) - mean) * inv
-        first_sum += jnp.sum(total, axis=1, keepdims=True)
-        second_sum += jnp.sum(total * normed, axis=1, keepdims=True)
-        npart(col, pl.ds(h * half, half))[...] = total.astype(BF)
+    normed = (s.xall[r, gcols].astype(F32) - mean) * inv
+    zsum = total_z(s.ng, sn, col, row)
+    first_sum = jnp.concatenate([sums[0] + sums[2], jnp.sum(zsum, axis=1, keepdims=True)])
+    second = jnp.sum(zsum * normed[YR:], axis=1, keepdims=True)
+    second_sum = jnp.concatenate([sums[1] + sums[3], second])
     lane = lax.broadcasted_iota(jnp.int32, (B, 128), 1)
-    s.ssend[...] = jnp.where(lane < 64, first_sum, second_sum)
-    ohalf = pl.ds(pl.multiple_of((1 - row) * half, half), half)
-    yn = net.go(npart(col, ohalf), s.yrecv.at[1], y1)
+    s.ssend[...] = jnp.where(lane < 4, first_sum, second_sum).T[:8, :]
     ys = net.go(s.ssend, s.srecv, y1)
-    interleave(rv, ra, rm)
+    interleave(r0, r2, r1, rv)
     vout[0] = s.vs[2]
     vout[1] = s.vs[3]
-    yn.wait_recv()
     ys.wait_recv()
-    sums = (s.ssend[...] + s.srecv[...]) * (1.0 / D)
-    normed = (tok[...].astype(F32) - mean) * inv
-    total = npart(col, gcols)[...].astype(F32) + s.yrecv[1].astype(F32)
+    both = (s.ssend[...] + s.srecv[...]) * (1.0 / D)
+    both = jnp.concatenate([both] * 16).T
+    total = jnp.concatenate([total_y(sn, row), zsum])
     tgrad[...] = (
-        cot[...].astype(F32) + inv * (total - sums[:, 0:1] - normed * sums[:, 64:65])
+        s.gall[r, gcols].astype(F32) + inv * (total - both[:, 0:1] - normed * both[:, 4:5])
     ).astype(BF)
     for copy in net.sent:
         copy.wait_send()
@@ -688,9 +780,9 @@
 
 
 def last(
-    fm, fa, vec, out, tgrad,
+    f0_h, f1_h, f2_h, vec_h, out_h, tgrad_h,
     out_o, tgrad_o, wq_o, bq_o, wo_o, bo_o, wu_o, bu_o, wd_o, bd_o, gain_o, bias_o,
-    wq, wo, wu, wd, sems,
+    f0, f1, f2, vec, out, tgrad, wq, wo, wu, wd, sems,
 ):
     row = lax.axis_index("row")
     copies = []
@@ -699,29 +791,38 @@
         copy = pltpu.make_async_copy(src, dst, sems.at[len(copies)])
         copy.start()
         copies.append(copy)
-
+        return copy
+
+    pairs = ((f0_h, f0), (f1_h, f1), (f2_h, f2), (vec_h, vec), (out_h, out), (tgrad_h, tgrad))
+    reads = [write(a, b) for a, b in pairs]
+    reads[0].wait()
+    for r in range(2):
+        for k in range(8):
+            piece = f0[k // 4, k % 4, r].astype(F32)
+            n = piece.shape[0]
+            inside = max(0, min(n, F - k * n))
+            if inside:
+                wd[pl.ds(r * F + k * n, inside), :] = piece[:inside]
+            if inside < n:
+                wo[pl.ds(r * E + k * n + inside - F, n - inside), :] = piece[inside:]
+        write(wd.at[pl.ds(r * F, F)], wd_o.at[pl.ds(r * F, F)])
+    write(wo, wo_o)
+    reads[1].wait()
+    for r in range(2):
+        for k in range(4):
+            pair = [f1[(2 * k + h) // 4, (2 * k + h) % 4, r].astype(F32) for h in range(2)]
+            wu[:, pl.ds(r * F + k * E, E)] = jnp.concatenate(pair).T
+        write(wu.at[:, pl.ds(r * F, F)], wu_o.at[:, pl.ds(r * F, F)])
+    reads[2].wait()
+    for r in range(2):
+        whole = jnp.concatenate([f2[k // 4, k % 4, r].astype(F32) for k in range(8)])
+        for k in range(3):
+            wq[k, :, pl.ds(r * E, E)] = whole[k * E : (k + 1) * E].T
+    write(wq, wq_o)
+    for copy in reads[3:]:
+        copy.wait()
     write(out, out_o)
     write(tgrad, tgrad_o)
-    for r in range(2):
-        for x in range(4):
-            at = r * F + x * (F // 4)
-            wd[pl.ds(at, F // 4), :] = fm[0, x, r].astype(F32)
-        write(wd.at[pl.ds(r * F, F)], wd_o.at[pl.ds(r * F, F)])
-    for r in range(2):
-        for x in range(4):
-            at = r * F + x * (F // 4)
-            wu[:, pl.ds(at, F // 4)] = fm[1, x, r].astype(F32).T
-        write(wu.at[:, pl.ds(r * F, F)], wu_o.at[:, pl.ds(r * F, F)])
-    for r in range(2):
-        for p in range(2):
-            wo[pl.ds(r * E + p * (E // 2), E // 2), :] = fa[0, p, r].astype(F32)
-    write(wo, wo_o)
-    for k in range(3):
-        for r in range(2):
-            a = fa[(k + 1) // 2, 2 * ((k + 1) % 2), r].astype(F32)
-            b = fa[(k + 1) // 2, 2 * ((k + 1) % 2) + 1, r].astype(F32)
-            wq[k, :, pl.ds(r * E, E)] = jnp.concatenate([a, b], axis=0).T
-        write(wq.at[k], wq_o.at[k])
     half = D // 2
     left = row == 0
 
@@ -736,7 +837,7 @@
     bu_o[...] = vec[0, 6:7, :]
     gain_o[...] = cut(vec[1, 0:2, :])
     bias_o[...] = cut(vec[1, 2:4, :])
-    for copy in copies:
+    for copy in copies[len(reads) :]:
         copy.wait()
 
 
@@ -747,17 +848,21 @@
     vmem = pl.BlockSpec(memory_space=pltpu.VMEM)
     hbm = pl.BlockSpec(memory_space=pl.ANY)
     shape = jax.ShapeDtypeStruct
-    out, tgrad, fm, fa, vec = pl.pallas_call(
+    early = [
+        shape((2, 4, 2, ROWS[0] // 8, D // 2), BF),
+        shape((2, 4, 2, ROWS[1] // 8, D // 2), BF),
+        shape((2, 4, 2, ROWS[2] // 8, D // 2), BF),
+        shape((2, 8, D), F32),
+    ]
+    out, tgrad, f0, f1, f2, vec = pl.pallas_call(
         body,
         out_shape=[
             shape((B, D // 2), BF),
             shape((B, D // 2), BF),
-            shape((2, 4, 2, F // 4, D // 2), BF),
-            shape((2, 4, 2, E // 2, D // 2), BF),
-            shape((2, 8, D), F32),
+            *early,
         ],
-        in_specs=[vmem, vmem, hbm, hbm, hbm, hbm] + [vmem] * 9,
-        out_specs=[vmem] * 5,
+        in_specs=[hbm] * 6 + [vmem] * 7 + [hbm] * 2,
+        out_specs=[vmem] * 6,
         scratch_shapes=[pltpu.VMEM(*spec) for spec in SCRATCH.values()]
         + [pltpu.SemaphoreType.DMA((NSEM,)), pltpu.SemaphoreType.DMA((NSEM,))],
         compiler_params=pltpu.CompilerParams(
@@ -791,12 +896,15 @@
             shape((2, D // 2), F32),
             shape((2, D // 2), F32),
         ],
-        in_specs=[vmem] * 5,
+        in_specs=[hbm] * 6,
         out_specs=[hbm, hbm, hbm, vmem, hbm, vmem, hbm, vmem, hbm, vmem, vmem, vmem],
-        scratch_shapes=[pltpu.VMEM(*spec) for spec in big] + [pltpu.SemaphoreType.DMA((12,))],
-        compiler_params=pltpu.CompilerParams(vmem_limit_bytes=40 * 1024 * 1024),
+        scratch_shapes=[pltpu.VMEM(e.shape, e.dtype) for e in early]
+        + [pltpu.VMEM((B, D // 2), BF)] * 2
+        + [pltpu.VMEM(*spec) for spec in big]
+        + [pltpu.SemaphoreType.DMA((16,))],
+        compiler_params=pltpu.CompilerParams(vmem_limit_bytes=60 * 1024 * 1024),
         name="last",
-    )(fm, fa, vec, out, tgrad)
+    )(f0, f1, f2, vec, out, tgrad)
     out, tgrad, wq, bq, wo, bo, wu, bu, wd, bd, gain, bias = results
     bo, bu, bd = bo.reshape(-1), bu.reshape(-1), bd.reshape(-1)
     return (out, tgrad, wq, bq, wo, bo, wu, bu, wd, bd, gain, bias)

time: 114 us -> 116 us (1.018)
  Pallas kernels: 108 us -> 115 us
  local copies, waits for them, and re-layouts: 5.55 us -> 0 us
    pallas_call x1, Pallas kernels: 104 us -> 110 us  [on_device(): pl.pallas_call(body, out_shape=[shape((B, D // 2), BF), shape((B, D // 2)...]
    unnamed x10 -> x0, local copies, waits for them, and re-layouts: 5.55 us -> none
    pallas_call x1, Pallas kernels: 3.64 us -> 4.96 us  [on_device(): pl.pallas_call(last, out_shape=[shape((B, D // 2), BF), shape((B, D // 2)...]
where the time goes in v3:
time: 116 us; the launch traced here: 115 us
  Pallas kernels  115 us (99%)
    pallas_call x1, Pallas kernels, on_device(): pl.pallas_call(body, out_shape=[shape((B, D // 2), BF), shape((B, D // 2)...  110 us
    pallas_call x1, Pallas kernels, on_device(): pl.pallas_call(last, out_shape=[shape((B, D // 2), BF), shape((B, D // 2)...  4.96 us

profile of v3, /device:TPU:1, one launch (start us, length us, event | category | flops | bytes accessed | tf_op | source)
XLA Modules:
  0.0 115.4 jit_solution(7731081305979942354)
XLA Ops:
  0.6 109.7 %block.1 = (bf16[256,512]{1,0:T(8,128)(2,1)}, bf16[256,512]{1,0:T(8,128)(2,1)}, bf16[2,4,2,80,512]{4,3,2,1,0:T(8,128)(2,1)}, bf16[2,4,2,64,512]{4,3,2,1,0:T(8,12...) custom-call(bf16[256,512]{1,0:T(8,128)(2,1)} %tok.1, bf16[256,512]{1,0:T(8,128)(2,1)} %cot.1, ...), custom_call_target="tpu_custom_call" | custom-call | tf_op jit(solution)/shard_map/block/pallas_call | solution.py:857
  110.3 5.0 %last.1 = (bf16[256,512]{1,0:T(8,128)(2,1)}, bf16[256,512]{1,0:T(8,128)(2,1)}, f32[3,512,256]{2,1,0:T(8,128)}, f32[3,256]{1,0:T(4,128)}, f32[256,512]{1,0:T(8,12...) custom-call(bf16[2,4,2,80,512]{4,3,2,1,0:T(8,128)(2,1)} %get-tuple-e, ...), custom_call_target="tpu_custom_call" | custom-call | tf_op jit(solution)/shard_map/last/pallas_call | solution.py:883

commit v4 on v3

--- a/solution.py
+++ b/solution.py
@@ -21,8 +21,23 @@
 B = 256
 EPSILON = 1e-05
 NSEM = 200
-YR = 144
-ZR = B - YR
+YROWS = dict(x=144, g=144, o=176, n=240)
+
+
+ORDER = (
+    0, 1, 2, 3, 4, 7, 8, 42, 2, 10, 3, 6, 11, 7, 4, 12, 8, 1, 5, 9, 15, 126, 38, 6, 14, 40, 40, 38,
+    127, 5, 13, 10, 11, 17, 130, 131, 12, 9, 16, 19, 20, 21, 22, 23, 26, 27, 128, 129, 14, 13, 18,
+    132, 133, 134, 39, 41, 135, 136, 21, 26, 29, 39, 137, 20, 22, 23, 24, 25, 27, 28, 30, 31, 34,
+    41, 138, 139, 140, 141, 29, 142, 143, 144, 30, 145, 25, 33, 146, 24, 32, 36, 148, 28, 35, 147,
+    31, 33, 32, 37, 77, 43, 47, 78, 44, 48, 50, 79, 45, 49, 51, 80, 46, 149, 150, 81, 151, 95, 152,
+    153, 81, 82, 83, 84, 85, 86, 154, 43, 53, 95, 44, 45, 46, 51, 50, 52, 54, 55, 56, 57, 96, 97,
+    98, 99, 100, 155, 56, 57, 58, 85, 86, 87, 156, 157, 158, 159, 99, 100, 101, 160, 60, 64, 161,
+    58, 61, 65, 67, 162, 52, 62, 66, 68, 87, 88, 59, 163, 60, 63, 70, 101, 102, 61, 71, 73, 165,
+    123, 164, 62, 72, 74, 109, 123, 74, 73, 63, 75, 75, 109, 110, 111, 112, 113, 114, 123, 68, 114,
+    113, 115, 67, 69, 88, 89, 90, 102, 103, 104, 123, 59, 166, 115, 116, 123, 124, 116, 117, 118,
+    104, 106, 69, 76, 103, 105, 107, 90, 92, 92, 106, 89, 91, 93, 91, 105, 117, 119, 119, 118, 120,
+    121, 120, 107, 108, 93, 94, 76, 125, 121, 122, 108, 94, 125, 122,
+)
 
 
 def nn(a, b):
@@ -70,70 +85,93 @@
         return copy
 
 
-def gather_tokens(net, own, full, at, half, col, row):
+def later(deps, cost, work):
+    yield deps, cost
+    work()
+
+
+def gather_tokens(net, add, done, name, begin, own, full, at, half, col, row, yr):
     right, left, peer = at["z1"], at["z3"], at["y1"]
-    cut = YR + 48
-
-    def place(c, h, start=0, size=B):
-        r = pl.ds(pl.multiple_of(c * B + start, 16), size)
+    zr = B - yr
+    part = zr // 32 * 16
+    cut = yr + part
+    c = {}
+
+    def place(b, h, start=0, size=B):
+        r = pl.ds(pl.multiple_of(b * B + start, 16), size)
         return full.at[r, pl.ds(pl.multiple_of(h * half, half), half)]
 
-    def move(device, *where):
-        return net.go(place(*where), place(*where), device)
-
-    mine = place(col, row)
+    def move(key, device, *where):
+        c[key] = net.go(place(*where), place(*where), device)
+        done.add(name + key)
+
+    def send(key, device, start, size):
+        c[key] = net.go(own.at[pl.ds(start, size)], place(col, row, start, size), device)
+        done.add(name + key)
+
     lcol, rcol, fcol = lax.rem(col + 3, 4), lax.rem(col + 1, 4), lax.rem(col + 2, 4)
-    c0 = net.go(own, mine, peer)
-    c1 = net.go(own, mine, right)
-    c2 = net.go(own, mine, left)
-    keep = net.local(own, mine)
-    yield
-    keep.wait()
-    c0.wait_recv()
-    c3 = move(right, col, 1 - row, 0, YR)
-    c4 = move(left, col, 1 - row, 0, YR)
-    yield
-    c1.wait_recv()
-    c5 = move(right, lcol, row, 0, cut)
-    e5 = move(peer, lcol, row, YR, ZR)
-    c2.wait_recv()
-    d4 = move(left, rcol, row, cut, B - cut)
-    e6 = move(peer, rcol, row, YR, ZR)
-    yield
-    c4.wait_recv()
-    c6 = move(left, rcol, 1 - row, 0, YR)
-    c3.wait_recv()
-    yield
-    e5.wait_recv()
-    e6.wait_recv()
-    yield
-    c5.wait_recv()
-    d4.wait_recv()
-    e7 = move(peer, fcol, row, YR, ZR)
-    yield
-    c6.wait_recv()
-    e7.wait_recv()
-
-
-def gather_weights(net, wqkv, wup, wout, wdown, s, at, core, row):
+
+    def begin_work():
+        yield begin, 0.1
+        c["keep"] = net.local(own, place(col, row))
+        send("p0", peer, 0, yr)
+        send("r1", right, yr, zr)
+        send("l1", left, yr, zr)
+        send("r0", right, 0, yr)
+        send("l0", left, 0, yr)
+        send("p1", peer, yr, zr)
+        c["keep"].wait()
+
+    def hop(keys, *work):
+        yield tuple(name + k for k in keys), 0.0
+        yield tuple(c[k] for k in keys), 0.05
+        for k in keys:
+            c[k].wait_recv()
+        for w in work:
+            move(*w)
+        done.update(name + k + "!" for k in keys)
+
+    def whole(flag, keys):
+        yield tuple(name + k + "!" for k in keys), 0.0
+        done.add(name + flag)
+
+    add(begin_work())
+    add(hop(["p0"], ("r2", right, col, 1 - row, 0, yr), ("l2", left, col, 1 - row, 0, yr)))
+    add(hop(["r1"], ("r3", right, lcol, row, yr, part), ("p2", peer, lcol, row, yr, zr)))
+    add(hop(["l1"], ("l3", left, rcol, row, cut, B - cut), ("p3", peer, rcol, row, yr, zr)))
+    add(hop(["r0"], ("r4", right, lcol, row, 0, yr)))
+    add(hop(["l2"], ("l4", left, rcol, 1 - row, 0, yr)))
+    add(hop(["r3", "l3"], ("p4", peer, fcol, row, yr, zr)))
+    add(hop(["p1"]))
+    add(hop(["l0"]))
+    add(hop(["r2"]))
+    add(hop(["p2"]))
+    add(hop(["p3"]))
+    add(hop(["r4"]))
+    add(hop(["l4"]))
+    add(hop(["p4"]))
+    add(whole("own", ["p0", "p1"]))
+    add(whole("left", ["r0", "r1", "r2", "p2"]))
+    add(whole("right", ["l0", "l1", "l2", "p3"]))
+    add(whole("far", ["r3", "r4", "l3", "l4", "p4"]))
+
+
+def gather_weights(net, add, done, wqkv, wup, wout, wdown, s, at, core, row):
     half, part = D // 2, D // 4
     mine, theirs = row, 1 - row
-    drows = rows(row, half)
+    drows, ocols = rows(row, half), rows(1 - row, half)
 
     def cut(which, size):
         return pl.ds(pl.multiple_of(which * size, size), size)
 
-    local = []
+    local = {}
     for k in range(3):
         kcols = pl.ds(k * E, E)
-        local.append(net.local(wqkv.at[k, :, cut(mine, E)], s.wq.at[drows, kcols]))
-    local.append(net.local(wup.at[:, cut(mine, F)], s.wu.at[drows]))
-    local.append(net.local(wout.at[cut(mine, E)], s.wo.at[:, drows]))
-    local.append(net.local(wdown.at[cut(mine, F)], s.wd.at[:, drows]))
-    src = cut(core, part)
-    dst = cut(row * 2 + core, part)
-    got = cut((1 - row) * 2 + core, part)
-    ocols = rows(1 - row, half)
+        local[k] = net.local(wqkv.at[k, :, cut(mine, E)], s.wq.at[drows, kcols])
+    local["u"] = net.local(wup.at[:, cut(mine, F)], s.wu.at[drows])
+    local["o"] = net.local(wout.at[cut(mine, E)], s.wo.at[:, drows])
+    local["d"] = net.local(wdown.at[cut(mine, F)], s.wd.at[:, drows])
+    src, dst, got = cut(core, part), cut(row * 2 + core, part), cut((1 - row) * 2 + core, part)
     far, near = at["y3"], at["core"]
     q = [
         net.go(wqkv.at[k, src, cut(theirs, E)], s.wq.at[dst, pl.ds(k * E, E)], far)
@@ -142,214 +180,213 @@
     u = net.go(wup.at[src, cut(theirs, F)], s.wu.at[dst], far)
     o = net.go(wout.at[cut(theirs * 2 + core, E // 2)], s.wo.at[cut(core, E // 2), drows], far)
     d = net.go(wdown.at[cut(theirs * 2 + core, F // 2)], s.wd.at[cut(core, F // 2), drows], far)
-    yield
-    for copy in q:
-        copy.wait_recv()
-    q2 = net.go(s.wq.at[got], s.wq.at[got], near)
-    yield
-    u.wait_recv()
-    u2 = net.go(s.wu.at[got], s.wu.at[got], near)
-    yield
-    q2.wait_recv()
-    for copy in local[:3]:
-        copy.wait()
-    yield
-    u2.wait_recv()
-    local[3].wait()
-    yield
-    o.wait_recv()
-    ov = s.wo.at[cut(core, E // 2), ocols]
-    o2 = net.go(ov, ov, near)
-    d.wait_recv()
-    dv = s.wd.at[cut(core, F // 2), ocols]
-    d2 = net.go(dv, dv, near)
-    yield
-    local[4].wait()
-    local[5].wait()
-    o2.wait_recv()
-    d2.wait_recv()
-
-
-def ring_scatter(net, part, bufs, me, right, left, size, width):
+
+    def share(flag, copies, view, locals_):
+        yield tuple(copies), 0.05
+        for copy in copies:
+            copy.wait_recv()
+        second = net.go(view, view, near)
+        yield (second,), 0.0
+        second.wait_recv()
+        for k in locals_:
+            local[k].wait()
+        done.add(flag)
+
+    add(share("wq", q, s.wq.at[got], range(3)))
+    add(share("wu", [u], s.wu.at[got], "u"))
+    add(share("wo", [o], s.wo.at[cut(core, E // 2), ocols], "o"))
+    add(share("wd", [d], s.wd.at[cut(core, F // 2), ocols], "d"))
+
+
+def ring_scatter(net, add, done, name, part, bufs, me, right, left, width, ready):
     ta, tb, inl, inr = bufs
     lo, hi = pl.ds(0, width), pl.ds(width, width)
     far, rb, lb = lax.rem(me + 2, 4), lax.rem(me + 1, 4), lax.rem(me + 3, 4)
-    a = net.go(part(far, lo), ta, right)
-    b = net.go(part(far, hi), tb, left)
-    c = net.go(part(rb, hi), inl.at[:, hi], right)
-    d = net.go(part(lb, lo), inr.at[:, lo], left)
-    yield
-    a.wait_recv()
-    view = part(rb, lo)
-    view[...] = (view[...].astype(F32) + ta[...].astype(F32)).astype(BF)
-    e = net.go(view, inl.at[:, lo], right)
-    b.wait_recv()
-    view = part(lb, hi)
-    view[...] = (view[...].astype(F32) + tb[...].astype(F32)).astype(BF)
-    f = net.go(view, inr.at[:, hi], left)
-    yield
-    for copy in (c, d, e, f):
-        copy.wait_recv()
-
-
-def scatter(net, p, s, at, col, row, look=None):
-    half = D // 2
-    far, rb, lb = lax.rem(col + 2, 4), lax.rem(col + 1, 4), lax.rem(col + 3, 4)
-    mcols, ocols = rows(row, half), rows(1 - row, half)
-
-    def yrows(b):
-        return pl.ds(pl.multiple_of(b * B, B), YR)
-
-    def zrows(b):
-        return pl.ds(pl.multiple_of(b * B + YR, 16), ZR)
-
-    def zpart(b, cols):
-        return p.at[zrows(b), pl.ds(pl.multiple_of(row * half + cols.start, 256), cols.size)]
-
-    order = (far, rb, lb, col)
-    first = [net.go(p.at[zrows(b), ocols], s.ry.at[k], at["y1"]) for k, b in enumerate(order)]
-    right, left = at["z1"], at["z3"]
-    ring = ring_scatter(
-        net, lambda b, cols: p.at[yrows(b), cols], (s.ta, s.tb, s.inl, s.inr), col, right, left, YR, half
-    )
-    step(ring)
-    yield
-
-    def add(k):
-        first[k].wait_recv()
-        view = p.at[zrows(order[k]), mcols]
-        view[...] = (view[...].astype(F32) + s.ry[k].astype(F32)).astype(BF)
-
-    step(ring)
-    yield
-    for k in range(3):
-        add(k)
-    ring2 = ring_scatter(
-        net, zpart, (s.ta2, s.tb2, s.inl2, s.inr2), col, right, left, ZR, half // 2
-    )
-    step(ring2)
-    yield
-    add(3)
-    finish(ring)
-    for h in range(2):
-        cols = pl.ds(h * half, half)
-        total = (
-            p[yrows(col), cols].astype(F32) + s.inl[:, cols].astype(F32) + s.inr[:, cols].astype(F32)
-        )
-        s.ysend[h] = total.astype(BF)
-        if look is not None:
-            look(h, total)
-    last = net.go(s.ysend.at[1 - row], s.yrecv, at["y1"])
-    yield
-    step(ring2)
-    yield
-    finish(ring2)
-    last.wait_recv()
-
-
-def total_y(s, row):
-    return s.ysend[row].astype(F32) + s.yrecv[...].astype(F32)
-
-
-def total_z(p, s, col, row):
-    own = p[pl.ds(pl.multiple_of(col * B + YR, 16), ZR), rows(row, D // 2)]
-    return own.astype(F32) + s.inl2[...].astype(F32) + s.inr2[...].astype(F32)
-
-
-def reduce_weights(net, grad, s, at, me, n):
+    c = {}
+
+    def send(deps, *sends):
+        yield deps, 0.05
+        for key, src, dst, device in sends:
+            c[key] = net.go(src, dst, device)
+            done.add(name + key)
+
+    def through(came, flag, buf, view, key, dst, device):
+        yield (name + came, flag), 0.0
+        yield (c[came],), 0.15
+        c[came].wait_recv()
+        view[...] = (view[...].astype(F32) + buf[...].astype(F32)).astype(BF)
+        c[key] = net.go(view, dst, device)
+        done.add(name + key)
+
+    def finish():
+        yield tuple(name + k for k in "cdef") + (ready[3],), 0.0
+        yield tuple(c[k] for k in "cdef"), 0.0
+        for k in "cdef":
+            c[k].wait_recv()
+        done.add(name + "sum")
+
+    add(send((ready[0],), ("a", part(far, lo), ta, right), ("b", part(far, hi), tb, left)))
+    add(send((ready[1],), ("c", part(rb, hi), inl.at[:, hi], right)))
+    add(send((ready[2],), ("d", part(lb, lo), inr.at[:, lo], left)))
+    add(through("a", ready[1], ta, part(rb, lo), "e", inl.at[:, lo], right))
+    add(through("b", ready[2], tb, part(lb, hi), "f", inr.at[:, hi], left))
+    add(finish())
+
+
+def reduce_weights(net, add, done, name, begin, grad, s, at, me, n):
     core, x, row = me["core"], me["x"], me["row"]
     half, size = n // 2, n // 8
-    base = core * half
-    away = (1 - core) * half
-    c = net.go(grad.at[pl.ds(pl.multiple_of(away, half), half)], s.rc, at["core"])
-    yield
-    c.wait_recv()
-    own = grad.at[pl.ds(pl.multiple_of(base, half), half)]
-    own[...] = (own[...].astype(F32) + s.rc[...].astype(F32)).astype(BF)
+    base, away = core * half, (1 - core) * half
+    x1, x3, near = at["x1"], at["x3"], at["core"]
+    lx, rx, fx = lax.rem(x + 3, 4), lax.rem(x + 1, 4), lax.rem(x + 2, 4)
+    c = {}
+
+    def start():
+        yield (begin,), 0.05
+        copy = net.go(grad.at[pl.ds(pl.multiple_of(away, half), half)], s.rc, near)
+        yield (copy,), 0.4 * n / 640
+        copy.wait_recv()
+        own = grad.at[pl.ds(pl.multiple_of(base, half), half)]
+        own[...] = (own[...].astype(F32) + s.rc[...].astype(F32)).astype(BF)
+        done.add(name + "core")
 
     def part(block, cols):
         return grad.at[pl.ds(pl.multiple_of(base + block * size, size), size), cols]
 
-    yield from ring_scatter(
-        net, part, (s.ta, s.tb, s.inl, s.inr), x, at["x1"], at["x3"], size, D // 2
-    )
-    for h in range(2):
-        cols = pl.ds(h * (D // 2), D // 2)
-        total = (
-            part(x, cols)[...].astype(F32) + s.inl[:, cols].astype(F32) + s.inr[:, cols].astype(F32)
-        )
-        s.sy[h] = total.astype(BF)
-    g0 = net.go(s.sy.at[row], s.ry.at[0], at["y2"])
-    g1 = net.go(s.sy.at[1 - row], s.ry.at[1], at["y1"])
-    g2 = net.go(s.sy.at[1 - row], s.ry.at[2], at["y3"])
-    yield
-    g0.wait_recv()
-    s.fin[core, x, row] = (s.sy[row].astype(F32) + s.ry[0].astype(F32)).astype(BF)
-    g1.wait_recv()
-    g2.wait_recv()
-    s.fin[core, x, 1 - row] = (s.ry[1].astype(F32) + s.ry[2].astype(F32)).astype(BF)
-    h0 = s.fin.at[core, x, 0]
-    h1 = s.fin.at[core, x, 1]
-    a0 = net.go(h0, h0, at["x1"])
-    a1 = net.go(h1, h1, at["x3"])
-    a2 = net.go(h1, h1, at["x1"])
-    a3 = net.go(h0, h0, at["x3"])
-    k0 = net.go(s.fin.at[core, x], s.fin.at[core, x], at["core"])
-    yield
-    lx, rx = lax.rem(x + 3, 4), lax.rem(x + 1, 4)
-    a0.wait_recv()
-    v = s.fin.at[core, lx, 0]
-    a4 = net.go(v, v, at["x1"])
-    a1.wait_recv()
-    v = s.fin.at[core, rx, 1]
-    a5 = net.go(v, v, at["x3"])
-    a2.wait_recv()
-    v = s.fin.at[core, lx]
-    k1 = net.go(v, v, at["core"])
-    a3.wait_recv()
-    v = s.fin.at[core, rx]
-    k2 = net.go(v, v, at["core"])
-    yield
-    a4.wait_recv()
-    a5.wait_recv()
-    v = s.fin.at[core, lax.rem(x + 2, 4)]
-    k3 = net.go(v, v, at["core"])
-    for copy in (k0, k1, k2):
-        copy.wait_recv()
-    yield
-    k3.wait_recv()
-
-
-def reduce_vectors(net, s, at):
+    def across():
+        yield (name + "sum",), 0.2
+        for h in range(2):
+            cols = pl.ds(h * (D // 2), D // 2)
+            total = part(x, cols)[...].astype(F32) + s.inl[:, cols].astype(F32)
+            s.sy[h] = (total + s.inr[:, cols].astype(F32)).astype(BF)
+        g0 = net.go(s.sy.at[row], s.ry.at[0], at["y2"])
+        g1 = net.go(s.sy.at[1 - row], s.ry.at[1], at["y1"])
+        g2 = net.go(s.sy.at[1 - row], s.ry.at[2], at["y3"])
+        yield (g0, g1, g2), 0.15
+        for copy in (g0, g1, g2):
+            copy.wait_recv()
+        s.fin[core, x, row] = (s.sy[row].astype(F32) + s.ry[0].astype(F32)).astype(BF)
+        s.fin[core, x, 1 - row] = (s.ry[1].astype(F32) + s.ry[2].astype(F32)).astype(BF)
+        for key, h, device in (("a", 0, x1), ("b", 1, x3), ("c", 1, x1), ("d", 0, x3)):
+            view = s.fin.at[core, x, h]
+            c[key] = net.go(view, view, device)
+        view = s.fin.at[core, x]
+        c["k"] = net.go(view, view, near)
+        done.add(name + "sent")
+
+    def hop(keys, flag, view, device, key, need=()):
+        yield (name + flag,) + tuple(name + k + "!" for k in need), 0.0
+        yield tuple(c[k] for k in keys), 0.05
+        for k in keys:
+            c[k].wait_recv()
+        c[key] = net.go(view, view, device)
+        done.update(name + k + "!" for k in keys)
+        done.add(name + key)
+
+    def end():
+        yield tuple(name + k for k in ("l", "m", "n")), 0.0
+        yield tuple(c[k] for k in "klmn"), 0.0
+        for k in "klmn":
+            c[k].wait_recv()
+        done.add(name + "end")
+
+    ready = (name + "core",) * 4
+    add(start())
+    ring_scatter(
+        net, add, done, name, part, (s.ta, s.tb, s.inl, s.inr), x, x1, x3, D // 2, ready
+    )
+    add(across())
+    add(hop("a", "sent", s.fin.at[core, lx, 0], x1, "p"))
+    add(hop("b", "sent", s.fin.at[core, rx, 1], x3, "q"))
+    add(hop("c", "sent", s.fin.at[core, lx], near, "l", "a"))
+    add(hop("d", "sent", s.fin.at[core, rx], near, "m", "b"))
+    add(hop("pq", "p", s.fin.at[core, fx], near, "n", "b"))
+    add(end())
+
+
+def reduce_vectors(net, done, s, at):
+    yield ("vec",), 0.0
     c = net.go(s.vec, s.vr.at[0], at["core"])
-    yield
+    yield (c,), 0.05
     c.wait_recv()
     s.vs[0] = s.vec[...] + s.vr[0]
     for n, axis in enumerate("xyz"):
         copies = [net.go(s.vs.at[n], s.vr.at[3 * n + k], at[axis + str(k)]) for k in (1, 2, 3)]
-        yield
+        yield tuple(copies), 0.05
         for copy in copies:
             copy.wait_recv()
         s.vs[n + 1] = (s.vs[n] + s.vr[3 * n + 1]) + (s.vr[3 * n + 2] + s.vr[3 * n + 3])
-
-
-def step(gen):
-    next(gen, None)
-
-
-def finish(gen):
-    for _ in gen:
-        pass
-
-
-def interleave(*gens):
-    live = list(gens)
-    while live:
-        for gen in list(live):
-            try:
-                next(gen)
-            except StopIteration:
-                live.remove(gen)
+    done.add("vsum")
+
+
+def scatter(net, add, done, name, ready, p, s, at, col, row, yr, look=None):
+    half, zr = D // 2, B - yr
+    far, rb, lb = lax.rem(col + 2, 4), lax.rem(col + 1, 4), lax.rem(col + 3, 4)
+    mcols, ocols = rows(row, half), rows(1 - row, half)
+    right, left, peer = at["z1"], at["z3"], at["y1"]
+
+    def yrows(b):
+        return pl.ds(pl.multiple_of(b * B, B), yr)
+
+    def zrows(b):
+        return pl.ds(pl.multiple_of(b * B + yr, 16), zr)
+
+    def zpart(b, cols):
+        return p.at[zrows(b), pl.ds(pl.multiple_of(row * half + cols.start, 256), cols.size)]
+
+    def pair(k, b):
+        yield (ready[k],), 0.05
+        copy = net.go(p.at[zrows(b), ocols], s.ry.at[k], peer)
+        yield (copy,), 0.15
+        copy.wait_recv()
+        view = p.at[zrows(b), mcols]
+        view[...] = (view[...].astype(F32) + s.ry[k].astype(F32)).astype(BF)
+        done.add(name + "z" + str(k))
+
+    def last():
+        yield (name + "y.sum",), 0.3
+        for h in range(2):
+            cols = pl.ds(h * half, half)
+            total = p[yrows(col), cols].astype(F32) + s.inl[:, cols].astype(F32)
+            total += s.inr[:, cols].astype(F32)
+            s.ysend[h] = total.astype(BF)
+            if look is not None:
+                look(h, total)
+        copy = net.go(s.ysend.at[1 - row], s.yrecv, peer)
+        yield (copy,), 0.0
+        copy.wait_recv()
+        done.add(name + "y.end")
+
+    for k, b in enumerate((far, rb, lb, col)):
+        add(pair(k, b))
+    ring_scatter(
+        net, add, done, name + "y.", lambda b, cols: p.at[yrows(b), cols],
+        (s.ta, s.tb, s.inl, s.inr), col, right, left, half, ready,
+    )
+    ring_scatter(
+        net, add, done, name + "z.", zpart,
+        (s.ta2, s.tb2, s.inl2, s.inr2), col, right, left, half // 2,
+        tuple(name + "z" + str(k) for k in range(4)),
+    )
+    add(last())
+
+
+def total_y(s, row):
+    return s.ysend[row].astype(F32) + s.yrecv[...].astype(F32)
+
+
+def total_z(p, s, col, row, yr):
+    own = p[pl.ds(pl.multiple_of(col * B + yr, 16), B - yr), rows(row, D // 2)]
+    return own.astype(F32) + s.inl2[...].astype(F32) + s.inr2[...].astype(F32)
+
+
+def run(tasks, done):
+    asked = [next(task)[0] for task in tasks]
+    for k in ORDER:
+        for need in asked[k]:
+            assert not isinstance(need, str) or need in done, "order"
+        asked[k] = next(tasks[k], ((),))[0]
+    assert all(next(task, None) is None for task in tasks), "unfinished"
 
 
 def turn(values, cos, sin):
@@ -410,19 +447,21 @@
     vr=((10, 8, D), F32),
     vs=((4, 8, D), F32),
 )
-SCATTER = dict(
-    ta=((YR, D // 2), BF),
-    tb=((YR, D // 2), BF),
-    inl=((YR, D), BF),
-    inr=((YR, D), BF),
-    ry=((4, ZR, D // 2), BF),
-    ta2=((ZR, D // 4), BF),
-    tb2=((ZR, D // 4), BF),
-    inl2=((ZR, D // 2), BF),
-    inr2=((ZR, D // 2), BF),
-    ysend=((2, YR, D // 2), BF),
-    yrecv=((YR, D // 2), BF),
-)
+def scatter_scratch(yr):
+    zr = B - yr
+    return dict(
+        ta=((yr, D // 2), BF),
+        tb=((yr, D // 2), BF),
+        inl=((yr, D), BF),
+        inr=((yr, D), BF),
+        ry=((4, zr, D // 2), BF),
+        ta2=((zr, D // 4), BF),
+        tb2=((zr, D // 4), BF),
+        inl2=((zr, D // 2), BF),
+        inr2=((zr, D // 2), BF),
+        ysend=((2, yr, D // 2), BF),
+        yrecv=((yr, D // 2), BF),
+    )
 
 
 def reduce_scratch(n):
@@ -439,7 +478,7 @@
 
 ROWS = (F + E, F, 3 * E)
 for name in "on":
-    SCRATCH.update({name + "_" + key: spec for key, spec in SCATTER.items()})
+    SCRATCH.update({name + "_" + key: v for key, v in scatter_scratch(YROWS[name]).items()})
 for k, n in enumerate(ROWS):
     SCRATCH.update({f"r{k}_{key}": spec for key, spec in reduce_scratch(n).items()})
 
@@ -480,12 +519,12 @@
         pl.semaphore_signal(barrier, inc=1, device_id=device, device_id_type=MESH)
     pl.semaphore_wait(barrier, len(at))
 
-    gx = gather_tokens(net, tok, s.xall, at, half, col, row)
-    gg = gather_tokens(net, cot, s.gall, at, half, col, row)
-    gw = gather_weights(net, wqkv, wup, wout, wdown, s, at, core, row)
+    tasks, done = [], set()
+    add = tasks.append
+    gather_tokens(net, add, done, "x.", (), tok, s.xall, at, half, col, row, YROWS["x"])
+    gather_tokens(net, add, done, "g.", ("x.r2!", "x.l2!"), cot, s.gall, at, half, col, row, YROWS["g"])
     nbc = net.go(s.nbs, s.nb.at[row], y1)
-    step(gx)
-    step(gw)
+    gather_weights(net, add, done, wqkv, wup, wout, wdown, s, at, core, row)
     tabs = [net.local(ctab_h, s.ctab), net.local(stab_h, s.stab)]
     s.nb[row] = s.nbs[...]
     s.vec[...] = jnp.zeros_like(s.vec)
@@ -508,14 +547,21 @@
     fcols = pl.ds(pl.multiple_of(row * F, F), F)
     gcols = pl.ds(pl.multiple_of(row * half, half), half)
 
-    nbc.wait_recv()
-
     def wide(k):
         return jnp.concatenate([s.nb[0, k : k + 1, :], s.nb[1, k : k + 1, :]], axis=1)
 
-    gain0, gain1, bias0, bias1 = wide(0), wide(1), wide(2), wide(3)
+    def params():
+        yield (nbc,), 0.0
+        nbc.wait_recv()
+        for copy in tabs:
+            copy.wait()
+        done.add("nb")
+
+    add(params())
 
     def norm(c):
+        gain0, gain1, bias0, bias1 = wide(0), wide(1), wide(2), wide(3)
+
         @pl.loop(0, 2)
         def _(b):
             r = rows(c * 2 + b, 128)
@@ -561,36 +607,19 @@
         split_heads(s.dom, r, dout)
 
     rb, lb, fb = lax.rem(col + 1, 4), lax.rem(col + 3, 4), lax.rem(col + 2, 4)
-    step(gx)
-    norm(col)
-    step(gx)
-    step(gw)
-    step(gx)
-    step(gx)
-    step(gg)
-    norm(lb)
-    norm(rb)
-    for copy in tabs:
-        copy.wait()
-    step(gw)
-    step(gw)
-    project(col)
-    project(lb)
-    step(gx)
-    project(rb)
-    step(gw)
-    expand(col)
-    step(gg)
-    expand(lb)
-    expand(rb)
-    step(gw)
-    finish(gx)
-    norm(fb)
-    project(fb)
-    expand(fb)
+    blocks = {"own": col, "left": lb, "right": rb, "far": fb}
+    outward = ("far", "right", "left", "own")
+
+    def mark(flag, work, *args):
+        def both():
+            work(*args)
+            done.add(flag)
+
+        return both
 
     first = [0, 256, 768, 1536]
-    for i in range(4):
+
+    def attend(i):
         n = (i + 1) * B
         q = pl.ds(i * B, B)
 
@@ -609,48 +638,8 @@
             s.mt[hrows, q] = nn(s.vt[hrows, pl.ds(0, n)], probs.astype(BF)).astype(BF)
 
         s.mixed[q, :] = s.mt[:, q].astype(F32).T.astype(BF)
-        step(gg) if i in (1, 3) else None
-
-    finish(gw)
-    step(gg)
-
-    @pl.loop(0, 4)
-    def _(b):
-        r = rows(b)
-        s.op[r, :] = (nn(s.mixed[r, :], s.wo[...]) + nn(s.hid[r, :], s.wd[...])).astype(BF)
-
-    step(gg)
-    contract(col)
-    contract(lb)
-    contract(rb)
-    finish(gg)
-    contract(fb)
-    so, sn = under(s, "o_"), under(s, "n_")
-    ro = scatter(net, s.op, so, at, col, row)
-    step(ro)
-
-    where = dict(core=core, x=x, row=row)
-    r0 = reduce_weights(net, s.g1, under(s, "r0_", fin=f0), at, where, ROWS[0])
-    r1 = reduce_weights(net, s.g2, under(s, "r1_", fin=f1), at, where, ROWS[1])
-    r2 = reduce_weights(net, s.g3, under(s, "r2_", fin=f2), at, where, ROWS[2])
-
-    @pl.loop(0, 4)
-    def _(b):
-        r = rows(b, 128)
-        s.g1[r, :] = tn(s.hid[:, r], s.gall[...]).astype(BF)
-
-    s.g1[F:, :] = nn(s.mt[...], s.gall[...]).astype(BF)
-    step(r0)
-
-    @pl.loop(0, 4)
-    def _(b):
-        r = rows(b, 128)
-        s.g2[r, :] = tn(s.hpg[:, r], s.mim[...]).astype(BF)
-
-    step(r1)
-    step(r0)
-
-    for i in range(4):
+
+    def attend_back(i):
         n = (i + 1) * B
         q = pl.ds(i * B, B)
 
@@ -665,16 +654,25 @@
             hrows = rows(h, HD)
             s.dqt[hrows, q] = nn(s.kt[hrows, pl.ds(0, n)], dscore) * (1.0 / math.sqrt(HD))
 
-        if i == 0:
-            step(r1)
-        if i == 2:
-            step(ro)
-        if i == 3:
-            step(r0)
-            step(ro)
-
-    @pl.loop(0, 4)
-    def _(b):
+    def branch(b):
+        r = rows(b)
+        s.op[r, :] = (nn(s.mixed[r, :], s.wo[...]) + nn(s.hid[r, :], s.wd[...])).astype(BF)
+
+    def down_grad():
+        @pl.loop(0, 4)
+        def _(b):
+            r = rows(b, 128)
+            s.g1[r, :] = tn(s.hid[:, r], s.gall[...]).astype(BF)
+
+        s.g1[F:, :] = nn(s.mt[...], s.gall[...]).astype(BF)
+
+    def up_grad():
+        @pl.loop(0, 4)
+        def _(b):
+            r = rows(b, 128)
+            s.g2[r, :] = tn(s.hpg[:, r], s.mim[...]).astype(BF)
+
+    def qkv_grad(b):
         r = rows(b)
         cos, sin = s.ctab[r, :], -s.stab[r, :]
         dq = turn(s.dqt[:, r].T, cos, sin).astype(BF)
@@ -685,19 +683,15 @@
         ecols3 = pl.ds(pl.multiple_of(row * 3 * E, 3 * E), 3 * E)
         s.vec[5:6, ecols3] += jnp.sum(both.astype(F32), axis=0, keepdims=True)
 
-    step(r1)
-    step(ro)
-
-    @pl.loop(0, 3)
-    def _(b):
-        r = rows(b, E)
-        s.g3[r, :] = tn(s.qkvg[:, r], s.ain[...]).astype(BF)
-
-    step(r2)
-
-    @pl.loop(0, 4)
-    def _(b):
+    def qkv_weight_grad():
+        @pl.loop(0, 3)
+        def _(b):
+            r = rows(b, E)
+            s.g3[r, :] = tn(s.qkvg[:, r], s.ain[...]).astype(BF)
+
+    def input_grad(b):
         r = rows(b)
+        gain0, gain1 = wide(0), wide(1)
         attn = nt(s.qkvg[r, :], s.wq[...])
         mlp = nt(s.hpg[r, :], s.wu[...])
         normed = (s.xall[r, :].astype(F32) - s.mean[r, :]) * s.inv[r, :]
@@ -707,63 +701,89 @@
         s.vec[2:3, :] += jnp.sum(attn, axis=0, keepdims=True)
         s.vec[3:4, :] += jnp.sum(mlp, axis=0, keepdims=True)
 
-    r = rows(col)
-    mean, inv = s.mean[r, :], s.inv[r, :]
+    so, sn = under(s, "o_"), under(s, "n_")
+    where = dict(core=core, x=x, row=row)
     sums = []
+    ny = YROWS["n"]
+    own = rows(col)
 
     def look(h, total):
-        xv = s.xall[pl.ds(pl.multiple_of(col * B, B), YR), pl.ds(h * half, half)].astype(F32)
-        normed = (xv - mean[:YR]) * inv[:YR]
+        mean, inv = s.mean[own, :], s.inv[own, :]
+        xv = s.xall[pl.ds(pl.multiple_of(col * B, B), ny), pl.ds(h * half, half)].astype(F32)
+        normed = (xv - mean[:ny]) * inv[:ny]
         sums.append(jnp.sum(total, axis=1, keepdims=True))
         sums.append(jnp.sum(total * normed, axis=1, keepdims=True))
 
-    rn = scatter(net, s.ng, sn, at, col, row, look)
-    step(rn)
-    rv = reduce_vectors(net, s, at)
-    step(rv)
-    step(r2)
-    step(r0)
-    step(ro)
-    step(r1)
-    finish(ro)
-    bias_out = flat(bout[...]) + flat(bdown[...])
-    xv = s.xall[r, gcols].astype(F32) + bias_out
-    out[...] = (xv + jnp.concatenate([total_y(so, row), total_z(s.op, so, col, row)])).astype(BF)
-    step(rv)
-    step(r0)
-    step(rn)
-    step(r2)
-    step(r1)
-    step(rv)
-    step(rn)
-    step(r0)
-    step(r2)
-    step(r1)
-    step(rv)
-    step(rn)
-    step(r2)
-    step(r0)
-    step(rn)
-    step(r1)
-    finish(rn)
-    normed = (s.xall[r, gcols].astype(F32) - mean) * inv
-    zsum = total_z(s.ng, sn, col, row)
-    first_sum = jnp.concatenate([sums[0] + sums[2], jnp.sum(zsum, axis=1, keepdims=True)])
-    second = jnp.sum(zsum * normed[YR:], axis=1, keepdims=True)
-    second_sum = jnp.concatenate([sums[1] + sums[3], second])
-    lane = lax.broadcasted_iota(jnp.int32, (B, 128), 1)
-    s.ssend[...] = jnp.where(lane < 4, first_sum, second_sum).T[:8, :]
-    ys = net.go(s.ssend, s.srecv, y1)
-    interleave(r0, r2, r1, rv)
-    vout[0] = s.vs[2]
-    vout[1] = s.vs[3]
-    ys.wait_recv()
-    both = (s.ssend[...] + s.srecv[...]) * (1.0 / D)
-    both = jnp.concatenate([both] * 16).T
-    total = jnp.concatenate([total_y(sn, row), zsum])
-    tgrad[...] = (
-        s.gall[r, gcols].astype(F32) + inv * (total - both[:, 0:1] - normed * both[:, 4:5])
-    ).astype(BF)
+    def write_out():
+        xv = s.xall[own, gcols].astype(F32) + (flat(bout[...]) + flat(bdown[...]))
+        total = jnp.concatenate([total_y(so, row), total_z(s.op, so, col, row, YROWS["o"])])
+        out[...] = (xv + total).astype(BF)
+
+    def write_grad():
+        yield ("n.y.sum", "n.y.end", "n.z.sum"), 0.4
+        mean, inv = s.mean[own, :], s.inv[own, :]
+        normed = (s.xall[own, gcols].astype(F32) - mean) * inv
+        zsum = total_z(s.ng, sn, col, row, ny)
+        first_sum = jnp.concatenate([sums[0] + sums[2], jnp.sum(zsum, axis=1, keepdims=True)])
+        second = jnp.sum(zsum * normed[ny:], axis=1, keepdims=True)
+        second_sum = jnp.concatenate([sums[1] + sums[3], second])
+        lane = lax.broadcasted_iota(jnp.int32, (B, 128), 1)
+        s.ssend[...] = jnp.where(lane < 4, first_sum, second_sum).T[:8, :]
+        ys = net.go(s.ssend, s.srecv, y1)
+        yield (ys,), 0.5
+        ys.wait_recv()
+        both = (s.ssend[...] + s.srecv[...]) * (1.0 / D)
+        both = jnp.concatenate([both] * 16).T
+        total = jnp.concatenate([total_y(sn, row), zsum])
+        tgrad[...] = (
+            s.gall[own, gcols].astype(F32) + inv * (total - both[:, 0:1] - normed * both[:, 4:5])
+        ).astype(BF)
+
+    def write_vectors():
+        vout[0] = s.vs[2]
+        vout[1] = s.vs[3]
+
+    scatter(net, add, done, "o.", tuple("send." + b for b in outward), s.op, so, at, col, row, YROWS["o"])
+    scatter(net, add, done, "n.", tuple("ng." + b for b in outward), s.ng, sn, at, col, row, ny, look)
+    for b in outward:
+        add(later(("op." + b, "g.far"), 0.0, mark("send." + b, lambda: None)))
+    reduce_weights(net, add, done, "a.", "g1", s.g1, under(s, "r0_", fin=f0), at, where, ROWS[0])
+    reduce_weights(net, add, done, "b.", "g2", s.g2, under(s, "r1_", fin=f1), at, where, ROWS[1])
+    reduce_weights(net, add, done, "c.", "g3", s.g3, under(s, "r2_", fin=f2), at, where, ROWS[2])
+    add(reduce_vectors(net, done, s, at))
+    add(later(("vsum",), 0.05, write_vectors))
+    add(write_grad())
+    for name, b in blocks.items():
+        add(later(("nb", "x." + name), 0.28, mark("norm." + name, norm, b)))
+        add(later(("wq", "norm." + name), 0.63, mark("proj." + name, project, b)))
+    needs = tuple("proj." + name for name in blocks)
+    for i in range(4):
+        add(later(needs, 0.58 * (i + 1), mark(f"attf{i}", attend, i)))
+        needs = (f"attf{i}",)
+    for name, b in blocks.items():
+        add(later(("wu", "norm." + name), 0.55, mark("exp." + name, expand, b)))
+    for name in outward:
+        needs = ("wo", "wd", "attf3", "exp." + name)
+        add(later(needs, 0.7, mark("op." + name, branch, blocks[name])))
+    for name, b in blocks.items():
+        needs = ("wo", "wd", "g." + name, "exp." + name)
+        add(later(needs, 0.4, mark("con." + name, contract, b)))
+    allg = tuple("g." + name for name in blocks) + tuple("exp." + name for name in blocks)
+    add(later(allg + ("attf3",), 1.85, mark("g1", down_grad)))
+    allc = tuple("con." + name for name in blocks)
+    add(later(allc, 1.65, mark("g2", up_grad)))
+    needs = allc + ("attf3",)
+    for i in range(4):
+        add(later(needs, 0.6 * (i + 1), mark(f"attb{i}", attend_back, i)))
+        needs = (f"attb{i}",)
+    for name in outward:
+        add(later(("attb3",), 0.46, mark("qg." + name, qkv_grad, blocks[name])))
+    for name in outward:
+        add(later(("qg." + name,), 0.65, mark("ng." + name, input_grad, blocks[name])))
+    add(later(tuple("qg." + name for name in blocks), 1.75, mark("g3", qkv_weight_grad)))
+    add(later(tuple("ng." + name for name in blocks), 0.0, mark("vec", lambda: None)))
+    add(later(("o.y.end", "o.z.sum"), 0.3, mark("out", write_out)))
+    run(tasks, done)
     for copy in net.sent:
         copy.wait_send()
 

time: 116 us -> 113 us (0.974)
  Pallas kernels: 115 us -> 112 us
    pallas_call x1, Pallas kernels: 110 us -> 107 us  [on_device(): pl.pallas_call(body, out_shape=[shape((B, D // 2), BF), shape((B, D // 2)...]
where the time goes in v4:
time: 113 us
  Pallas kernels  112 us (99%)
    pallas_call x1, Pallas kernels, on_device(): pl.pallas_call(body, out_shape=[shape((B, D // 2), BF), shape((B, D // 2)...  107 us
    pallas_call x1, Pallas kernels, on_device(): pl.pallas_call(last, out_shape=[shape((B, D // 2), BF), shape((B, D // 2)...  4.96 us

profile of v4, /device:TPU:1, one launch (start us, length us, event | category | flops | bytes accessed | tf_op | source)
XLA Modules:
  0.0 112.9 jit_solution(301855454009756117)
XLA Ops:
  0.6 107.1 %block.1 = (bf16[256,512]{1,0:T(8,128)(2,1)}, bf16[256,512]{1,0:T(8,128)(2,1)}, bf16[2,4,2,80,512]{4,3,2,1,0:T(8,128)(2,1)}, bf16[2,4,2,64,512]{4,3,2,1,0:T(8,12...) custom-call(bf16[256,512]{1,0:T(8,128)(2,1)} %tok.1, bf16[256,512]{1,0:T(8,128)(2,1)} %cot.1, ...), custom_call_target="tpu_custom_call" | custom-call | tf_op jit(solution)/shard_map/block/pallas_call | solution.py:877
  107.7 5.0 %last.1 = (bf16[256,512]{1,0:T(8,128)(2,1)}, bf16[256,512]{1,0:T(8,128)(2,1)}, f32[3,512,256]{2,1,0:T(8,128)}, f32[3,256]{1,0:T(4,128)}, f32[256,512]{1,0:T(8,12...) custom-call(bf16[2,4,2,80,512]{4,3,2,1,0:T(8,128)(2,1)} %get-tuple-e, ...), custom_call_target="tpu_custom_call" | custom-call | tf_op jit(solution)/shard_map/last/pallas_call | solution.py:903

commit v5 on v4

--- a/solution.py
+++ b/solution.py
@@ -21,22 +21,22 @@
 B = 256
 EPSILON = 1e-05
 NSEM = 200
-YROWS = dict(x=144, g=144, o=176, n=240)
+YROWS = dict(x=112, g=144, o=160, n=208)
 
 
 ORDER = (
-    0, 1, 2, 3, 4, 7, 8, 42, 2, 10, 3, 6, 11, 7, 4, 12, 8, 1, 5, 9, 15, 126, 38, 6, 14, 40, 40, 38,
-    127, 5, 13, 10, 11, 17, 130, 131, 12, 9, 16, 19, 20, 21, 22, 23, 26, 27, 128, 129, 14, 13, 18,
-    132, 133, 134, 39, 41, 135, 136, 21, 26, 29, 39, 137, 20, 22, 23, 24, 25, 27, 28, 30, 31, 34,
-    41, 138, 139, 140, 141, 29, 142, 143, 144, 30, 145, 25, 33, 146, 24, 32, 36, 148, 28, 35, 147,
-    31, 33, 32, 37, 77, 43, 47, 78, 44, 48, 50, 79, 45, 49, 51, 80, 46, 149, 150, 81, 151, 95, 152,
-    153, 81, 82, 83, 84, 85, 86, 154, 43, 53, 95, 44, 45, 46, 51, 50, 52, 54, 55, 56, 57, 96, 97,
-    98, 99, 100, 155, 56, 57, 58, 85, 86, 87, 156, 157, 158, 159, 99, 100, 101, 160, 60, 64, 161,
-    58, 61, 65, 67, 162, 52, 62, 66, 68, 87, 88, 59, 163, 60, 63, 70, 101, 102, 61, 71, 73, 165,
-    123, 164, 62, 72, 74, 109, 123, 74, 73, 63, 75, 75, 109, 110, 111, 112, 113, 114, 123, 68, 114,
-    113, 115, 67, 69, 88, 89, 90, 102, 103, 104, 123, 59, 166, 115, 116, 123, 124, 116, 117, 118,
-    104, 106, 69, 76, 103, 105, 107, 90, 92, 92, 106, 89, 91, 93, 91, 105, 117, 119, 119, 118, 120,
-    121, 120, 107, 108, 93, 94, 76, 125, 121, 122, 108, 94, 125, 122,
+    0, 1, 2, 3, 4, 5, 8, 9, 44, 2, 6, 10, 3, 4, 7, 11, 12, 40, 5, 9, 13, 8, 16, 128, 40, 129, 6, 14,
+    10, 21, 25, 24, 29, 23, 11, 17, 130, 131, 41, 7, 20, 22, 28, 15, 42, 13, 12, 18, 132, 14, 41,
+    141, 42, 140, 142, 133, 24, 32, 23, 27, 31, 15, 19, 134, 135, 143, 43, 136, 137, 22, 25, 26, 33,
+    30, 29, 138, 43, 27, 35, 139, 28, 36, 144, 26, 32, 34, 38, 30, 79, 45, 49, 150, 145, 80, 50, 46,
+    52, 146, 81, 47, 51, 53, 31, 37, 147, 33, 82, 48, 148, 149, 35, 34, 39, 152, 45, 55, 52, 83,
+    151, 153, 46, 53, 54, 56, 97, 58, 154, 155, 47, 57, 58, 59, 83, 84, 85, 86, 87, 88, 156, 48, 59,
+    60, 97, 99, 100, 98, 101, 102, 157, 54, 87, 88, 89, 61, 158, 159, 60, 160, 161, 162, 111, 101,
+    102, 103, 163, 66, 89, 90, 62, 165, 61, 64, 70, 68, 166, 65, 111, 112, 116, 114, 115, 113, 168,
+    103, 104, 164, 67, 69, 63, 167, 125, 116, 115, 117, 125, 90, 91, 92, 69, 70, 71, 62, 72, 64, 74,
+    76, 117, 118, 65, 125, 91, 93, 104, 105, 106, 92, 94, 95, 63, 75, 73, 93, 94, 118, 119, 120,
+    106, 108, 71, 78, 105, 107, 109, 76, 75, 77, 108, 125, 107, 95, 96, 119, 121, 77, 120, 123, 122,
+    121, 96, 122, 125, 126, 109, 110, 78, 127, 123, 124, 110, 127, 124,
 )
 
 
@@ -111,16 +111,20 @@
 
     lcol, rcol, fcol = lax.rem(col + 3, 4), lax.rem(col + 1, 4), lax.rem(col + 2, 4)
 
-    def begin_work():
-        yield begin, 0.1
+    def begin_y():
+        yield begin[0], 0.1
         c["keep"] = net.local(own, place(col, row))
         send("p0", peer, 0, yr)
+        send("p1", peer, yr, zr)
+        c["keep"].wait()
+        done.add(name + "keep")
+
+    def begin_z():
+        yield begin[1], 0.1
         send("r1", right, yr, zr)
         send("l1", left, yr, zr)
         send("r0", right, 0, yr)
         send("l0", left, 0, yr)
-        send("p1", peer, yr, zr)
-        c["keep"].wait()
 
     def hop(keys, *work):
         yield tuple(name + k for k in keys), 0.0
@@ -132,10 +136,11 @@
         done.update(name + k + "!" for k in keys)
 
     def whole(flag, keys):
-        yield tuple(name + k + "!" for k in keys), 0.0
+        yield tuple(name + k + ("" if k == "keep" else "!") for k in keys), 0.0
         done.add(name + flag)
 
-    add(begin_work())
+    add(begin_y())
+    add(begin_z())
     add(hop(["p0"], ("r2", right, col, 1 - row, 0, yr), ("l2", left, col, 1 - row, 0, yr)))
     add(hop(["r1"], ("r3", right, lcol, row, yr, part), ("p2", peer, lcol, row, yr, zr)))
     add(hop(["l1"], ("l3", left, rcol, row, cut, B - cut), ("p3", peer, rcol, row, yr, zr)))
@@ -150,7 +155,7 @@
     add(hop(["r4"]))
     add(hop(["l4"]))
     add(hop(["p4"]))
-    add(whole("own", ["p0", "p1"]))
+    add(whole("own", ["p0", "p1", "keep"]))
     add(whole("left", ["r0", "r1", "r2", "p2"]))
     add(whole("right", ["l0", "l1", "l2", "p3"]))
     add(whole("far", ["r3", "r4", "l3", "l4", "p4"]))
@@ -521,8 +526,8 @@
 
     tasks, done = [], set()
     add = tasks.append
-    gather_tokens(net, add, done, "x.", (), tok, s.xall, at, half, col, row, YROWS["x"])
-    gather_tokens(net, add, done, "g.", ("x.r2!", "x.l2!"), cot, s.gall, at, half, col, row, YROWS["g"])
+    gather_tokens(net, add, done, "x.", ((), ()), tok, s.xall, at, half, col, row, YROWS["x"])
+    gather_tokens(net, add, done, "g.", (("x.p4",), ("x.r3", "x.r4", "x.l3", "x.l4")), cot, s.gall, at, half, col, row, YROWS["g"])
     nbc = net.go(s.nbs, s.nb.at[row], y1)
     gather_weights(net, add, done, wqkv, wup, wout, wdown, s, at, core, row)
     tabs = [net.local(ctab_h, s.ctab), net.local(stab_h, s.stab)]
@@ -745,8 +750,9 @@
 
     scatter(net, add, done, "o.", tuple("send." + b for b in outward), s.op, so, at, col, row, YROWS["o"])
     scatter(net, add, done, "n.", tuple("ng." + b for b in outward), s.ng, sn, at, col, row, ny, look)
+    gate = ("g.r3", "g.r4", "g.l3", "g.l4")
     for b in outward:
-        add(later(("op." + b, "g.far"), 0.0, mark("send." + b, lambda: None)))
+        add(later(("op." + b,) + gate, 0.0, mark("send." + b, lambda: None)))
     reduce_weights(net, add, done, "a.", "g1", s.g1, under(s, "r0_", fin=f0), at, where, ROWS[0])
     reduce_weights(net, add, done, "b.", "g2", s.g2, under(s, "r1_", fin=f1), at, where, ROWS[1])
     reduce_weights(net, add, done, "c.", "g3", s.g3, under(s, "r2_", fin=f2), at, where, ROWS[2])
@@ -778,9 +784,9 @@
         needs = (f"attb{i}",)
     for name in outward:
         add(later(("attb3",), 0.46, mark("qg." + name, qkv_grad, blocks[name])))
+    add(later(tuple("qg." + name for name in blocks), 1.75, mark("g3", qkv_weight_grad)))
     for name in outward:
         add(later(("qg." + name,), 0.65, mark("ng." + name, input_grad, blocks[name])))
-    add(later(tuple("qg." + name for name in blocks), 1.75, mark("g3", qkv_weight_grad)))
     add(later(tuple("ng." + name for name in blocks), 0.0, mark("vec", lambda: None)))
     add(later(("o.y.end", "o.z.sum"), 0.3, mark("out", write_out)))
     run(tasks, done)

time: 113 us -> 97.7 us (0.86)
  Pallas kernels: 112 us -> 96.7 us
    pallas_call x1, Pallas kernels: 107 us -> 91.7 us  [on_device(): pl.pallas_call(body, out_shape=[shape((B, D // 2), BF), shape((B, D // 2)...]
where the time goes in v5:
time: 97.7 us; the launch traced here: 97.5 us
  Pallas kernels  96.7 us (99%)
    pallas_call x1, Pallas kernels, on_device(): pl.pallas_call(body, out_shape=[shape((B, D // 2), BF), shape((B, D // 2)...  91.7 us
    pallas_call x1, Pallas kernels, on_device(): pl.pallas_call(last, out_shape=[shape((B, D // 2), BF), shape((B, D // 2)...  4.96 us

profile of v5, /device:TPU:1, one launch (start us, length us, event | category | flops | bytes accessed | tf_op | source)
XLA Modules:
  0.0 97.5 jit_solution(16839261890369599102)
XLA Ops:
  0.6 91.7 %block.1 = (bf16[256,512]{1,0:T(8,128)(2,1)}, bf16[256,512]{1,0:T(8,128)(2,1)}, bf16[2,4,2,80,512]{4,3,2,1,0:T(8,128)(2,1)}, bf16[2,4,2,64,512]{4,3,2,1,0:T(8,12...) custom-call(bf16[256,512]{1,0:T(8,128)(2,1)} %tok.1, bf16[256,512]{1,0:T(8,128)(2,1)} %cot.1, ...), custom_call_target="tpu_custom_call" | custom-call | tf_op jit(solution)/shard_map/block/pallas_call | solution.py:883
  92.4 5.0 %last.1 = (bf16[256,512]{1,0:T(8,128)(2,1)}, bf16[256,512]{1,0:T(8,128)(2,1)}, f32[3,512,256]{2,1,0:T(8,128)}, f32[3,256]{1,0:T(4,128)}, f32[256,512]{1,0:T(8,12...) custom-call(bf16[2,4,2,80,512]{4,3,2,1,0:T(8,128)(2,1)} %get-tuple-e, ...), custom_call_target="tpu_custom_call" | custom-call | tf_op jit(solution)/shard_map/last/pallas_call | solution.py:909

commit v6 on v5

--- a/solution.py
+++ b/solution.py
@@ -21,22 +21,22 @@
 B = 256
 EPSILON = 1e-05
 NSEM = 200
-YROWS = dict(x=112, g=144, o=160, n=208)
+YROWS = dict(x=112, g=144, o=128, n=208)
 
 
 ORDER = (
-    0, 1, 2, 3, 4, 5, 8, 9, 44, 2, 6, 10, 3, 4, 7, 11, 12, 40, 5, 9, 13, 8, 16, 128, 40, 129, 6, 14,
-    10, 21, 25, 24, 29, 23, 11, 17, 130, 131, 41, 7, 20, 22, 28, 15, 42, 13, 12, 18, 132, 14, 41,
-    141, 42, 140, 142, 133, 24, 32, 23, 27, 31, 15, 19, 134, 135, 143, 43, 136, 137, 22, 25, 26, 33,
-    30, 29, 138, 43, 27, 35, 139, 28, 36, 144, 26, 32, 34, 38, 30, 79, 45, 49, 150, 145, 80, 50, 46,
-    52, 146, 81, 47, 51, 53, 31, 37, 147, 33, 82, 48, 148, 149, 35, 34, 39, 152, 45, 55, 52, 83,
-    151, 153, 46, 53, 54, 56, 97, 58, 154, 155, 47, 57, 58, 59, 83, 84, 85, 86, 87, 88, 156, 48, 59,
-    60, 97, 99, 100, 98, 101, 102, 157, 54, 87, 88, 89, 61, 158, 159, 60, 160, 161, 162, 111, 101,
-    102, 103, 163, 66, 89, 90, 62, 165, 61, 64, 70, 68, 166, 65, 111, 112, 116, 114, 115, 113, 168,
-    103, 104, 164, 67, 69, 63, 167, 125, 116, 115, 117, 125, 90, 91, 92, 69, 70, 71, 62, 72, 64, 74,
-    76, 117, 118, 65, 125, 91, 93, 104, 105, 106, 92, 94, 95, 63, 75, 73, 93, 94, 118, 119, 120,
-    106, 108, 71, 78, 105, 107, 109, 76, 75, 77, 108, 125, 107, 95, 96, 119, 121, 77, 120, 123, 122,
-    121, 96, 122, 125, 126, 109, 110, 78, 127, 123, 124, 110, 127, 124,
+    1, 5, 0, 2, 8, 3, 4, 9, 44, 2, 6, 10, 3, 11, 4, 12, 7, 40, 5, 13, 9, 8, 16, 128, 40, 129, 6, 14,
+    21, 23, 25, 24, 29, 10, 11, 17, 130, 131, 41, 7, 15, 20, 28, 22, 42, 13, 12, 18, 132, 14, 41,
+    142, 133, 42, 140, 141, 23, 31, 24, 27, 32, 15, 19, 134, 135, 136, 143, 43, 137, 25, 33, 138,
+    22, 26, 30, 29, 139, 27, 35, 43, 145, 147, 28, 36, 148, 144, 146, 33, 31, 26, 34, 79, 45, 49,
+    82, 48, 81, 53, 47, 51, 80, 52, 50, 46, 30, 37, 149, 32, 38, 150, 35, 52, 34, 39, 152, 83, 151,
+    53, 54, 45, 55, 153, 97, 48, 154, 83, 86, 84, 87, 88, 85, 155, 156, 54, 47, 57, 59, 157, 87, 46,
+    58, 58, 56, 59, 60, 160, 97, 98, 88, 100, 102, 89, 101, 99, 61, 158, 163, 66, 62, 159, 161, 162,
+    111, 102, 164, 67, 63, 101, 103, 69, 60, 165, 61, 64, 68, 70, 89, 90, 166, 65, 111, 113, 114,
+    167, 125, 112, 116, 115, 62, 72, 168, 63, 75, 73, 103, 104, 70, 69, 71, 64, 74, 76, 125, 115,
+    116, 117, 90, 91, 92, 125, 65, 76, 75, 77, 117, 118, 91, 93, 92, 95, 94, 104, 105, 106, 93, 94,
+    125, 71, 78, 95, 96, 77, 118, 119, 120, 105, 107, 106, 109, 108, 96, 107, 108, 125, 126, 119,
+    121, 120, 123, 122, 121, 122, 78, 127, 109, 110, 123, 124, 127, 110, 124,
 )
 
 
@@ -436,6 +436,7 @@
     mt=((E, T), BF),
     mixed=((T, E), BF),
     dqt=((E, T), F32),
+    cap=((T, B), F32),
     dk=((T, E), F32),
     dv=((T, E), F32),
     qkvg=((T, 3 * E), BF),
@@ -624,40 +625,65 @@
 
     first = [0, 256, 768, 1536]
 
+    def fold(values, how):
+        return how(values.reshape(-1, 8, B), axis=0)
+
     def attend(i):
-        n = (i + 1) * B
         q = pl.ds(i * B, B)
-
-        @pl.loop(0, 2)
-        def _(h):
-            scores = nt(s.km[h, pl.ds(0, n), :], s.qs[q, :])
-            kid = lax.broadcasted_iota(jnp.int32, (n, B), 0)
-            qid = lax.broadcasted_iota(jnp.int32, (n, B), 1) + i * B
-            allowed = (kid <= qid) & (s.segc[pl.ds(0, n), 0:1] == segr[:, i * B : (i + 1) * B])
-            scores = jnp.where(allowed, scores, -1e30)
-            top = jnp.max(scores, axis=0, keepdims=True)
-            expo = jnp.exp(scores - top)
-            probs = expo * (1.0 / jnp.sum(expo, axis=0, keepdims=True))
-            s.probs[h, pl.ds(first[i], n), :] = probs
-            hrows = rows(h, HD)
-            s.mt[hrows, q] = nn(s.vt[hrows, pl.ds(0, n)], probs.astype(BF)).astype(BF)
+        for c in range(i + 1):
+            kid = lax.broadcasted_iota(jnp.int32, (B, B), 0)
+            qid = lax.broadcasted_iota(jnp.int32, (B, B), 1)
+            allowed = s.segc[pl.ds(c * B, B), 0:1] == segr[:, i * B : (i + 1) * B]
+            allowed = allowed & (kid <= qid) if c == i else allowed
+            s.cap[pl.ds(c * B, B), :] = jnp.where(allowed, 3e38, -1e30)
+
+        for h in range(2):
+            top = jnp.full((8, B), -1e30, F32)
+            for c in range(i + 1):
+                k, at_c = pl.ds(c * B, B), pl.ds(first[i] + c * B, B)
+                scores = jnp.minimum(nt(s.km[h, k, :], s.qs[q, :]), s.cap[k, :])
+                s.probs[h, at_c, :] = scores
+                top = jnp.maximum(top, fold(scores, jnp.max))
+            top = jnp.max(top, axis=0, keepdims=True)
+            total = jnp.zeros((8, B), F32)
+            for c in range(i + 1):
+                at_c = pl.ds(first[i] + c * B, B)
+                expo = jnp.exp(s.probs[h, at_c, :] - top)
+                s.probs[h, at_c, :] = expo
+                total = total + fold(expo, jnp.sum)
+            inverse = 1.0 / jnp.sum(total, axis=0, keepdims=True)
+            hrows = pl.ds(h * HD, HD)
+            mix = jnp.zeros((HD, B), F32)
+            for c in range(i + 1):
+                at_c = pl.ds(first[i] + c * B, B)
+                probs = s.probs[h, at_c, :] * inverse
+                s.probs[h, at_c, :] = probs
+                mix = mix + nn(s.vt[hrows, pl.ds(c * B, B)], probs.astype(BF))
+            s.mt[hrows, q] = mix.astype(BF)
 
         s.mixed[q, :] = s.mt[:, q].astype(F32).T.astype(BF)
 
     def attend_back(i):
-        n = (i + 1) * B
         q = pl.ds(i * B, B)
 
-        @pl.loop(0, 2)
-        def _(h):
-            probs = s.probs[h, pl.ds(first[i], n), :]
-            dprob = nt(s.vm[h, pl.ds(0, n), :], s.do[q, :])
-            inner = jnp.sum(probs * dprob, axis=0, keepdims=True)
-            dscore = (probs * (dprob - inner)).astype(BF)
-            s.dv[pl.ds(0, n), :] += nn(probs.astype(BF), s.dom[h, q, :])
-            s.dk[pl.ds(0, n), :] += nn(dscore, s.qsm[h, q, :])
-            hrows = rows(h, HD)
-            s.dqt[hrows, q] = nn(s.kt[hrows, pl.ds(0, n)], dscore) * (1.0 / math.sqrt(HD))
+        for h in range(2):
+            inner = jnp.zeros((8, B), F32)
+            for c in range(i + 1):
+                k, at_c = pl.ds(c * B, B), pl.ds(first[i] + c * B, B)
+                probs = s.probs[h, at_c, :]
+                dprob = nt(s.vm[h, k, :], s.do[q, :])
+                s.cap[k, :] = dprob
+                inner = inner + fold(probs * dprob, jnp.sum)
+                s.dv[k, :] += nn(probs.astype(BF), s.dom[h, q, :])
+            inner = jnp.sum(inner, axis=0, keepdims=True)
+            hrows = pl.ds(h * HD, HD)
+            dquery = jnp.zeros((HD, B), F32)
+            for c in range(i + 1):
+                k, at_c = pl.ds(c * B, B), pl.ds(first[i] + c * B, B)
+                dscore = (s.probs[h, at_c, :] * (s.cap[k, :] - inner)).astype(BF)
+                s.dk[k, :] += nn(dscore, s.qsm[h, q, :])
+                dquery = dquery + nn(s.kt[hrows, k], dscore)
+            s.dqt[hrows, q] = dquery * (1.0 / math.sqrt(HD))
 
     def branch(b):
         r = rows(b)
@@ -760,33 +786,33 @@
     add(later(("vsum",), 0.05, write_vectors))
     add(write_grad())
     for name, b in blocks.items():
-        add(later(("nb", "x." + name), 0.28, mark("norm." + name, norm, b)))
-        add(later(("wq", "norm." + name), 0.63, mark("proj." + name, project, b)))
+        add(later(("nb", "x." + name), 0.5, mark("norm." + name, norm, b)))
+        add(later(("wq", "norm." + name), 0.45, mark("proj." + name, project, b)))
     needs = tuple("proj." + name for name in blocks)
     for i in range(4):
-        add(later(needs, 0.58 * (i + 1), mark(f"attf{i}", attend, i)))
+        add(later(needs, 0.37 * (i + 1), mark(f"attf{i}", attend, i)))
         needs = (f"attf{i}",)
     for name, b in blocks.items():
-        add(later(("wu", "norm." + name), 0.55, mark("exp." + name, expand, b)))
+        add(later(("wu", "norm." + name), 0.36, mark("exp." + name, expand, b)))
     for name in outward:
         needs = ("wo", "wd", "attf3", "exp." + name)
-        add(later(needs, 0.7, mark("op." + name, branch, blocks[name])))
+        add(later(needs, 0.55, mark("op." + name, branch, blocks[name])))
     for name, b in blocks.items():
         needs = ("wo", "wd", "g." + name, "exp." + name)
-        add(later(needs, 0.4, mark("con." + name, contract, b)))
+        add(later(needs, 0.43, mark("con." + name, contract, b)))
     allg = tuple("g." + name for name in blocks) + tuple("exp." + name for name in blocks)
-    add(later(allg + ("attf3",), 1.85, mark("g1", down_grad)))
+    add(later(allg + ("attf3",), 2.5, mark("g1", down_grad)))
     allc = tuple("con." + name for name in blocks)
-    add(later(allc, 1.65, mark("g2", up_grad)))
+    add(later(allc, 2.2, mark("g2", up_grad)))
     needs = allc + ("attf3",)
     for i in range(4):
-        add(later(needs, 0.6 * (i + 1), mark(f"attb{i}", attend_back, i)))
+        add(later(needs, 0.43 * (i + 1), mark(f"attb{i}", attend_back, i)))
         needs = (f"attb{i}",)
     for name in outward:
-        add(later(("attb3",), 0.46, mark("qg." + name, qkv_grad, blocks[name])))
-    add(later(tuple("qg." + name for name in blocks), 1.75, mark("g3", qkv_weight_grad)))
+        add(later(("attb3",), 0.26, mark("qg." + name, qkv_grad, blocks[name])))
+    add(later(tuple("qg." + name for name in blocks), 1.4, mark("g3", qkv_weight_grad)))
     for name in outward:
-        add(later(("qg." + name,), 0.65, mark("ng." + name, input_grad, blocks[name])))
+        add(later(("qg." + name,), 0.68, mark("ng." + name, input_grad, blocks[name])))
     add(later(tuple("ng." + name for name in blocks), 0.0, mark("vec", lambda: None)))
     add(later(("o.y.end", "o.z.sum"), 0.3, mark("out", write_out)))
     run(tasks, done)

time: 97.7 us -> 95.3 us (0.975)
  Pallas kernels: 96.7 us -> 94.2 us
    pallas_call x1, Pallas kernels: 91.7 us -> 89.3 us  [on_device(): pl.pallas_call(body, out_shape=[shape((B, D // 2), BF), shape((B, D // 2)...]
where the time goes in v6:
time: 95.3 us; the launch traced here: 95.1 us
  Pallas kernels  94.2 us (99%)
    pallas_call x1, Pallas kernels, on_device(): pl.pallas_call(body, out_shape=[shape((B, D // 2), BF), shape((B, D // 2)...  89.3 us
    pallas_call x1, Pallas kernels, on_device(): pl.pallas_call(last, out_shape=[shape((B, D // 2), BF), shape((B, D // 2)...  4.96 us

profile of v6, /device:TPU:1, one launch (start us, length us, event | category | flops | bytes accessed | tf_op | source)
XLA Modules:
  0.0 95.1 jit_solution(7734498488486325513)
XLA Ops:
  0.6 89.3 %block.1 = (bf16[256,512]{1,0:T(8,128)(2,1)}, bf16[256,512]{1,0:T(8,128)(2,1)}, bf16[2,4,2,80,512]{4,3,2,1,0:T(8,128)(2,1)}, bf16[2,4,2,64,512]{4,3,2,1,0:T(8,12...) custom-call(bf16[256,512]{1,0:T(8,128)(2,1)} %tok.1, bf16[256,512]{1,0:T(8,128)(2,1)} %cot.1, ...), custom_call_target="tpu_custom_call" | custom-call | tf_op jit(solution)/shard_map/block/pallas_call | solution.py:909
  89.9 5.0 %last.1 = (bf16[256,512]{1,0:T(8,128)(2,1)}, bf16[256,512]{1,0:T(8,128)(2,1)}, f32[3,512,256]{2,1,0:T(8,128)}, f32[3,256]{1,0:T(4,128)}, f32[256,512]{1,0:T(8,12...) custom-call(bf16[2,4,2,80,512]{4,3,2,1,0:T(8,128)(2,1)} %get-tuple-e, ...), custom_call_target="tpu_custom_call" | custom-call | tf_op jit(solution)/shard_map/last/pallas_call | solution.py:935

commit v7 on v6

--- a/solution.py
+++ b/solution.py
@@ -1,3 +1,4 @@
+from functools import partial
 from types import SimpleNamespace
 import math
 
@@ -21,22 +22,22 @@
 B = 256
 EPSILON = 1e-05
 NSEM = 200
-YROWS = dict(x=112, g=144, o=128, n=208)
+YROWS = dict(x=112, g=144, o=160, n=176)
 
 
 ORDER = (
-    1, 5, 0, 2, 8, 3, 4, 9, 44, 2, 6, 10, 3, 11, 4, 12, 7, 40, 5, 13, 9, 8, 16, 128, 40, 129, 6, 14,
-    21, 23, 25, 24, 29, 10, 11, 17, 130, 131, 41, 7, 15, 20, 28, 22, 42, 13, 12, 18, 132, 14, 41,
-    142, 133, 42, 140, 141, 23, 31, 24, 27, 32, 15, 19, 134, 135, 136, 143, 43, 137, 25, 33, 138,
-    22, 26, 30, 29, 139, 27, 35, 43, 145, 147, 28, 36, 148, 144, 146, 33, 31, 26, 34, 79, 45, 49,
-    82, 48, 81, 53, 47, 51, 80, 52, 50, 46, 30, 37, 149, 32, 38, 150, 35, 52, 34, 39, 152, 83, 151,
-    53, 54, 45, 55, 153, 97, 48, 154, 83, 86, 84, 87, 88, 85, 155, 156, 54, 47, 57, 59, 157, 87, 46,
-    58, 58, 56, 59, 60, 160, 97, 98, 88, 100, 102, 89, 101, 99, 61, 158, 163, 66, 62, 159, 161, 162,
-    111, 102, 164, 67, 63, 101, 103, 69, 60, 165, 61, 64, 68, 70, 89, 90, 166, 65, 111, 113, 114,
-    167, 125, 112, 116, 115, 62, 72, 168, 63, 75, 73, 103, 104, 70, 69, 71, 64, 74, 76, 125, 115,
-    116, 117, 90, 91, 92, 125, 65, 76, 75, 77, 117, 118, 91, 93, 92, 95, 94, 104, 105, 106, 93, 94,
-    125, 71, 78, 95, 96, 77, 118, 119, 120, 105, 107, 106, 109, 108, 96, 107, 108, 125, 126, 119,
-    121, 120, 123, 122, 121, 122, 78, 127, 109, 110, 123, 124, 127, 110, 124,
+    0, 8, 1, 4, 5, 9, 2, 3, 44, 44, 2, 10, 6, 4, 12, 3, 11, 7, 40, 5, 9, 8, 13, 16, 131, 40, 132,
+    10, 6, 21, 25, 23, 14, 29, 24, 12, 18, 135, 41, 136, 7, 20, 28, 22, 15, 42, 13, 41, 143, 11, 17,
+    14, 133, 42, 144, 134, 145, 23, 31, 24, 27, 32, 15, 19, 137, 138, 146, 43, 139, 140, 25, 22, 29,
+    30, 26, 33, 141, 27, 35, 43, 142, 28, 36, 149, 151, 31, 26, 34, 33, 81, 51, 47, 148, 80, 50, 46,
+    150, 82, 48, 147, 32, 79, 49, 52, 53, 38, 45, 153, 30, 37, 152, 35, 34, 39, 155, 47, 57, 83,
+    154, 46, 56, 156, 52, 53, 97, 48, 54, 83, 84, 86, 45, 55, 59, 58, 88, 87, 85, 157, 158, 159, 88,
+    87, 89, 97, 99, 100, 98, 102, 101, 54, 61, 160, 59, 58, 89, 60, 90, 162, 161, 164, 163, 165,
+    111, 102, 60, 101, 103, 61, 166, 62, 66, 171, 168, 111, 113, 114, 70, 68, 112, 64, 116, 90, 91,
+    103, 104, 92, 115, 167, 69, 67, 63, 62, 72, 169, 65, 170, 128, 64, 69, 70, 71, 74, 116, 76, 115,
+    117, 128, 91, 93, 92, 94, 95, 104, 106, 105, 93, 94, 63, 75, 73, 117, 118, 75, 76, 65, 77, 128,
+    95, 96, 71, 78, 118, 120, 119, 105, 107, 106, 109, 108, 77, 107, 96, 125, 128, 108, 119, 121,
+    120, 122, 123, 121, 122, 78, 130, 109, 110, 128, 129, 123, 124, 130, 110, 126, 124, 127,
 )
 
 
@@ -449,6 +450,9 @@
     g1=((F + E, D), BF),
     g2=((F, D), BF),
     g3=((3 * E, D), BF),
+    f0=((2, 4, 2, (F + E) // 8, D // 2), BF),
+    f1=((2, 4, 2, F // 8, D // 2), BF),
+    f2=((2, 4, 2, 3 * E // 8, D // 2), BF),
     vec=((8, D), F32),
     vr=((10, 8, D), F32),
     vs=((4, 8, D), F32),
@@ -496,7 +500,7 @@
 
 def body(
     tok, cot, wqkv, wout, wup, wdown, bqkv, bup, bout, bdown, gain, bias, seg, ctab_h, stab_h,
-    out, tgrad, f0, f1, f2, vout, *scratch,
+    out, tgrad, f0_h, f1_h, f2_h, vout, *scratch,
 ):
     s = SimpleNamespace(**dict(zip(SCRATCH, scratch)))
     send, recv = scratch[len(SCRATCH) :]
@@ -532,24 +536,11 @@
     nbc = net.go(s.nbs, s.nb.at[row], y1)
     gather_weights(net, add, done, wqkv, wup, wout, wdown, s, at, core, row)
     tabs = [net.local(ctab_h, s.ctab), net.local(stab_h, s.stab)]
-    s.nb[row] = s.nbs[...]
-    s.vec[...] = jnp.zeros_like(s.vec)
-    s.dk[...] = jnp.zeros_like(s.dk)
-    s.dv[...] = jnp.zeros_like(s.dv)
-
     def flat(values):
         values = values.astype(F32)
         return jnp.concatenate([values[k : k + 1, :] for k in range(values.shape[0])], axis=1)
 
-    segr = flat(seg[...])
-    s.segc[...] = jnp.broadcast_to(segr, (8, T)).T
-    bq_all = bqkv[...].astype(F32)
-    mine = row == 0
-    bq = jnp.concatenate(
-        [jnp.where(mine, bq_all[k : k + 1, :E], bq_all[k : k + 1, E:]) for k in range(3)], axis=1
-    )
-    bu_all = flat(bup[...])
-    bu = jnp.where(mine, bu_all[:, :F], bu_all[:, F:])
+    rowv = {}
     fcols = pl.ds(pl.multiple_of(row * F, F), F)
     gcols = pl.ds(pl.multiple_of(row * half, half), half)
 
@@ -557,6 +548,19 @@
         return jnp.concatenate([s.nb[0, k : k + 1, :], s.nb[1, k : k + 1, :]], axis=1)
 
     def params():
+        yield ("x.r0", "x.p1"), 0.4
+        s.nb[row] = s.nbs[...]
+        s.vec[...] = jnp.zeros_like(s.vec)
+        s.dk[...] = jnp.zeros_like(s.dk)
+        s.dv[...] = jnp.zeros_like(s.dv)
+        rowv["seg"] = flat(seg[...])
+        s.segc[...] = jnp.broadcast_to(rowv["seg"], (8, T)).T
+        bq_all, bu_all, mine = bqkv[...].astype(F32), flat(bup[...]), row == 0
+        parts = [
+            jnp.where(mine, bq_all[k : k + 1, :E], bq_all[k : k + 1, E:]) for k in range(3)
+        ]
+        rowv["bq"] = jnp.concatenate(parts, axis=1)
+        rowv["bu"] = jnp.where(mine, bu_all[:, :F], bu_all[:, F:])
         yield (nbc,), 0.0
         nbc.wait_recv()
         for copy in tabs:
@@ -583,7 +587,7 @@
 
     def project(c):
         r = rows(c)
-        pre = nn(s.ain[r, :], s.wq[...]) + bq
+        pre = nn(s.ain[r, :], s.wq[...]) + rowv["bq"]
         cos, sin = s.ctab[r, :], s.stab[r, :]
         query = (turn(pre[:, :E], cos, sin)).astype(BF).astype(F32) * (1.0 / math.sqrt(HD))
         key = turn(pre[:, E : 2 * E], cos, sin).astype(BF).astype(F32)
@@ -597,7 +601,7 @@
 
     def expand(c):
         r = rows(c)
-        pre = nn(s.mim[r, :], s.wu[...]) + bu
+        pre = nn(s.mim[r, :], s.wu[...]) + rowv["bu"]
         cdf = 0.5 * (1.0 + lax.erf(pre * math.sqrt(0.5)))
         s.hid[r, :] = (pre * cdf).astype(BF)
         s.slope[r, :] = cdf + pre * jnp.exp(-0.5 * pre * pre) * (1.0 / math.sqrt(2.0 * math.pi))
@@ -633,7 +637,7 @@
         for c in range(i + 1):
             kid = lax.broadcasted_iota(jnp.int32, (B, B), 0)
             qid = lax.broadcasted_iota(jnp.int32, (B, B), 1)
-            allowed = s.segc[pl.ds(c * B, B), 0:1] == segr[:, i * B : (i + 1) * B]
+            allowed = s.segc[pl.ds(c * B, B), 0:1] == rowv["seg"][:, i * B : (i + 1) * B]
             allowed = allowed & (kid <= qid) if c == i else allowed
             s.cap[pl.ds(c * B, B), :] = jnp.where(allowed, 3e38, -1e30)
 
@@ -779,9 +783,16 @@
     gate = ("g.r3", "g.r4", "g.l3", "g.l4")
     for b in outward:
         add(later(("op." + b,) + gate, 0.0, mark("send." + b, lambda: None)))
-    reduce_weights(net, add, done, "a.", "g1", s.g1, under(s, "r0_", fin=f0), at, where, ROWS[0])
-    reduce_weights(net, add, done, "b.", "g2", s.g2, under(s, "r1_", fin=f1), at, where, ROWS[1])
-    reduce_weights(net, add, done, "c.", "g3", s.g3, under(s, "r2_", fin=f2), at, where, ROWS[2])
+    reduce_weights(net, add, done, "a.", "g1", s.g1, under(s, "r0_", fin=s.f0), at, where, ROWS[0])
+    reduce_weights(net, add, done, "b.", "g2", s.g2, under(s, "r1_", fin=s.f1), at, where, ROWS[1])
+    reduce_weights(net, add, done, "c.", "g3", s.g3, under(s, "r2_", fin=s.f2), at, where, ROWS[2])
+    writes = []
+
+    def write_reduced(src, dst):
+        writes.append(net.local(src, dst))
+
+    for name, src, dst in (("a.", s.f0, f0_h), ("b.", s.f1, f1_h), ("c.", s.f2, f2_h)):
+        add(later((name + "end",), 0.02, partial(write_reduced, src, dst)))
     add(reduce_vectors(net, done, s, at))
     add(later(("vsum",), 0.05, write_vectors))
     add(write_grad())
@@ -816,6 +827,8 @@
     add(later(tuple("ng." + name for name in blocks), 0.0, mark("vec", lambda: None)))
     add(later(("o.y.end", "o.z.sum"), 0.3, mark("out", write_out)))
     run(tasks, done)
+    for copy in writes:
+        copy.wait()
     for copy in net.sent:
         copy.wait_send()
 
@@ -914,7 +927,7 @@
             *early,
         ],
         in_specs=[hbm] * 6 + [vmem] * 7 + [hbm] * 2,
-        out_specs=[vmem] * 6,
+        out_specs=[vmem, vmem, hbm, hbm, hbm, vmem],
         scratch_shapes=[pltpu.VMEM(*spec) for spec in SCRATCH.values()]
         + [pltpu.SemaphoreType.DMA((NSEM,)), pltpu.SemaphoreType.DMA((NSEM,))],
         compiler_params=pltpu.CompilerParams(

time: 95.3 us -> 96.6 us (1.014)
  Pallas kernels: 94.2 us -> 95.5 us
    pallas_call x1, Pallas kernels: 89.3 us -> 90.5 us  [on_device(): pl.pallas_call(body, out_shape=[shape((B, D // 2), BF), shape((B, D // 2)...]
where the time goes in v7:
time: 96.6 us; the launch traced here: 96.3 us
  Pallas kernels  95.5 us (99%)
    pallas_call x1, Pallas kernels, on_device(): pl.pallas_call(body, out_shape=[shape((B, D // 2), BF), shape((B, D // 2)...  90.5 us
    pallas_call x1, Pallas kernels, on_device(): pl.pallas_call(last, out_shape=[shape((B, D // 2), BF), shape((B, D // 2)...  4.96 us

profile of v7, /device:TPU:1, one launch (start us, length us, event | category | flops | bytes accessed | tf_op | source)
XLA Modules:
  0.0 96.3 jit_solution(10869030675002146116)
XLA Ops:
  0.6 90.5 %block.1 = (bf16[256,512]{1,0:T(8,128)(2,1)}, bf16[256,512]{1,0:T(8,128)(2,1)}, bf16[2,4,2,80,512]{4,3,2,1,0:T(8,128)(2,1)}, bf16[2,4,2,64,512]{4,3,2,1,0:T(8,12...) custom-call(bf16[256,512]{1,0:T(8,128)(2,1)} %tok.1, bf16[256,512]{1,0:T(8,128)(2,1)} %cot.1, ...), custom_call_target="tpu_custom_call" | custom-call | tf_op jit(solution)/shard_map/block/pallas_call | solution.py:922
  91.2 5.0 %last.1 = (bf16[256,512]{1,0:T(8,128)(2,1)}, bf16[256,512]{1,0:T(8,128)(2,1)}, f32[3,512,256]{2,1,0:T(8,128)}, f32[3,256]{1,0:T(4,128)}, f32[256,512]{1,0:T(8,12...) custom-call(bf16[2,4,2,80,512]{4,3,2,1,0:T(8,128)(2,1)} %get-tuple-e, ...), custom_call_target="tpu_custom_call" | custom-call | tf_op jit(solution)/shard_map/last/pallas_call | solution.py:948

commit v8 on v7

--- a/solution.py
+++ b/solution.py
@@ -22,22 +22,22 @@
 B = 256
 EPSILON = 1e-05
 NSEM = 200
-YROWS = dict(x=112, g=144, o=160, n=176)
+YROWS = dict(x=112, g=128, o=160, n=208)
 
 
 ORDER = (
-    0, 8, 1, 4, 5, 9, 2, 3, 44, 44, 2, 10, 6, 4, 12, 3, 11, 7, 40, 5, 9, 8, 13, 16, 131, 40, 132,
-    10, 6, 21, 25, 23, 14, 29, 24, 12, 18, 135, 41, 136, 7, 20, 28, 22, 15, 42, 13, 41, 143, 11, 17,
-    14, 133, 42, 144, 134, 145, 23, 31, 24, 27, 32, 15, 19, 137, 138, 146, 43, 139, 140, 25, 22, 29,
-    30, 26, 33, 141, 27, 35, 43, 142, 28, 36, 149, 151, 31, 26, 34, 33, 81, 51, 47, 148, 80, 50, 46,
-    150, 82, 48, 147, 32, 79, 49, 52, 53, 38, 45, 153, 30, 37, 152, 35, 34, 39, 155, 47, 57, 83,
-    154, 46, 56, 156, 52, 53, 97, 48, 54, 83, 84, 86, 45, 55, 59, 58, 88, 87, 85, 157, 158, 159, 88,
-    87, 89, 97, 99, 100, 98, 102, 101, 54, 61, 160, 59, 58, 89, 60, 90, 162, 161, 164, 163, 165,
-    111, 102, 60, 101, 103, 61, 166, 62, 66, 171, 168, 111, 113, 114, 70, 68, 112, 64, 116, 90, 91,
-    103, 104, 92, 115, 167, 69, 67, 63, 62, 72, 169, 65, 170, 128, 64, 69, 70, 71, 74, 116, 76, 115,
-    117, 128, 91, 93, 92, 94, 95, 104, 106, 105, 93, 94, 63, 75, 73, 117, 118, 75, 76, 65, 77, 128,
-    95, 96, 71, 78, 118, 120, 119, 105, 107, 106, 109, 108, 77, 107, 96, 125, 128, 108, 119, 121,
-    120, 122, 123, 121, 122, 78, 130, 109, 110, 128, 129, 123, 124, 130, 110, 126, 124, 127,
+    1, 4, 3, 5, 0, 8, 2, 9, 44, 44, 2, 6, 10, 4, 12, 3, 7, 11, 40, 5, 13, 9, 8, 16, 131, 40, 132, 6,
+    14, 21, 23, 24, 25, 29, 10, 12, 18, 135, 136, 41, 7, 15, 20, 22, 28, 42, 13, 11, 17, 133, 14,
+    41, 134, 145, 42, 144, 143, 23, 31, 24, 32, 27, 15, 19, 137, 146, 138, 139, 43, 140, 25, 33,
+    141, 22, 29, 30, 26, 142, 43, 27, 35, 148, 147, 28, 36, 151, 149, 150, 33, 26, 80, 34, 50, 46,
+    82, 48, 81, 47, 79, 45, 49, 53, 31, 52, 51, 30, 37, 152, 32, 38, 153, 155, 34, 35, 39, 154, 156,
+    83, 157, 53, 97, 46, 52, 56, 54, 158, 48, 159, 83, 85, 84, 88, 86, 87, 160, 47, 57, 97, 100, 99,
+    98, 101, 102, 161, 45, 88, 55, 59, 58, 54, 61, 162, 167, 66, 62, 163, 87, 89, 164, 165, 166, 59,
+    58, 60, 111, 168, 63, 67, 69, 101, 102, 103, 169, 64, 68, 70, 170, 89, 90, 61, 171, 128, 65,
+    111, 112, 113, 114, 115, 62, 72, 116, 69, 63, 73, 70, 75, 71, 103, 104, 128, 60, 172, 64, 74,
+    76, 115, 116, 117, 90, 91, 92, 65, 128, 75, 76, 77, 117, 118, 91, 93, 92, 94, 95, 104, 106, 105,
+    94, 93, 71, 78, 128, 77, 95, 96, 118, 119, 120, 105, 107, 106, 109, 108, 96, 125, 107, 108, 128,
+    129, 119, 121, 120, 122, 123, 121, 122, 78, 130, 109, 110, 123, 124, 130, 110, 126, 124, 127,
 )
 
 
@@ -438,6 +438,7 @@
     mixed=((T, E), BF),
     dqt=((E, T), F32),
     cap=((T, B), F32),
+    acc=((F, D), F32),
     dk=((T, E), F32),
     dv=((T, E), F32),
     qkvg=((T, 3 * E), BF),
@@ -693,11 +694,20 @@
         r = rows(b)
         s.op[r, :] = (nn(s.mixed[r, :], s.wo[...]) + nn(s.hid[r, :], s.wd[...])).astype(BF)
 
+    def down_early():
+        gall = jnp.concatenate([s.gall[rows(b), :] for b in (col, lb, rb)])
+
+        @pl.loop(0, 4)
+        def _(f):
+            r = rows(f, 128)
+            hid = jnp.concatenate([s.hid[rows(b), r] for b in (col, lb, rb)])
+            s.acc[r, :] = tn(hid, gall)
+
     def down_grad():
         @pl.loop(0, 4)
-        def _(b):
-            r = rows(b, 128)
-            s.g1[r, :] = tn(s.hid[:, r], s.gall[...]).astype(BF)
+        def _(f):
+            r = rows(f, 128)
+            s.g1[r, :] = (s.acc[r, :] + tn(s.hid[rows(fb), r], s.gall[rows(fb), :])).astype(BF)
 
         s.g1[F:, :] = nn(s.mt[...], s.gall[...]).astype(BF)
 
@@ -811,8 +821,10 @@
     for name, b in blocks.items():
         needs = ("wo", "wd", "g." + name, "exp." + name)
         add(later(needs, 0.43, mark("con." + name, contract, b)))
-    allg = tuple("g." + name for name in blocks) + tuple("exp." + name for name in blocks)
-    add(later(allg + ("attf3",), 2.5, mark("g1", down_grad)))
+    near = ("own", "left", "right")
+    needs = tuple("g." + name for name in near) + tuple("exp." + name for name in near)
+    add(later(needs, 1.9, mark("g1early", down_early)))
+    add(later(("g1early", "g.far", "exp.far", "attf3"), 0.95, mark("g1", down_grad)))
     allc = tuple("con." + name for name in blocks)
     add(later(allc, 2.2, mark("g2", up_grad)))
     needs = allc + ("attf3",)
@@ -847,7 +859,7 @@
 def last(
     f0_h, f1_h, f2_h, vec_h, out_h, tgrad_h,
     out_o, tgrad_o, wq_o, bq_o, wo_o, bo_o, wu_o, bu_o, wd_o, bd_o, gain_o, bias_o,
-    f0, f1, f2, vec, out, tgrad, wq, wo, wu, wd, sems,
+    f0, f1, f2, vec, out, tgrad, wq, wo, wu, wd, bq, bo, bu, gain, bias, sems,
 ):
     row = lax.axis_index("row")
     copies = []
@@ -894,14 +906,15 @@
     def cut(values):
         return jnp.where(left, values[:, :half], values[:, half:])
 
-    bo_o[...] = cut(vec[0, 4:5, :])
-    bd_o[...] = cut(vec[0, 4:5, :])
+    bo[...] = cut(vec[0, 4:5, :])
     for k in range(3):
-        bq_o[k : k + 1, :E] = vec[0, 5:6, k * E : (k + 1) * E]
-        bq_o[k : k + 1, E:] = vec[0, 5:6, (k + 3) * E : (k + 4) * E]
-    bu_o[...] = vec[0, 6:7, :]
-    gain_o[...] = cut(vec[1, 0:2, :])
-    bias_o[...] = cut(vec[1, 2:4, :])
+        bq[k : k + 1, :E] = vec[0, 5:6, k * E : (k + 1) * E]
+        bq[k : k + 1, E:] = vec[0, 5:6, (k + 3) * E : (k + 4) * E]
+    bu[...] = vec[0, 6:7, :]
+    gain[...] = cut(vec[1, 0:2, :])
+    bias[...] = cut(vec[1, 2:4, :])
+    for a, b in ((bq, bq_o), (bo, bo_o), (bo, bd_o), (bu, bu_o), (gain, gain_o), (bias, bias_o)):
+        write(a, b)
     for copy in copies[len(reads) :]:
         copy.wait()
 
@@ -945,6 +958,7 @@
         ((D // 2, 2 * F), F32),
         ((2 * F, D // 2), F32),
     ]
+    small = [((3, 2 * E), F32), ((1, D // 2), F32), ((1, 2 * F), F32)] + [((2, D // 2), F32)] * 2
     results = pl.pallas_call(
         last,
         out_shape=[
@@ -962,11 +976,11 @@
             shape((2, D // 2), F32),
         ],
         in_specs=[hbm] * 6,
-        out_specs=[hbm, hbm, hbm, vmem, hbm, vmem, hbm, vmem, hbm, vmem, vmem, vmem],
+        out_specs=[hbm] * 12,
         scratch_shapes=[pltpu.VMEM(e.shape, e.dtype) for e in early]
         + [pltpu.VMEM((B, D // 2), BF)] * 2
-        + [pltpu.VMEM(*spec) for spec in big]
-        + [pltpu.SemaphoreType.DMA((16,))],
+        + [pltpu.VMEM(*spec) for spec in big + small]
+        + [pltpu.SemaphoreType.DMA((24,))],
         compiler_params=pltpu.CompilerParams(vmem_limit_bytes=60 * 1024 * 1024),
         name="last",
     )(f0, f1, f2, vec, out, tgrad)

time: 96.6 us -> 93.5 us (0.968)
  Pallas kernels: 95.5 us -> 92.5 us
    pallas_call x1, Pallas kernels: 90.5 us -> 88 us  [on_device(): pl.pallas_call(body, out_shape=[shape((B, D // 2), BF), shape((B, D // 2)...]
where the time goes in v8:
time: 93.5 us; the launch traced here: 93.3 us
  Pallas kernels  92.5 us (99%)
    pallas_call x1, Pallas kernels, on_device(): pl.pallas_call(body, out_shape=[shape((B, D // 2), BF), shape((B, D // 2)...  88 us
    pallas_call x1, Pallas kernels, on_device(): pl.pallas_call(last, out_shape=[shape((B, D // 2), BF), shape((B, D // 2)...  4.42 us

profile of v8, /device:TPU:1, one launch (start us, length us, event | category | flops | bytes accessed | tf_op | source)
XLA Modules:
  0.0 93.3 jit_solution(14366194967322939131)
XLA Ops:
  0.6 88.0 %block.1 = (bf16[256,512]{1,0:T(8,128)(2,1)}, bf16[256,512]{1,0:T(8,128)(2,1)}, bf16[2,4,2,80,512]{4,3,2,1,0:T(8,128)(2,1)}, bf16[2,4,2,64,512]{4,3,2,1,0:T(8,12...) custom-call(bf16[256,512]{1,0:T(8,128)(2,1)} %tok.1, bf16[256,512]{1,0:T(8,128)(2,1)} %cot.1, ...), custom_call_target="tpu_custom_call" | custom-call | tf_op jit(solution)/shard_map/block/pallas_call | solution.py:935
  88.7 4.4 %last.1 = (bf16[256,512]{1,0:T(8,128)(2,1)}, bf16[256,512]{1,0:T(8,128)(2,1)}, f32[3,512,256]{2,1,0:T(8,128)}, f32[3,256]{1,0:T(4,128)}, f32[256,512]{1,0:T(8,12...) custom-call(bf16[2,4,2,80,512]{4,3,2,1,0:T(8,128)(2,1)} %get-tuple-e, ...), custom_call_target="tpu_custom_call" | custom-call | tf_op jit(solution)/shard_map/last/pallas_call | solution.py:962

commit v9 on v8

--- a/solution.py
+++ b/solution.py
@@ -870,33 +870,38 @@
         copies.append(copy)
         return copy
 
-    pairs = ((f0_h, f0), (f1_h, f1), (f2_h, f2), (vec_h, vec), (out_h, out), (tgrad_h, tgrad))
+    pairs = ((f0_h.at[0], f0.at[0]), (f0_h.at[1], f0.at[1]), (f1_h.at[0], f1.at[0]), (f1_h.at[1], f1.at[1]), (f2_h, f2), (vec_h, vec), (out_h, out), (tgrad_h, tgrad))
     reads = [write(a, b) for a, b in pairs]
-    reads[0].wait()
-    for r in range(2):
-        for k in range(8):
-            piece = f0[k // 4, k % 4, r].astype(F32)
-            n = piece.shape[0]
-            inside = max(0, min(n, F - k * n))
-            if inside:
-                wd[pl.ds(r * F + k * n, inside), :] = piece[:inside]
-            if inside < n:
-                wo[pl.ds(r * E + k * n + inside - F, n - inside), :] = piece[inside:]
-        write(wd.at[pl.ds(r * F, F)], wd_o.at[pl.ds(r * F, F)])
+    for core in range(2):
+        reads[core].wait()
+        for r in range(2):
+            for k in range(4 * core, 4 * core + 4):
+                piece = f0[core, k % 4, r].astype(F32)
+                n = piece.shape[0]
+                inside = max(0, min(n, F - k * n))
+                if inside:
+                    wd[pl.ds(r * F + k * n, inside), :] = piece[:inside]
+                if inside < n:
+                    wo[pl.ds(r * E + k * n + inside - F, n - inside), :] = piece[inside:]
+            first, end = 4 * core * n, min(F, 4 * (core + 1) * n)
+            done = pl.ds(r * F + first, end - first)
+            write(wd.at[done], wd_o.at[done])
     write(wo, wo_o)
-    reads[1].wait()
-    for r in range(2):
-        for k in range(4):
-            pair = [f1[(2 * k + h) // 4, (2 * k + h) % 4, r].astype(F32) for h in range(2)]
-            wu[:, pl.ds(r * F + k * E, E)] = jnp.concatenate(pair).T
-        write(wu.at[:, pl.ds(r * F, F)], wu_o.at[:, pl.ds(r * F, F)])
-    reads[2].wait()
+    for core in range(2):
+        reads[2 + core].wait()
+        for r in range(2):
+            for k in (2 * core, 2 * core + 1):
+                pair = [f1[core, (2 * k + h) % 4, r].astype(F32) for h in range(2)]
+                wu[:, pl.ds(r * F + k * E, E)] = jnp.concatenate(pair).T
+            done = pl.ds(r * F + 2 * core * E, 2 * E)
+            write(wu.at[:, done], wu_o.at[:, done])
+    reads[4].wait()
     for r in range(2):
         whole = jnp.concatenate([f2[k // 4, k % 4, r].astype(F32) for k in range(8)])
         for k in range(3):
             wq[k, :, pl.ds(r * E, E)] = whole[k * E : (k + 1) * E].T
     write(wq, wq_o)
-    for copy in reads[3:]:
+    for copy in reads[5:]:
         copy.wait()
     write(out, out_o)
     write(tgrad, tgrad_o)
@@ -980,7 +985,7 @@
         scratch_shapes=[pltpu.VMEM(e.shape, e.dtype) for e in early]
         + [pltpu.VMEM((B, D // 2), BF)] * 2
         + [pltpu.VMEM(*spec) for spec in big + small]
-        + [pltpu.SemaphoreType.DMA((24,))],
+        + [pltpu.SemaphoreType.DMA((32,))],
         compiler_params=pltpu.CompilerParams(vmem_limit_bytes=60 * 1024 * 1024),
         name="last",
     )(f0, f1, f2, vec, out, tgrad)

time: 93.5 us -> 93.3 us (level)
  no operation moved by 1% of the time
where the time goes in v9:
time: 93.3 us; the launch traced here: 93.1 us
  Pallas kernels  92.3 us (99%)
    pallas_call x1, Pallas kernels, on_device(): pl.pallas_call(body, out_shape=[shape((B, D // 2), BF), shape((B, D // 2)...  88 us
    pallas_call x1, Pallas kernels, on_device(): pl.pallas_call(last, out_shape=[shape((B, D // 2), BF), shape((B, D // 2)...  4.22 us

profile of v9, /device:TPU:1, one launch (start us, length us, event | category | flops | bytes accessed | tf_op | source)
XLA Modules:
  0.0 93.1 jit_solution(1984381425543582328)
XLA Ops:
  0.6 88.0 %block.1 = (bf16[256,512]{1,0:T(8,128)(2,1)}, bf16[256,512]{1,0:T(8,128)(2,1)}, bf16[2,4,2,80,512]{4,3,2,1,0:T(8,128)(2,1)}, bf16[2,4,2,64,512]{4,3,2,1,0:T(8,12...) custom-call(bf16[256,512]{1,0:T(8,128)(2,1)} %tok.1, bf16[256,512]{1,0:T(8,128)(2,1)} %cot.1, ...), custom_call_target="tpu_custom_call" | custom-call | tf_op jit(solution)/shard_map/block/pallas_call | solution.py:940
  88.7 4.2 %last.1 = (bf16[256,512]{1,0:T(8,128)(2,1)}, bf16[256,512]{1,0:T(8,128)(2,1)}, f32[3,512,256]{2,1,0:T(8,128)}, f32[3,256]{1,0:T(4,128)}, f32[256,512]{1,0:T(8,12...) custom-call(bf16[2,4,2,80,512]{4,3,2,1,0:T(8,128)(2,1)} %get-tuple-e, ...), custom_call_target="tpu_custom_call" | custom-call | tf_op jit(solution)/shard_map/last/pallas_call | solution.py:967
